TPU v7x, 256 devices: a whole 4x4x8 slice. The times are simulated.
256 devices in a mesh: state: 8 (over x, core), walker: 32 (over y, z).
Axes of the slice: x: 4, y: 4, z: 8, core: 2. Of those that a mesh axis runs over, the one named last changes fastest.
Arguments:
- positions: float32 [2, 30, 16, 4096], P(None, None, None, 'walker'), may hold values from 0 to 6
- recip: int32 [2, 128], replicated, may hold values from -3 to 3
- moire_coef: float32 [128], replicated, may hold values from -0.09375 to 0.09375
- counts: int32 [4096], P('walker'), may hold values from 1 to 7
- w_first: bfloat16 [256, 16, 256], P(None, 'state'), may hold values from -0.0625 to 0.0625
- w_second: bfloat16 [256, 16, 256], P(None, 'state'), may hold values from -0.375 to 0.375
- w_heads: bfloat16 [2, 16, 256], P(None, 'state'), may hold values from -0.375 to 0.375
Outputs:
- energy_matrix: float32 [16, 16], replicated
- grad_first: float32 [256, 16, 256], P(None, 'state')
- grad_second: float32 [256, 16, 256], P(None, 'state')
- grad_heads: float32 [2, 16, 256], P(None, 'state')
All inputs are finite; a program needn't handle non-finite values.
Results may differ from a plain program's by a relative error of at most 0.0046.
Values sent between devices are 32-bit elements; how exact they have to be, the bound alone decides.
No kernel may reach another device: no remote copies, remote signals or barrier semaphores. Data moves between devices by JAX's collectives and lax.ppermute only.
A program may use at most 64 MiB of HBM per device.

v0:
```python
import math

import jax
import jax.numpy as jnp
from jax import lax
from jax.sharding import PartitionSpec as P

TWO_PI = 6.283185307179586
ROOT_THREE = 1.7320508075688772
HIGHEST = lax.Precision.HIGHEST


def wave_vectors(recip):
    first_index = recip[0].astype(jnp.float32)
    second_index = recip[1].astype(jnp.float32)
    return (TWO_PI * first_index, TWO_PI * (2.0 * second_index - first_index) / ROOT_THREE)


def config_features(positions, recip, moire_coef):
    row_count = positions.shape[2] * positions.shape[3]
    wave_x, wave_y = wave_vectors(recip)

    def one_block(portion):
        phase = (
            portion[0][:, :, None] * wave_x[None, None, :]
            + portion[1][:, :, None] * wave_y[None, None, :]
        )
        cosines = jnp.sum(jnp.cos(phase), axis=0)
        sines = jnp.sum(jnp.sin(phase), axis=0)
        potential = jnp.dot(cosines, moire_coef, precision=HIGHEST)
        return (jnp.concatenate([cosines, sines], axis=1).astype(jnp.bfloat16), potential)

    features_bf, potential = lax.map(one_block, jnp.moveaxis(positions, 2, 0))
    return (features_bf.reshape(row_count, -1), potential.reshape(row_count))


def invert(matrix):
    size = matrix.shape[0]
    inverse = jnp.broadcast_to(jnp.eye(size, dtype=jnp.float32)[:, :, None], matrix.shape)
    for pivot in range(size):
        factor = 1.0 / matrix[pivot, pivot]
        row_matrix = matrix[pivot] * factor
        row_inverse = inverse[pivot] * factor
        column = matrix[:, pivot]
        matrix = matrix - column[:, None, :] * row_matrix[None]
        inverse = inverse - column[:, None, :] * row_inverse[None]
        matrix = matrix.at[pivot].set(row_matrix)
        inverse = inverse.at[pivot].set(row_inverse)
    return inverse


def energy_terms(amp_tiles, hps_tiles, weights):
    inverse = invert(amp_tiles)
    local_energy = jnp.einsum("ijb,jkb->ikb", inverse, hps_tiles, precision=HIGHEST)
    energy_trace = jnp.trace(local_energy, axis1=0, axis2=1)
    weighted = jnp.einsum("ikb,b->ik", local_energy, weights, precision=HIGHEST)
    return (inverse, local_energy, energy_trace, weighted)


def cotangent_terms(inverse, local_energy, energy_trace, energy_total, total_count, weights):
    mean_energy = jnp.trace(energy_total) / total_count
    walker_share = weights / total_count
    flipped = jnp.transpose(inverse, (1, 0, 2))
    along = jnp.einsum("kib,jkb->ijb", inverse, local_energy, precision=HIGHEST)
    d_amp = walker_share * (2.0 * (energy_trace - mean_energy) * flipped - along)
    d_hps = walker_share * flipped
    return (d_amp, d_hps)


def hidden_block(portion, w_one, w_two):
    first_act = jnp.tanh(
        jnp.einsum("rf,fsh->rsh", portion, w_one, preferred_element_type=jnp.float32)
    )
    first_bf = first_act.astype(jnp.bfloat16)
    second_tanh = jnp.tanh(
        jnp.einsum("rsh,hsg->rsg", first_bf, w_two, preferred_element_type=jnp.float32)
    )
    second_bf = (second_tanh + first_act).astype(jnp.bfloat16)
    return (first_act, first_bf, second_tanh, second_bf)


def shards(positions, recip, moire_coef, counts, w_first, w_second, w_heads):
    state_count = w_first.shape[1]
    slot_count = positions.shape[2]
    walker_count = positions.shape[3]
    row_count = slot_count * walker_count
    features_bf, potential = config_features(positions, recip, moire_coef)
    block_rows = math.gcd(row_count, 512)
    block_count = row_count // block_rows
    feature_blocks = features_bf.reshape(block_count, block_rows, -1)

    def forward_block(portion):
        first_act, first_bf, second_tanh, second_bf = hidden_block(portion, w_first, w_second)
        return jnp.einsum("rsh,tsh->tsr", second_bf, w_heads, preferred_element_type=jnp.float32)

    outputs = lax.map(forward_block, feature_blocks)
    outputs = jnp.moveaxis(outputs, 0, 2).reshape(2, state_count, slot_count, walker_count)
    squashed = jnp.tanh(outputs[0])
    grid_shape = (state_count, slot_count, walker_count)
    slot_index = lax.broadcasted_iota(jnp.int32, grid_shape, 1)
    state_index = (
        lax.broadcasted_iota(jnp.int32, grid_shape, 0) + lax.axis_index("state") * state_count
    )
    kronecker = (slot_index == state_index).astype(jnp.float32)
    spread = 0.75 / slot_count
    amplitude = kronecker + spread * squashed
    potential_grid = potential.reshape(slot_count, walker_count)[None]
    local_hps = outputs[1] + potential_grid * amplitude
    groups = lax.axis_size("state")
    per_group = walker_count // groups
    split_shape = (state_count, slot_count, groups, per_group)
    amp_tiles, hps_tiles = (
        lax.all_to_all(
            amplitude.reshape(split_shape), "state", split_axis=2, concat_axis=0, tiled=True
        ),
        lax.all_to_all(
            local_hps.reshape(split_shape), "state", split_axis=2, concat_axis=0, tiled=True
        ),
    )
    amp_tiles = amp_tiles.reshape(slot_count, slot_count, per_group)
    hps_tiles = hps_tiles.reshape(slot_count, slot_count, per_group)
    weights = lax.dynamic_slice_in_dim(
        counts, lax.axis_index("state") * per_group, per_group
    ).astype(jnp.float32)
    inverse, local_energy, energy_trace, weighted = energy_terms(amp_tiles, hps_tiles, weights)
    energy_total, total_count = lax.psum((weighted, jnp.sum(weights)), ("state", "walker"))
    d_amp, d_hps = cotangent_terms(
        inverse, local_energy, energy_trace, energy_total, total_count, weights
    )
    back_shape = (slot_count, slot_count, 1, per_group)
    d_amp, d_hps = (
        lax.all_to_all(d_amp.reshape(back_shape), "state", split_axis=0, concat_axis=2, tiled=True),
        lax.all_to_all(d_hps.reshape(back_shape), "state", split_axis=0, concat_axis=2, tiled=True),
    )
    d_amp = d_amp.reshape(grid_shape)
    d_hps = d_hps.reshape(grid_shape)
    energy_matrix = energy_total / total_count
    slope = spread * (1.0 - squashed * squashed)
    cot_amp = (d_amp + d_hps * potential_grid) * slope
    cotangent = (
        jnp.stack([cot_amp, d_hps])
        .astype(jnp.bfloat16)
        .reshape(2, state_count, block_count, block_rows)
    )
    cot_blocks = jnp.moveaxis(cotangent, 2, 0)

    def backward_step(block_index, grads):
        grad_one, grad_two, grad_three = grads
        portion = lax.dynamic_index_in_dim(feature_blocks, block_index, 0, keepdims=False)
        cot_part = lax.dynamic_index_in_dim(cot_blocks, block_index, 0, keepdims=False)
        first_act, first_bf, second_tanh, second_bf = hidden_block(portion, w_first, w_second)
        grad_three = grad_three + jnp.einsum(
            "tsr,rsh->tsh", cot_part, second_bf, preferred_element_type=jnp.float32
        )
        back_two = jnp.einsum("tsr,tsh->rsh", cot_part, w_heads, preferred_element_type=jnp.float32)
        inner_two = (back_two * (1.0 - second_tanh * second_tanh)).astype(jnp.bfloat16)
        grad_two = grad_two + jnp.einsum(
            "rsh,rsg->hsg", first_bf, inner_two, preferred_element_type=jnp.float32
        )
        back_one = back_two + jnp.einsum(
            "rsg,hsg->rsh", inner_two, w_second, preferred_element_type=jnp.float32
        )
        inner_one = (back_one * (1.0 - first_act * first_act)).astype(jnp.bfloat16)
        grad_one = grad_one + jnp.einsum(
            "rf,rsh->fsh", portion, inner_one, preferred_element_type=jnp.float32
        )
        return (grad_one, grad_two, grad_three)

    start_grads = (
        jnp.zeros(w_first.shape, jnp.float32),
        jnp.zeros(w_second.shape, jnp.float32),
        jnp.zeros(w_heads.shape, jnp.float32),
    )
    grad_one, grad_two, grad_three = lax.fori_loop(0, block_count, backward_step, start_grads)
    grad_first, grad_second, grad_heads = lax.psum((grad_one, grad_two, grad_three), "walker")
    return (energy_matrix, grad_first, grad_second, grad_heads)


def solution(mesh):
    in_specs = (
        P(None, None, None, "walker"),
        P(),
        P(),
        P("walker"),
        P(None, "state", None),
        P(None, "state", None),
        P(None, "state", None),
    )
    out_specs = (P(), P(None, "state", None), P(None, "state", None), P(None, "state", None))
    return jax.shard_map(shards, mesh=mesh, in_specs=in_specs, out_specs=out_specs, check_vma=False)
```

profile of v0, /device:TPU:32, one launch (start us, length us, event | category | flops | bytes accessed | tf_op | source)
XLA Modules:
  0.0 519.7 jit_solution(5378864188823617936)
XLA Ops:
  9.2 143.8 %while.71 = (s32[]{:T(128)}, bf16[16,128,256]{2,1,0:T(8,128)(2,1)}, f32[16,128]{1,0:T(8,128)S(1)}, f32[16,2,30,128]{3,2,1,0:T(8,128)S(1)}, f32[128]{0:T(128)S(1)...) while((s32[]{:T(128)}, bf16[16,128,256]{2,1,0:T(8,128)(2,1)}, ...), condition=%wide.region_3.4_spmd, body=%wide.region_0.3_spmd.sunk | while | flops 2768899 | bytes 491161 | solution.py:33
  9.2 8.0 %cosine_reduce_fusion.2 = (f32[128,128]{1,0:T(8,128)S(1)}, bf16[128,128]{1,0:T(8,128)(2,1)S(1)}) fusion(f32[128]{0:T(128)S(1)} %get-tuple-element.994, f32[30,128]{1,0:T(8,128)S(1)} %get-tuple-element.950, f32[128]{0:T(128)S(1)} %get-tuple-element.993, f32[30,128]{1,0:T(8,128)S(1)} %get-tuple-element.951), kind=kLoop, calls=%fused_computation.1.clone.1 | loop fusion | flops 2424832 | bytes 130048 | tf_op jit(solution)/shard_map/while/body/eval_jaxpr/reduce_sum | solution.py:28
  18.2 8.0 %cosine_reduce_fusion.2 = (f32[128,128]{1,0:T(8,128)S(1)}, bf16[128,128]{1,0:T(8,128)(2,1)S(1)}) fusion(f32[128]{0:T(128)S(1)} %get-tuple-element.994, f32[30,128]{1,0:T(8,128)S(1)} %get-tuple-element.950, f32[128]{0:T(128)S(1)} %get-tuple-element.993, f32[30,128]{1,0:T(8,128)S(1)} %get-tuple-element.951), kind=kLoop, calls=%fused_computation.1.clone.1 | loop fusion | flops 2424832 | bytes 130048 | tf_op jit(solution)/shard_map/while/body/eval_jaxpr/reduce_sum | solution.py:28
  27.2 8.0 %cosine_reduce_fusion.2 = (f32[128,128]{1,0:T(8,128)S(1)}, bf16[128,128]{1,0:T(8,128)(2,1)S(1)}) fusion(f32[128]{0:T(128)S(1)} %get-tuple-element.994, f32[30,128]{1,0:T(8,128)S(1)} %get-tuple-element.950, f32[128]{0:T(128)S(1)} %get-tuple-element.993, f32[30,128]{1,0:T(8,128)S(1)} %get-tuple-element.951), kind=kLoop, calls=%fused_computation.1.clone.1 | loop fusion | flops 2424832 | bytes 130048 | tf_op jit(solution)/shard_map/while/body/eval_jaxpr/reduce_sum | solution.py:28
  36.2 8.0 %cosine_reduce_fusion.2 = (f32[128,128]{1,0:T(8,128)S(1)}, bf16[128,128]{1,0:T(8,128)(2,1)S(1)}) fusion(f32[128]{0:T(128)S(1)} %get-tuple-element.994, f32[30,128]{1,0:T(8,128)S(1)} %get-tuple-element.950, f32[128]{0:T(128)S(1)} %get-tuple-element.993, f32[30,128]{1,0:T(8,128)S(1)} %get-tuple-element.951), kind=kLoop, calls=%fused_computation.1.clone.1 | loop fusion | flops 2424832 | bytes 130048 | tf_op jit(solution)/shard_map/while/body/eval_jaxpr/reduce_sum | solution.py:28
  45.2 8.0 %cosine_reduce_fusion.2 = (f32[128,128]{1,0:T(8,128)S(1)}, bf16[128,128]{1,0:T(8,128)(2,1)S(1)}) fusion(f32[128]{0:T(128)S(1)} %get-tuple-element.994, f32[30,128]{1,0:T(8,128)S(1)} %get-tuple-element.950, f32[128]{0:T(128)S(1)} %get-tuple-element.993, f32[30,128]{1,0:T(8,128)S(1)} %get-tuple-element.951), kind=kLoop, calls=%fused_computation.1.clone.1 | loop fusion | flops 2424832 | bytes 130048 | tf_op jit(solution)/shard_map/while/body/eval_jaxpr/reduce_sum | solution.py:28
  54.1 8.0 %cosine_reduce_fusion.2 = (f32[128,128]{1,0:T(8,128)S(1)}, bf16[128,128]{1,0:T(8,128)(2,1)S(1)}) fusion(f32[128]{0:T(128)S(1)} %get-tuple-element.994, f32[30,128]{1,0:T(8,128)S(1)} %get-tuple-element.950, f32[128]{0:T(128)S(1)} %get-tuple-element.993, f32[30,128]{1,0:T(8,128)S(1)} %get-tuple-element.951), kind=kLoop, calls=%fused_computation.1.clone.1 | loop fusion | flops 2424832 | bytes 130048 | tf_op jit(solution)/shard_map/while/body/eval_jaxpr/reduce_sum | solution.py:28
  63.1 8.0 %cosine_reduce_fusion.2 = (f32[128,128]{1,0:T(8,128)S(1)}, bf16[128,128]{1,0:T(8,128)(2,1)S(1)}) fusion(f32[128]{0:T(128)S(1)} %get-tuple-element.994, f32[30,128]{1,0:T(8,128)S(1)} %get-tuple-element.950, f32[128]{0:T(128)S(1)} %get-tuple-element.993, f32[30,128]{1,0:T(8,128)S(1)} %get-tuple-element.951), kind=kLoop, calls=%fused_computation.1.clone.1 | loop fusion | flops 2424832 | bytes 130048 | tf_op jit(solution)/shard_map/while/body/eval_jaxpr/reduce_sum | solution.py:28
  72.1 8.0 %cosine_reduce_fusion.2 = (f32[128,128]{1,0:T(8,128)S(1)}, bf16[128,128]{1,0:T(8,128)(2,1)S(1)}) fusion(f32[128]{0:T(128)S(1)} %get-tuple-element.994, f32[30,128]{1,0:T(8,128)S(1)} %get-tuple-element.950, f32[128]{0:T(128)S(1)} %get-tuple-element.993, f32[30,128]{1,0:T(8,128)S(1)} %get-tuple-element.951), kind=kLoop, calls=%fused_computation.1.clone.1 | loop fusion | flops 2424832 | bytes 130048 | tf_op jit(solution)/shard_map/while/body/eval_jaxpr/reduce_sum | solution.py:28
  81.1 8.0 %cosine_reduce_fusion.2 = (f32[128,128]{1,0:T(8,128)S(1)}, bf16[128,128]{1,0:T(8,128)(2,1)S(1)}) fusion(f32[128]{0:T(128)S(1)} %get-tuple-element.994, f32[30,128]{1,0:T(8,128)S(1)} %get-tuple-element.950, f32[128]{0:T(128)S(1)} %get-tuple-element.993, f32[30,128]{1,0:T(8,128)S(1)} %get-tuple-element.951), kind=kLoop, calls=%fused_computation.1.clone.1 | loop fusion | flops 2424832 | bytes 130048 | tf_op jit(solution)/shard_map/while/body/eval_jaxpr/reduce_sum | solution.py:28
  90.1 8.0 %cosine_reduce_fusion.2 = (f32[128,128]{1,0:T(8,128)S(1)}, bf16[128,128]{1,0:T(8,128)(2,1)S(1)}) fusion(f32[128]{0:T(128)S(1)} %get-tuple-element.994, f32[30,128]{1,0:T(8,128)S(1)} %get-tuple-element.950, f32[128]{0:T(128)S(1)} %get-tuple-element.993, f32[30,128]{1,0:T(8,128)S(1)} %get-tuple-element.951), kind=kLoop, calls=%fused_computation.1.clone.1 | loop fusion | flops 2424832 | bytes 130048 | tf_op jit(solution)/shard_map/while/body/eval_jaxpr/reduce_sum | solution.py:28
  99.1 8.0 %cosine_reduce_fusion.2 = (f32[128,128]{1,0:T(8,128)S(1)}, bf16[128,128]{1,0:T(8,128)(2,1)S(1)}) fusion(f32[128]{0:T(128)S(1)} %get-tuple-element.994, f32[30,128]{1,0:T(8,128)S(1)} %get-tuple-element.950, f32[128]{0:T(128)S(1)} %get-tuple-element.993, f32[30,128]{1,0:T(8,128)S(1)} %get-tuple-element.951), kind=kLoop, calls=%fused_computation.1.clone.1 | loop fusion | flops 2424832 | bytes 130048 | tf_op jit(solution)/shard_map/while/body/eval_jaxpr/reduce_sum | solution.py:28
  108.1 8.0 %cosine_reduce_fusion.2 = (f32[128,128]{1,0:T(8,128)S(1)}, bf16[128,128]{1,0:T(8,128)(2,1)S(1)}) fusion(f32[128]{0:T(128)S(1)} %get-tuple-element.994, f32[30,128]{1,0:T(8,128)S(1)} %get-tuple-element.950, f32[128]{0:T(128)S(1)} %get-tuple-element.993, f32[30,128]{1,0:T(8,128)S(1)} %get-tuple-element.951), kind=kLoop, calls=%fused_computation.1.clone.1 | loop fusion | flops 2424832 | bytes 130048 | tf_op jit(solution)/shard_map/while/body/eval_jaxpr/reduce_sum | solution.py:28
  117.1 8.0 %cosine_reduce_fusion.2 = (f32[128,128]{1,0:T(8,128)S(1)}, bf16[128,128]{1,0:T(8,128)(2,1)S(1)}) fusion(f32[128]{0:T(128)S(1)} %get-tuple-element.994, f32[30,128]{1,0:T(8,128)S(1)} %get-tuple-element.950, f32[128]{0:T(128)S(1)} %get-tuple-element.993, f32[30,128]{1,0:T(8,128)S(1)} %get-tuple-element.951), kind=kLoop, calls=%fused_computation.1.clone.1 | loop fusion | flops 2424832 | bytes 130048 | tf_op jit(solution)/shard_map/while/body/eval_jaxpr/reduce_sum | solution.py:28
  126.0 8.0 %cosine_reduce_fusion.2 = (f32[128,128]{1,0:T(8,128)S(1)}, bf16[128,128]{1,0:T(8,128)(2,1)S(1)}) fusion(f32[128]{0:T(128)S(1)} %get-tuple-element.994, f32[30,128]{1,0:T(8,128)S(1)} %get-tuple-element.950, f32[128]{0:T(128)S(1)} %get-tuple-element.993, f32[30,128]{1,0:T(8,128)S(1)} %get-tuple-element.951), kind=kLoop, calls=%fused_computation.1.clone.1 | loop fusion | flops 2424832 | bytes 130048 | tf_op jit(solution)/shard_map/while/body/eval_jaxpr/reduce_sum | solution.py:28
  135.0 8.0 %cosine_reduce_fusion.2 = (f32[128,128]{1,0:T(8,128)S(1)}, bf16[128,128]{1,0:T(8,128)(2,1)S(1)}) fusion(f32[128]{0:T(128)S(1)} %get-tuple-element.994, f32[30,128]{1,0:T(8,128)S(1)} %get-tuple-element.950, f32[128]{0:T(128)S(1)} %get-tuple-element.993, f32[30,128]{1,0:T(8,128)S(1)} %get-tuple-element.951), kind=kLoop, calls=%fused_computation.1.clone.1 | loop fusion | flops 2424832 | bytes 130048 | tf_op jit(solution)/shard_map/while/body/eval_jaxpr/reduce_sum | solution.py:28
  144.0 8.0 %cosine_reduce_fusion.2 = (f32[128,128]{1,0:T(8,128)S(1)}, bf16[128,128]{1,0:T(8,128)(2,1)S(1)}) fusion(f32[128]{0:T(128)S(1)} %get-tuple-element.994, f32[30,128]{1,0:T(8,128)S(1)} %get-tuple-element.950, f32[128]{0:T(128)S(1)} %get-tuple-element.993, f32[30,128]{1,0:T(8,128)S(1)} %get-tuple-element.951), kind=kLoop, calls=%fused_computation.1.clone.1 | loop fusion | flops 2424832 | bytes 130048 | tf_op jit(solution)/shard_map/while/body/eval_jaxpr/reduce_sum | solution.py:28
  153.8 7.7 %while.72 = (s32[]{:T(128)}, f32[4,2,2,512]{3,0,2,1:T(4,128)S(1)}, bf16[4,512,256]{2,1,0:T(8,128)(2,1)}, bf16[256,2,256]{2,0,1:T(8,128)(2,1)}, bf16[256,2,256]{2...) while((s32[]{:T(128)}, f32[4,2,2,512]{3,0,2,1:T(4,128)S(1)}, ...), condition=%wide.region_5.6_spmd, body=%wide.region_4.5_spmd.sunk | while | flops 270270464 | bytes 2927193 | solution.py:96
  153.8 1.3 convolution_tanh_fusion.6
  155.8 1.3 convolution_tanh_fusion.6
  157.7 1.3 convolution_tanh_fusion.6
  159.6 1.3 convolution_tanh_fusion.6
  162.7 4.3 all-to-all-start.1
  168.7 3.7 all-to-all-done.1
  172.4 3.3 all-to-all-start
  180.8 1.2 scatter.106
  184.2 1.2 scatter.110
  186.1 1.2 scatter.115
  191.1 1.2 scatter.116
  192.9 1.2 scatter.121
  194.5 1.2 scatter.120
  196.4 1.2 scatter.125
  201.3 1.4 scatter.126
  203.4 1.2 scatter.131
  208.4 1.2 scatter.134
  210.3 1.2 scatter.139
  211.8 1.2 scatter.136
  213.7 1.2 scatter.141
  218.7 1.2 scatter.144
  220.5 1.2 scatter.149
  222.1 1.2 scatter.146
  224.0 1.2 scatter.151
  230.9 80.7 %all-reduce = (f32[16,16]{1,0:T(8,128)S(1)}, f32[]{:T(128)}) all-reduce(f32[16,16]{1,0:T(8,128)S(1)} %bitcast.342, f32[]{:T(128)} %convert_reduce_fusion), channel_id=1, replica_groups=mesh['state'=8,'walker'=32] {'state','walker'}, use_global_device_ids=true, to_apply=%region_6.7 | all-reduce | flops 257 | bytes 2056 | tf_op jit(solution)/shard_map/psum | solution.py:126
  311.6 1.8 select_reduce_fusion
  316.9 3.3 all-to-all-start.2
  321.1 4.5 all-to-all-done.2
  325.6 3.3 all-to-all-start.3
  330.3 3.9 all-to-all-done.3
  335.3 26.6 %while.73 = (s32[]{:T(128)}, f32[256,2,256]{2,0,1:T(8,128)}, f32[256,2,256]{0,2,1:T(8,128)}, f32[2,2,256]{2,0,1:T(2,128)S(1)}, bf16[4,512,256]{2,1,0:T(8,128)(2,...) while((s32[]{:T(128)}, f32[256,2,256]{2,0,1:T(8,128)}, ...), condition=%wide.region_12.13_spmd.clone, body=%wide.region_11.12_spmd.clone.sunk | while | flops 678168576 | bytes 17058944 | solution.py:174
  335.3 1.3 convolution_tanh_fusion.7
  338.5 2.3 fusion.123
  341.0 1.3 convolution_tanh_fusion.7
  343.0 2.2 fusion.124
  345.2 2.5 fusion.123
  347.9 1.3 convolution_tanh_fusion.7
  350.0 2.2 fusion.124
  352.2 2.5 fusion.123
  354.9 1.3 convolution_tanh_fusion.7
  356.9 2.2 fusion.124
  359.1 2.5 fusion.123
  361.8 2.3 copy.299
  365.2 71.4 %psum.39 = f32[2,2,256]{2,1,0:T(2,128)} all-reduce(f32[2,2,256]{2,1,0:T(2,128)S(1)} %copy.301), channel_id=1, replica_groups=mesh['state'=8,'walker'=32] {'walker'}, use_global_device_ids=true, to_apply=%region_15.16 | all-reduce | flops 1024 | bytes 8192 | tf_op jit(solution)/shard_map/psum | solution.py:175
  436.6 73.4 %all-reduce.4.cloned.1.call-done = (f32[256,2,256]{2,1,0:T(2,128)}, f32[256,2,256]{2,1,0:T(2,128)}) async-done(((f32[256,2,256]{2,1,0:T(2,128)}, f32[256,2,256]{2,1,0:T(2,128)}), (f32[256,2,256]{2,1,0:T(2,128)}, f32[256,2,256]{2,1,0:T(2,128)})) %all-reduce.4.cloned.1.call-update) | async-done | bytes 1048592 | tf_op jit(solution)/shard_map/psum | solution.py:175
  510.0 2.1 copy.418
  (323 shorter events, 67.1 us)
Async XLA Ops:
  9.2 143.8 %copy-start.2 = (bf16[256,2,256]{2,1,0:T(2,128)(2,1)S(1)}, bf16[256,2,256]{2,1,0:T(2,128)(2,1)}, u32[]{:S(2)}) copy-start(bf16[256,2,256]{2,1,0:T(2,128)(2,1)} %param.79) | copy-start | bytes 786436
  9.2 144.6 %copy-start.3 = (bf16[256,2,256]{2,1,0:T(2,128)(2,1)S(1)}, bf16[256,2,256]{2,1,0:T(2,128)(2,1)}, u32[]{:S(2)}) copy-start(bf16[256,2,256]{2,1,0:T(2,128)(2,1)} %param.80) | copy-start | bytes 786436
  9.2 8.7 %copy-start.4 = (f32[128]{0:T(128)S(1)}, f32[128]{0:T(128)}, u32[]{:S(2)}) copy-start(f32[128]{0:T(128)} %get-tuple-element.995) | copy-start | bytes 1540 | tf_op jit(solution)/shard_map/while
  18.2 8.7 %copy-start.4 = (f32[128]{0:T(128)S(1)}, f32[128]{0:T(128)}, u32[]{:S(2)}) copy-start(f32[128]{0:T(128)} %get-tuple-element.995) | copy-start | bytes 1540 | tf_op jit(solution)/shard_map/while
  27.2 8.7 %copy-start.4 = (f32[128]{0:T(128)S(1)}, f32[128]{0:T(128)}, u32[]{:S(2)}) copy-start(f32[128]{0:T(128)} %get-tuple-element.995) | copy-start | bytes 1540 | tf_op jit(solution)/shard_map/while
  36.2 8.7 %copy-start.4 = (f32[128]{0:T(128)S(1)}, f32[128]{0:T(128)}, u32[]{:S(2)}) copy-start(f32[128]{0:T(128)} %get-tuple-element.995) | copy-start | bytes 1540 | tf_op jit(solution)/shard_map/while
  45.2 8.7 %copy-start.4 = (f32[128]{0:T(128)S(1)}, f32[128]{0:T(128)}, u32[]{:S(2)}) copy-start(f32[128]{0:T(128)} %get-tuple-element.995) | copy-start | bytes 1540 | tf_op jit(solution)/shard_map/while
  54.1 8.7 %copy-start.4 = (f32[128]{0:T(128)S(1)}, f32[128]{0:T(128)}, u32[]{:S(2)}) copy-start(f32[128]{0:T(128)} %get-tuple-element.995) | copy-start | bytes 1540 | tf_op jit(solution)/shard_map/while
  63.1 8.7 %copy-start.4 = (f32[128]{0:T(128)S(1)}, f32[128]{0:T(128)}, u32[]{:S(2)}) copy-start(f32[128]{0:T(128)} %get-tuple-element.995) | copy-start | bytes 1540 | tf_op jit(solution)/shard_map/while
  72.1 8.7 %copy-start.4 = (f32[128]{0:T(128)S(1)}, f32[128]{0:T(128)}, u32[]{:S(2)}) copy-start(f32[128]{0:T(128)} %get-tuple-element.995) | copy-start | bytes 1540 | tf_op jit(solution)/shard_map/while
  81.1 8.7 %copy-start.4 = (f32[128]{0:T(128)S(1)}, f32[128]{0:T(128)}, u32[]{:S(2)}) copy-start(f32[128]{0:T(128)} %get-tuple-element.995) | copy-start | bytes 1540 | tf_op jit(solution)/shard_map/while
  90.1 8.7 %copy-start.4 = (f32[128]{0:T(128)S(1)}, f32[128]{0:T(128)}, u32[]{:S(2)}) copy-start(f32[128]{0:T(128)} %get-tuple-element.995) | copy-start | bytes 1540 | tf_op jit(solution)/shard_map/while
  99.1 8.7 %copy-start.4 = (f32[128]{0:T(128)S(1)}, f32[128]{0:T(128)}, u32[]{:S(2)}) copy-start(f32[128]{0:T(128)} %get-tuple-element.995) | copy-start | bytes 1540 | tf_op jit(solution)/shard_map/while
  108.1 8.7 %copy-start.4 = (f32[128]{0:T(128)S(1)}, f32[128]{0:T(128)}, u32[]{:S(2)}) copy-start(f32[128]{0:T(128)} %get-tuple-element.995) | copy-start | bytes 1540 | tf_op jit(solution)/shard_map/while
  117.1 8.7 %copy-start.4 = (f32[128]{0:T(128)S(1)}, f32[128]{0:T(128)}, u32[]{:S(2)}) copy-start(f32[128]{0:T(128)} %get-tuple-element.995) | copy-start | bytes 1540 | tf_op jit(solution)/shard_map/while
  126.0 8.7 %copy-start.4 = (f32[128]{0:T(128)S(1)}, f32[128]{0:T(128)}, u32[]{:S(2)}) copy-start(f32[128]{0:T(128)} %get-tuple-element.995) | copy-start | bytes 1540 | tf_op jit(solution)/shard_map/while
  135.0 8.7 %copy-start.4 = (f32[128]{0:T(128)S(1)}, f32[128]{0:T(128)}, u32[]{:S(2)}) copy-start(f32[128]{0:T(128)} %get-tuple-element.995) | copy-start | bytes 1540 | tf_op jit(solution)/shard_map/while
  144.0 8.7 %copy-start.4 = (f32[128]{0:T(128)S(1)}, f32[128]{0:T(128)}, u32[]{:S(2)}) copy-start(f32[128]{0:T(128)} %get-tuple-element.995) | copy-start | bytes 1540 | tf_op jit(solution)/shard_map/while
  153.0 0.8 copy-start.6
  161.5 6.4 %copy-start.5 = (s32[128]{0:T(128)S(1)}, s32[128]{0:T(128)}, u32[]{:S(2)}) copy-start(s32[128]{0:T(128)} %param.78) | copy-start | bytes 1540
  162.7 9.7 %all-to-all-start.1 = ((f32[8,1,512]{2,1,0:T(1,128)}), f32[8,1,512]{2,1,0:T(1,128)S(1)}, u32[]{:S(2)}, u32[]{:S(2)}) async-start(f32[8,1,512]{2,1,0:T(1,128)} %reshape.1533), calls=%async_computation.1 | async-start | bytes 32768 | tf_op jit(solution)/shard_map/all_to_all | solution.py:113
  172.4 54.6 %all-to-all-start = ((f32[8,1,512]{2,1,0:T(1,128)}), f32[8,1,512]{2,1,0:T(1,128)S(1)}, u32[]{:S(2)}, u32[]{:S(2)}) async-start(f32[8,1,512]{2,1,0:T(1,128)} %reshape.1531), calls=%async_computation | async-start | bytes 32768 | tf_op jit(solution)/shard_map/all_to_all | solution.py:116
  316.9 8.6 %all-to-all-start.2 = ((f32[8,1,512]{2,1,0:T(1,128)}), f32[8,1,512]{2,1,0:T(1,128)S(1)}, u32[]{:S(2)}, u32[]{:S(2)}) async-start(f32[8,1,512]{2,1,0:T(1,128)} %reshape.1537), calls=%async_computation.2 | async-start | bytes 32768 | tf_op jit(solution)/shard_map/all_to_all | solution.py:132
  325.6 8.6 %all-to-all-start.3 = ((f32[8,1,512]{2,1,0:T(1,128)}), f32[8,1,512]{2,1,0:T(1,128)S(1)}, u32[]{:S(2)}, u32[]{:S(2)}) async-start(f32[8,1,512]{2,1,0:T(1,128)} %reshape.1535), calls=%async_computation.3 | async-start | bytes 32768 | tf_op jit(solution)/shard_map/all_to_all | solution.py:133
  328.9 181.1 %all-reduce.4.cloned.1.call-start = ((), (), s32[]{:S(2)}) async-start(), calls=%async_computation.4 | async-start | bytes 2097152 | tf_op jit(solution)/shard_map/psum | solution.py:175
  361.8 2.3 copy-start
  510.0 2.1 copy-start.1
Sparse Core Ops, SparseCore 0:
  365.3 144.6 all-reduce.3
where the time goes:
time: 522 us; the launch traced here: 520 us
  other arithmetic  155 us (30%)
  blocking collectives  152 us (29%)
  waiting for transfers between devices  85.6 us (16%)
  local copies, waits for them, and re-layouts  56.3 us (11%)
  matrix products  38.3 us (7%)
  between operations  16.4 us (3%)
  starting transfers between devices  14.6 us (3%)
    reduce_sum x16, other arithmetic, one_block(): cosines = jnp.sum(jnp.cos(phase), axis=0)  129 us
    psum x1, blocking collectives, shards(): lax.psum((weighted, jnp.sum(weights)), ('state', 'walker'))  80.7 us
    psum x1, waiting for transfers between devices, shards(): lax.psum((grad_one, grad_two, grad_three), 'walker')  73.4 us
    psum x1, blocking collectives, shards(): lax.psum((grad_one, grad_two, grad_three), 'walker')  71.4 us
    scatter x16, local copies, waits for them, and re-layouts, invert(): inverse = inverse.at[pivot].set(row_inverse)  18.8 us
    scatter x15, local copies, waits for them, and re-layouts, invert(): matrix = matrix.at[pivot].set(row_matrix)  17.4 us
    dot_general x8, matrix products, hidden_block(): jnp.einsum('rf,fsh->rsh', portion, w_one, preferred_element_type=jnp.floa...  10.6 us
  transfers between devices with their start and end apart: 5, of which 4 were waited for; matrix products, arithmetic and copies ran while one was open for 10% of the time, Pallas kernels for 0%

commit v1 on v0

v1 whole, which is shorter than its diff:
```python
import jax
import jax.numpy as jnp
import numpy as np
from jax import lax
from jax.experimental import pallas as pl
from jax.experimental.pallas import tpu as pltpu
from jax.sharding import PartitionSpec as P

F32 = jnp.float32
BF16 = jnp.bfloat16
INV_ROOT_THREE = 1.0 / 1.7320508075688772
BASIS = 64
COSINES = 25
CHUNK = 256
NN = (((1,), (0,)), ((), ()))
NT = (((1,), (1,)), ((), ()))


def half_turn_polynomials():
    squares = np.linspace(0.0, 0.25, 4001)
    root = np.sqrt(squares)
    ratio = np.where(root > 0, np.sin(np.pi * root) / np.where(root > 0, root, 1.0), np.pi)
    cheb = np.polynomial.chebyshev.Chebyshev
    sine = cheb.fit(squares, ratio, 5).convert(kind=np.polynomial.Polynomial).coef
    cosine = cheb.fit(squares, np.cos(np.pi * root), 6).convert(kind=np.polynomial.Polynomial).coef
    return [float(c) for c in sine], [float(c) for c in cosine]


SIN_COEF, COS_COEF = half_turn_polynomials()


def horner(coef, at):
    total = jnp.full_like(at, coef[-1])
    for c in coef[-2::-1]:
        total = total * at + c
    return total


def turn(t):
    rest = t - jnp.round(t)
    square = rest * rest
    sine = rest * horner(SIN_COEF, square)
    cosine = horner(COS_COEF, square)
    return 1.0 - 2.0 * sine * sine, 2.0 * sine * cosine


def mul(a, b):
    return a[0] * b[0] - a[1] * b[1], a[0] * b[1] + a[1] * b[0]


def selection(recip, copies):
    count = recip.shape[1]
    key = 7 * recip[0:1, :] + recip[1:2, :]
    size = jnp.abs(key)
    row = lax.broadcasted_iota(jnp.int32, (BASIS * copies, count), 0) % BASIS
    cosine = jnp.where(row == size, 1.0, 0.0)
    sign = jnp.where(key < 0, -1.0, 1.0)
    sine = jnp.where((row == size + (COSINES - 1)) & (size > 0), sign, 0.0)
    return cosine, sine


def three_parts(value):
    high = value.astype(BF16)
    rest = value - high.astype(F32)
    middle = rest.astype(BF16)
    low = (rest - middle.astype(F32)).astype(BF16)
    return high, middle, low


def forward_kernel(pos, recip, coef, w_one, w_two, w_heads, send, potential, basis, first, second,
                   turns, sums, w_eff, w_two_t, basis_three):
    electrons, slots, walkers = pos.shape[1:]
    states = w_one.shape[0]

    def phases(e, carry):
        x, y = pos[0, e], pos[1, e]
        third = y * INV_ROOT_THREE
        turns[0, e], turns[1, e] = turn(x - third)
        turns[2, e], turns[3, e] = turn(2.0 * third)
        return carry

    lax.fori_loop(0, electrons, phases, 0, unroll=5)

    def powers(e, rows, at, upto):
        one = (turns[at, e, rows], turns[at + 1, e, rows])
        result = [one]
        for _ in range(upto - 1):
            result.append(mul(result[-1], one))
        return result

    for half in range(slots // 8):
        rows = pl.ds(half * 8, 8)

        def put(index, value, half=half):
            sums[pl.ds(half * 8 * BASIS + index, 8, stride=BASIS), :] = value

        zero = jnp.zeros((8, walkers), F32)
        for firsts in ((1, 2), (3,)):
            alone = 3 in firsts

            def add(e, totals, firsts=firsts, alone=alone, rows=rows):
                u, v = powers(e, rows, 0, 3 if alone else 2), powers(e, rows, 2, 3)
                parts = []
                for m in firsts:
                    for n in (1, 2, 3):
                        (cu, su), (cv, sv) = u[m - 1], v[n - 1]
                        parts += [cu * cv, su * sv, su * cv, cu * sv]
                if alone:
                    for p in u + v:
                        parts += list(p)
                return tuple(t + p for t, p in zip(totals, parts, strict=True))

            number = 12 * len(firsts) + (12 if alone else 0)
            totals = lax.fori_loop(0, electrons, add, (zero,) * number, unroll=2)
            for i, m in enumerate(firsts):
                for n in (1, 2, 3):
                    cc, ss, sc, cs = totals[12 * i + 4 * (n - 1) : 12 * i + 4 * n]
                    put(7 * m + n, cc - ss)
                    put(7 * m - n, cc + ss)
                    put(COSINES - 1 + 7 * m + n, sc + cs)
                    put(COSINES - 1 + 7 * m - n, sc - cs)
            if alone:
                rest = totals[12:]
                for m in (1, 2, 3):
                    put(7 * m, rest[2 * (m - 1)])
                    put(COSINES - 1 + 7 * m, rest[2 * (m - 1) + 1])
                    put(m, rest[6 + 2 * (m - 1)])
                    put(COSINES - 1 + m, rest[6 + 2 * (m - 1) + 1])
        put(0, jnp.full((8, walkers), float(electrons), F32))
        for index in range(2 * COSINES - 1, BASIS):
            put(index, zero)

    cosine, sine = selection(recip[...], 1)
    basis_coef = jnp.sum(cosine * coef[...], axis=1, keepdims=True)
    for slot in range(slots):
        tile = sums[pl.ds(slot * BASIS, BASIS), :]
        potential[pl.ds(slot, 1), :] = jnp.sum(tile * basis_coef, axis=0, keepdims=True)
        rounded = tile.astype(BF16)
        lanes = pl.ds(slot * walkers, walkers)
        basis[:, lanes] = rounded
        for copy in range(3):
            basis_three[pl.ds(copy * BASIS, BASIS), lanes] = rounded

    cosine, sine = selection(recip[...], 3)
    select = jnp.concatenate([cosine, sine], axis=1).astype(BF16)
    part = lax.broadcasted_iota(jnp.int32, (3 * BASIS, w_one.shape[2]), 0) // BASIS
    for s in range(states):
        value = lax.dot_general(select, w_one[s], NN, preferred_element_type=F32)
        high, middle, low = (p.astype(F32) for p in three_parts(value))
        value = jnp.where(part == 0, high, jnp.where(part == 1, middle, low))
        w_eff[s] = value.T.astype(BF16)
        w_two_t[s] = w_two[s].astype(F32).T.astype(BF16)

    def chunk(c, carry):
        lanes = pl.ds(pl.multiple_of(c * CHUNK, CHUNK), CHUNK)
        for s in range(states):
            pre = lax.dot_general(w_eff[s], basis_three[:, lanes], NN, preferred_element_type=F32)
            first_act = jnp.tanh(pre)
            first[s, :, lanes] = first_act
            pre = lax.dot_general(w_two_t[s], first_act.astype(BF16), NN, preferred_element_type=F32)
            second_tanh = jnp.tanh(pre)
            second[s, :, lanes] = second_tanh
            second_bf = (second_tanh + first_act).astype(BF16)
            out = lax.dot_general(w_heads[s], second_bf, NN, preferred_element_type=F32)
            for k in range(CHUNK // walkers):
                slot = c * (CHUNK // walkers) + k
                at = slice(k * walkers, (k + 1) * walkers)
                squashed = jnp.tanh(out[0:1, at])
                other = out[1:2, at]
                for d in range(send.shape[0]):
                    send[d, pl.ds(s * 2 * slots + slot, 1), :] = squashed
                    send[d, pl.ds((s * 2 + 1) * slots + slot, 1), :] = other
        return carry

    lax.fori_loop(0, slots * walkers // CHUNK, chunk, 0)


def energy_kernel(spread, gathered, potential, counts, message, d_amp, d_hps, inverse_t):
    slots, walkers = potential.shape
    weights = counts[...].astype(F32)
    column = lax.broadcasted_iota(jnp.int32, (slots, walkers), 0)
    rows = []
    for j in range(slots):
        squashed = gathered[pl.ds(j, slots, stride=2 * slots), :]
        rows.append(jnp.where(column == j, 1.0, 0.0) + spread * squashed)
    for p in range(slots):
        factor = 1.0 / rows[p][p : p + 1, :]
        pivot = jnp.where(column == p, factor, rows[p] * factor)
        for r in range(slots):
            if r != p:
                rows[r] = jnp.where(column == p, 0.0, rows[r]) - rows[r][p : p + 1, :] * pivot
        rows[p] = pivot
    for j in range(slots):
        inverse_t[j] = rows[j]
    pot = potential[...]
    energies = [jnp.zeros((slots, walkers), F32) for _ in range(slots)]
    for j in range(slots):
        squashed = gathered[pl.ds(2 * slots * j, slots), :]
        amplitude = jnp.where(column == j, 1.0, 0.0) + spread * squashed
        hps = gathered[pl.ds(2 * slots * j + slots, slots), :] + pot * amplitude
        for k in range(slots):
            energies[k] = energies[k] + rows[j] * hps[k : k + 1, :]
    trace = jnp.zeros((1, walkers), F32)
    lane = lax.broadcasted_iota(jnp.int32, (8, walkers), 1)
    note = jnp.where(lane == 2 * slots, jnp.sum(weights, axis=1, keepdims=True), 0.0)
    for k in range(slots):
        trace = trace + energies[k][k : k + 1, :]
        total = jnp.sum(energies[k] * weights, axis=1, keepdims=True)
        for half in range(slots // 8):
            note = jnp.where(lane == half * slots + k, total[half * 8 : half * 8 + 8], note)
    for d in range(message.shape[0]):
        message[d] = note
    states = d_amp.shape[0]
    for s in range(states):
        own = inverse_t[lax.axis_index("state") * states + s]
        along = jnp.zeros((slots, walkers), F32)
        for k in range(slots):
            along = along + own[k : k + 1, :] * energies[k]
        d_amp[s] = weights * (2.0 * trace * own - along)
        d_hps[s] = weights * own


def backward_kernel(spread, messages, d_amp, d_hps, send, potential, basis, first, second, w_two,
                    w_heads, out, energy, cot, w_heads_t, first_bf, inner_one, inner_two):
    states, slots, walkers = d_amp.shape
    hidden = w_two.shape[1]
    note = messages[0]
    for d in range(1, messages.shape[0]):
        note = note + messages[d]
    lane = lax.broadcasted_iota(jnp.int32, note.shape, 1)
    sub = lax.broadcasted_iota(jnp.int32, note.shape, 0)
    count = jnp.max(jnp.where((lane == 2 * slots) & (sub == 0), note, 0.0))
    share = 1.0 / jnp.full((1, walkers), count, F32)
    diagonal = jnp.zeros(note.shape, jnp.bool_)
    for half in range(slots // 8):
        diagonal = diagonal | (lane == half * (slots + 8) + sub)
    mean = jnp.sum(jnp.where(diagonal, note, 0.0)) * share
    matrix = note * share
    for half in range(slots // 8):
        energy[pl.ds(half * 8, 8), :] = matrix[:, half * slots : (half + 1) * slots]
    pot = potential[...]
    cot[...] = jnp.zeros(cot.shape, F32)
    for s in range(states):
        squashed = send[0, pl.ds(s * 2 * slots, slots), :]
        hps = d_hps[s] * share
        amp = (d_amp[s] - 2.0 * mean * d_hps[s]) * share
        amp = (amp + hps * pot) * (spread * (1.0 - squashed * squashed))
        for slot in range(slots):
            lanes = pl.ds(slot * walkers, walkers)
            cot[s, 0:1, lanes] = amp[slot : slot + 1, :]
            cot[s, 1:2, lanes] = hps[slot : slot + 1, :]
        w_heads_t[s] = w_heads[s].astype(F32).T.astype(BF16)

    def put(start, s, value):
        for half in range(hidden // 128):
            at = pl.ds(4 * start + 2 * half + s, value.shape[0], stride=4)
            out[at, :] = value[:, half * 128 : (half + 1) * 128]

    heads0 = (jnp.zeros((16, hidden), F32),) * states

    def chunk(c, heads):
        lanes = pl.ds(pl.multiple_of(c * CHUNK, CHUNK), CHUNK)
        result = []
        for s in range(states):
            cot_bf = cot[s, :, lanes].astype(BF16)
            first_act = first[s, :, lanes]
            second_tanh = second[s, :, lanes]
            second_bf = (second_tanh + first_act).astype(BF16)
            result.append(heads[s] + lax.dot_general(cot_bf, second_bf, NT, preferred_element_type=F32))
            back_two = lax.dot_general(w_heads_t[s], cot_bf, NN, preferred_element_type=F32)
            inner = (back_two * (1.0 - second_tanh * second_tanh)).astype(BF16)
            inner_two[s, :, lanes] = inner
            back_one = back_two + lax.dot_general(w_two[s], inner, NN, preferred_element_type=F32)
            inner_one[s, :, lanes] = (back_one * (1.0 - first_act * first_act)).astype(BF16)
            first_bf[s, :, lanes] = first_act.astype(BF16)
        return tuple(result)

    heads = lax.fori_loop(0, slots * walkers // CHUNK, chunk, heads0)
    for s in range(states):
        grad_two = lax.dot_general(first_bf[s], inner_two[s], NT, preferred_element_type=F32)
        put(BASIS, s, grad_two)
        grad_one = lax.dot_general(basis[...], inner_one[s], NT, preferred_element_type=F32)
        put(0, s, grad_one)
        put(2 * COSINES - 1, s, heads[s][0:2])


def expand_kernel(summed, recip, grad_first, grad_second, grad_heads):
    cosine, sine = selection(recip[...], 3)
    select = jnp.concatenate([cosine, sine], axis=1).T.astype(BF16)
    states = grad_first.shape[1]
    rows = grad_second.shape[0]
    for half in range(2):
        lanes = pl.ds(half * 128, 128)
        for s in range(states):
            value = summed[pl.ds(2 * half + s, BASIS, stride=4), :]
            parts = jnp.concatenate(three_parts(value), axis=0)
            grad_first[:, s, lanes] = lax.dot_general(select, parts, NN, preferred_element_type=F32)
            grad_second[:, s, lanes] = summed[pl.ds(4 * BASIS + 2 * half + s, rows, stride=4), :]
            grad_heads[:, s, lanes] = value[2 * COSINES - 1 : 2 * COSINES + 1]


def vmem(count):
    return [pl.BlockSpec(memory_space=pltpu.VMEM)] * count


def call(body, outs, scratch, limit, *args):
    return pl.pallas_call(
        body,
        out_shape=[jax.ShapeDtypeStruct(s, t) for s, t in outs],
        in_specs=vmem(len(args)),
        out_specs=vmem(len(outs)),
        scratch_shapes=[pltpu.VMEM(s, t) for s, t in scratch],
        compiler_params=pltpu.CompilerParams(vmem_limit_bytes=limit << 20),
    )(*args)


def shards(positions, recip, moire_coef, counts, w_first, w_second, w_heads):
    electrons, slots, walkers = positions.shape[1:]
    features, states, hidden = w_first.shape
    rows = slots * walkers
    groups, shares = lax.axis_size("state"), lax.axis_size("walker")
    spread = 0.75 / slots
    w_one = jnp.moveaxis(w_first, 1, 0)
    w_two = jnp.moveaxis(w_second, 1, 0)
    heads = jnp.pad(jnp.moveaxis(w_heads, 1, 0), ((0, 0), (0, 16 - w_heads.shape[0]), (0, 0)))
    send, potential, basis, first, second = call(
        forward_kernel,
        [((groups, 4 * slots, walkers), F32), ((slots, walkers), F32), ((BASIS, rows), BF16),
         ((states, hidden, rows), F32), ((states, hidden, rows), F32)],
        [((4, electrons, slots, walkers), F32), ((slots * BASIS, walkers), F32),
         ((states, hidden, 3 * BASIS), BF16), ((states, hidden, hidden), BF16), ((3 * BASIS, rows), BF16)],
        40, positions, recip, moire_coef[None], w_one, w_two, heads)
    gathered = lax.all_to_all(send, "state", 0, 0, tiled=True)
    def energy_body(*refs):
        energy_kernel(spread, *refs)
    message, d_amp, d_hps = call(
        energy_body,
        [((shares, 8, walkers), F32), ((states, slots, walkers), F32), ((states, slots, walkers), F32)],
        [((slots, slots, walkers), F32)],
        16, gathered.reshape(groups * 4 * slots, walkers), potential, counts[None])
    messages = lax.all_to_all(message, "walker", 0, 0, tiled=True)
    total = 4 * (BASIS + hidden)
    def backward_body(*refs):
        backward_kernel(spread, *refs)
    grads, energy_matrix = call(
        backward_body,
        [((total, 128), F32), ((slots, slots), F32)],
        [((states, 16, rows), F32), ((states, hidden, 16), BF16), ((states, hidden, rows), BF16),
         ((states, hidden, rows), BF16), ((states, hidden, rows), BF16)],
        40, messages, d_amp, d_hps, send, potential, basis, first, second, w_two, heads)
    pieces = lax.all_to_all(grads.reshape(shares, total // shares, 128), "walker", 0, 0, tiled=True)
    piece = jnp.broadcast_to(jnp.sum(pieces, axis=0)[None], pieces.shape)
    summed = lax.all_to_all(piece, "walker", 0, 0, tiled=True)
    grad_first, grad_second, grad_heads = call(
        expand_kernel,
        [(w_first.shape, F32), (w_second.shape, F32), (w_heads.shape, F32)],
        [], 16, summed.reshape(total, 128), recip)
    return (energy_matrix, grad_first, grad_second, grad_heads)


def solution(mesh):
    in_specs = (
        P(None, None, None, "walker"),
        P(),
        P(),
        P("walker"),
        P(None, "state", None),
        P(None, "state", None),
        P(None, "state", None),
    )
    out_specs = (P(), P(None, "state", None), P(None, "state", None), P(None, "state", None))
    return jax.shard_map(shards, mesh=mesh, in_specs=in_specs, out_specs=out_specs, check_vma=False)
```

time: 522 us -> 103 us (0.20)
  other arithmetic: 155 us -> 0.05 us
  waiting for transfers between devices: 85.6 us -> 0 us
  blocking collectives: 152 us -> 78.2 us
  local copies, waits for them, and re-layouts: 56.3 us -> 4.86 us
  matrix products: 38.3 us -> 0 us
  Pallas kernels: 0 us -> 18.9 us
  between operations: 16.4 us -> 0.66 us
  starting transfers between devices: 14.6 us -> 0 us
    psum x2 -> x0, blocking collectives: 152 us -> none  [the longest x1 80.7 us: shards(): lax.psum((weighted, jnp.sum(weights)), ('state', 'walker'))]
    reduce_sum x18 -> x1, other arithmetic: 131 us -> 0.05 us  [shards(): piece = jnp.broadcast_to(jnp.sum(pieces, axis=0)[None], pieces.shape)]
    all_to_all x0 -> x4, blocking collectives: none -> 78.2 us  [the longest x1 23.2 us: shards(): lax.all_to_all(grads.reshape(shares, total // shares, 128), 'walker', 0,...]
    psum x1 -> x0, waiting for transfers between devices: 73.4 us -> none  [shards(): lax.psum((grad_one, grad_two, grad_three), 'walker')]
    dot_general x51 -> x0, matrix products: 38.3 us -> none  [the longest x8 10.6 us: hidden_block(): jnp.einsum('rf,fsh->rsh', portion, w_one, preferred_element_type=jnp.floa...]
    scatter x31 -> x0, local copies, waits for them, and re-layouts: 36.2 us -> none  [the longest x16 18.8 us: invert(): inverse = inverse.at[pivot].set(row_inverse)]
    pallas_call x0 -> x4, Pallas kernels: none -> 18.9 us  [call(): pl.pallas_call(body, out_shape=[jax.ShapeDtypeStruct(s, t) for s, t in ou...]
    all_to_all x4 -> x0, starting transfers between devices: 14.3 us -> none  [the longest x1 4.31 us: shards(): lax.all_to_all(amplitude.reshape(split_shape), 'state', split_axis=2, con...]
  transfers between devices with their start and end apart: 5 -> 0, of which waited for: 4 -> 0; matrix products, arithmetic and copies ran while one was open for 10% -> 0% of each run, Pallas kernels for 0% -> 0%
where the time goes in v1:
time: 103 us
  blocking collectives  78.2 us (76%)
  Pallas kernels  18.9 us (18%)
  local copies, waits for them, and re-layouts  4.86 us (5%)
    all_to_all x1, blocking collectives, shards(): lax.all_to_all(grads.reshape(shares, total // shares, 128), 'walker', 0,...  23.2 us
    all_to_all x1, blocking collectives, shards(): summed = lax.all_to_all(piece, 'walker', 0, 0, tiled=True)  22.6 us
    all_to_all x1, blocking collectives, shards(): messages = lax.all_to_all(message, 'walker', 0, 0, tiled=True)  20.8 us
    pallas_call x4, Pallas kernels, call(): pl.pallas_call(body, out_shape=[jax.ShapeDtypeStruct(s, t) for s, t in ou...  18.9 us
    all_to_all x1, blocking collectives, shards(): gathered = lax.all_to_all(send, 'state', 0, 0, tiled=True)  11.6 us
    unnamed x11, local copies, waits for them, and re-layouts  3.7 us

profile of v1, /device:TPU:32, one launch (start us, length us, event | category | flops | bytes accessed | tf_op | source)
XLA Modules:
  0.0 102.8 jit_solution(16078241547080482638)
XLA Ops:
  0.6 0.7 copy.17
  1.3 1.1 %copy_bitcast_fusion = (bf16[2,256,256]{2,1,0:T(8,128)(2,1)S(1)}, bf16[2,256,256]{2,1,0:T(8,128)(2,1)S(1)}) fusion(bf16[256,2,256]{2,1,0:T(2,128)(2,1)} %param.12, bf16[256,2,256]{2,1,0:T(2,128)(2,1)} %param.11), kind=kLoop, calls=%fused_computation | loop fusion | bytes 1048576 | tf_op jit(solution)/shard_map/transpose | solution.py:324
  2.4 0.0 copy-start
  2.4 1.0 copy-done
  3.5 0.0 copy-start.1
  3.5 0.7 copy-done.1
  4.1 0.0 copy-start.3
  4.1 0.7 copy-done.3
  4.8 9.1 %shard_map.102 = (f32[8,64,128]{2,1,0:T(8,128)S(1)}, f32[16,128]{1,0:T(8,128)S(1)}, bf16[64,2048]{1,0:T(8,128)(2,1)S(1)}, f32[2,256,2048]{2,1,0:T(8,128)S(1)}, f32[2,256,2048]{2,1,0:T(8,128)S(1)}) custom-call(f32[2,30,16,128]{3,2,1,0:T(8,128)S(1)} %copy-done, s32[2,128]{1,0:T(2,128)S(1)} %copy-done.1, f32[1,128]{1,0:T(1,128)S(1)} %bitcast.15, ...), custom_call_target="tpu_custom_call" | custom-call | tf_op jit(solution)/shard_map/pallas_call | solution.py:307
  13.9 11.6 %all_to_all.20 = f32[8,64,128]{2,1,0:T(8,128)S(1)} all-to-all(f32[8,64,128]{2,1,0:T(8,128)S(1)} %get-tuple-element.17.refs_3_), channel_id=1, replica_groups=mesh['state'=8,'walker'=32] {'state'}, dimensions={0} | all-to-all | bytes 524288 | tf_op jit(solution)/shard_map/all_to_all | solution.py:333
  25.5 0.0 copy-start.4
  25.5 0.7 copy-done.4
  26.1 0.6 shard_map.103
  26.8 20.8 %all_to_all.21.refs_0_ = f32[32,8,128]{2,1,0:T(8,128)S(1)} all-to-all(f32[32,8,128]{2,1,0:T(8,128)S(1)} %get-tuple-element.19), channel_id=1, replica_groups=mesh['state'=8,'walker'=32] {'walker'}, dimensions={0} | all-to-all | bytes 262144 | tf_op jit(solution)/shard_map/all_to_all | solution.py:341
  47.6 0.0 copy-start.2
  47.6 7.6 %shard_map.104 = (f32[1280,128]{1,0:T(8,128)S(1)}, f32[16,16]{1,0:T(8,128)}) custom-call(f32[32,8,128]{2,1,0:T(8,128)S(1)} %all_to_all.21.refs_0_, f32[2,16,128]{2,1,0:T(8,128)S(1)} %get-tuple-element.20.refs_1_, f32[2,16,128]{2,1,0:T(8,128)S(1)} %get-tuple-element.21.refs_2_, f32[8,64,128]{2,1,0:T(8,128)S(1)} %get-tuple-element.17.refs_3_, ...), custom_call_target="tpu_custom_call" | custom-call | tf_op jit(solution)/shard_map/pallas_call | solution.py:307
  55.2 23.2 %all_to_all.22 = f32[32,40,128]{2,1,0:T(8,128)S(1)} all-to-all(f32[32,40,128]{2,1,0:T(8,128)S(1)} %bitcast.14), channel_id=1, replica_groups=mesh['state'=8,'walker'=32] {'walker'}, dimensions={0} | all-to-all | bytes 1310720 | tf_op jit(solution)/shard_map/all_to_all | solution.py:351
  78.3 0.1 reduce_sum.9
  78.4 22.6 %all_to_all.23 = f32[32,40,128]{2,1,0:T(8,128)S(1)} all-to-all(f32[32,40,128]{2,1,0:T(8,128)S(1)} %broadcast_in_dim.14), channel_id=1, replica_groups=mesh['state'=8,'walker'=32] {'walker'}, dimensions={0} | all-to-all | bytes 1310720 | tf_op jit(solution)/shard_map/all_to_all | solution.py:353
  101.1 0.0 copy-done.2
  101.1 1.7 %shard_map.105 = (f32[256,2,256]{2,1,0:T(2,128)}, f32[256,2,256]{2,1,0:T(2,128)}, f32[2,2,256]{2,1,0:T(2,128)}) custom-call(f32[1280,128]{1,0:T(8,128)S(1)} %bitcast.12, s32[2,128]{1,0:T(2,128)S(1)} %copy-done.2), custom_call_target="tpu_custom_call" | custom-call | tf_op jit(solution)/shard_map/pallas_call | solution.py:307
  (2 shorter events, 0.1 us)
Async XLA Ops:
  2.4 1.0 %copy-start = (f32[2,30,16,128]{3,2,1,0:T(8,128)S(1)}, f32[2,30,16,128]{3,2,1,0:T(8,128)}, u32[]{:S(2)}) copy-start(f32[2,30,16,128]{3,2,1,0:T(8,128)} %pos.1) | copy-start | bytes 1474564
  3.5 0.7 copy-start.1
  4.1 0.7 copy-start.3
  25.5 0.7 copy-start.4
  47.6 53.5 %copy-start.2 = (s32[2,128]{1,0:T(2,128)S(1)}, s32[2,128]{1,0:T(2,128)}, u32[]{:S(2)}) copy-start(s32[2,128]{1,0:T(2,128)} %recip.3) | copy-start | bytes 3076

commit v2 on v1

v2 whole, which is shorter than its diff:
```python
import jax
import jax.numpy as jnp
import numpy as np
from jax import lax
from jax.experimental import pallas as pl
from jax.experimental.pallas import tpu as pltpu
from jax.sharding import Mesh
from jax.sharding import PartitionSpec as P

F32 = jnp.float32
BF16 = jnp.bfloat16
INV_ROOT_THREE = 1.0 / 1.7320508075688772
XS, YS, ZS = 4, 4, 8
BASIS = 64
COSINES = 25
NN = (((1,), (0,)), ((), ()))
NT = (((1,), (1,)), ((), ()))


def half_turn_polynomials():
    squares = np.linspace(0.0, 0.25, 4001)
    root = np.sqrt(squares)
    ratio = np.where(root > 0, np.sin(np.pi * root) / np.where(root > 0, root, 1.0), np.pi)
    cheb = np.polynomial.chebyshev.Chebyshev
    sine = cheb.fit(squares, ratio, 5).convert(kind=np.polynomial.Polynomial).coef
    cosine = cheb.fit(squares, np.cos(np.pi * root), 6).convert(kind=np.polynomial.Polynomial).coef
    return [float(c) for c in sine], [float(c) for c in cosine]


SIN_COEF, COS_COEF = half_turn_polynomials()


def horner(coef, at):
    total = jnp.full_like(at, coef[-1])
    for c in coef[-2::-1]:
        total = total * at + c
    return total


def turn(t):
    rest = t - jnp.round(t)
    square = rest * rest
    sine = rest * horner(SIN_COEF, square)
    cosine = horner(COS_COEF, square)
    return 1.0 - 2.0 * sine * sine, 2.0 * sine * cosine


def mul(a, b):
    return a[0] * b[0] - a[1] * b[1], a[0] * b[1] + a[1] * b[0]


def selection(recip, copies):
    count = recip.shape[1]
    key = 7 * recip[0:1, :] + recip[1:2, :]
    size = jnp.abs(key)
    row = lax.broadcasted_iota(jnp.int32, (BASIS * copies, count), 0) % BASIS
    cosine = jnp.where(row == size, 1.0, 0.0)
    sign = jnp.where(key < 0, -1.0, 1.0)
    sine = jnp.where((row == size + (COSINES - 1)) & (size > 0), sign, 0.0)
    return cosine, sine


def three_parts(value):
    high = value.astype(BF16)
    rest = value - high.astype(F32)
    middle = rest.astype(BF16)
    low = (rest - middle.astype(F32)).astype(BF16)
    return high, middle, low


def forward_kernel(pos_in, recip_in, coef_in, counts_in, w_one_in, w_two_in, w_heads_in,
                   send, potential, basis, first, second, weights, select_out, w_two, w_heads_t,
                   pos, recip, coef, counts, w_one_raw, w_two_raw, w_heads_raw, arrived,
                   turns, sums, w_eff, w_two_t, basis_three):
    electrons, slots, walkers = pos.shape[1:]
    states = w_two.shape[0]
    copies = []
    for source, target in ((pos_in, pos), (recip_in, recip), (coef_in, coef), (counts_in, counts),
                           (w_one_in, w_one_raw), (w_two_in, w_two_raw), (w_heads_in, w_heads_raw)):
        copies.append(pltpu.make_async_copy(source, target, arrived.at[len(copies)]))
        copies[-1].start()
    copies[0].wait()

    def phases(e, carry):
        x, y = pos[0, e], pos[1, e]
        third = y * INV_ROOT_THREE
        turns[0, e], turns[1, e] = turn(x - third)
        turns[2, e], turns[3, e] = turn(2.0 * third)
        return carry

    lax.fori_loop(0, electrons, phases, 0, unroll=5)

    def powers(e, rows, at, upto):
        one = (turns[at, e, rows], turns[at + 1, e, rows])
        result = [one]
        for _ in range(upto - 1):
            result.append(mul(result[-1], one))
        return result

    for half in range(slots // 8):
        rows = pl.ds(half * 8, 8)

        def put(index, value, half=half):
            sums[pl.ds(half * 8 * BASIS + index, 8, stride=BASIS), :] = value

        zero = jnp.zeros((8, walkers), F32)
        for firsts in ((1, 2), (3,)):
            alone = 3 in firsts

            def add(e, totals, firsts=firsts, alone=alone, rows=rows):
                u, v = powers(e, rows, 0, 3 if alone else 2), powers(e, rows, 2, 3)
                parts = []
                for m in firsts:
                    for n in (1, 2, 3):
                        (cu, su), (cv, sv) = u[m - 1], v[n - 1]
                        parts += [cu * cv, su * sv, su * cv, cu * sv]
                if alone:
                    for p in u + v:
                        parts += list(p)
                return tuple(t + p for t, p in zip(totals, parts, strict=True))

            number = 12 * len(firsts) + (12 if alone else 0)
            totals = lax.fori_loop(0, electrons, add, (zero,) * number, unroll=2)
            for i, m in enumerate(firsts):
                for n in (1, 2, 3):
                    cc, ss, sc, cs = totals[12 * i + 4 * (n - 1) : 12 * i + 4 * n]
                    put(7 * m + n, cc - ss)
                    put(7 * m - n, cc + ss)
                    put(COSINES - 1 + 7 * m + n, sc + cs)
                    put(COSINES - 1 + 7 * m - n, sc - cs)
            if alone:
                rest = totals[12:]
                for m in (1, 2, 3):
                    put(7 * m, rest[2 * (m - 1)])
                    put(COSINES - 1 + 7 * m, rest[2 * (m - 1) + 1])
                    put(m, rest[6 + 2 * (m - 1)])
                    put(COSINES - 1 + m, rest[6 + 2 * (m - 1) + 1])
        put(0, jnp.full((8, walkers), float(electrons), F32))
        for index in range(2 * COSINES - 1, BASIS):
            put(index, zero)

    for copy in copies[1:]:
        copy.wait()
    weights[...] = counts[...].astype(F32)
    cosine, sine = selection(recip[...], 1)
    basis_coef = jnp.sum(cosine * coef[...], axis=1, keepdims=True)
    for slot in range(slots):
        tile = sums[pl.ds(slot * BASIS, BASIS), :]
        potential[pl.ds(slot, 1), :] = jnp.sum(tile * basis_coef, axis=0, keepdims=True)
        rounded = tile.astype(BF16)
        lanes = pl.ds(slot * walkers, walkers)
        basis[:, lanes] = rounded
        for copy in range(3):
            basis_three[pl.ds(copy * BASIS, BASIS), lanes] = rounded

    cosine, sine = selection(recip[...], 3)
    select = jnp.concatenate([cosine, sine], axis=1)
    select_out[...] = select.T.astype(BF16)
    select = select.astype(BF16)
    part = lax.broadcasted_iota(jnp.int32, (3 * BASIS, w_two.shape[2]), 0) // BASIS
    heads = []
    for s in range(states):
        value = lax.dot_general(select, w_one_raw[:, s, :], NN, preferred_element_type=F32)
        high, middle, low = (p.astype(F32) for p in three_parts(value))
        value = jnp.where(part == 0, high, jnp.where(part == 1, middle, low))
        w_eff[s] = value.T.astype(BF16)
        value = w_two_raw[:, s, :]
        w_two[s] = value
        w_two_t[s] = value.astype(F32).T.astype(BF16)
        value = w_heads_raw[:, s, :].astype(F32)
        value = jnp.concatenate([value, jnp.zeros((16 - value.shape[0], value.shape[1]), F32)], axis=0)
        heads.append(value.astype(BF16))
        w_heads_t[s, 0] = value.T.astype(BF16)
        value = jnp.concatenate([jnp.zeros((2, value.shape[1]), F32), value[0:1], jnp.zeros((13, value.shape[1]), F32)], axis=0)
        w_heads_t[s, 1] = value.T.astype(BF16)

    for s in range(states):
        pre = lax.dot_general(w_eff[s], basis_three[...], NN, preferred_element_type=F32)
        first_act = jnp.tanh(pre)
        first[s] = first_act
        pre = lax.dot_general(w_two_t[s], first_act.astype(BF16), NN, preferred_element_type=F32)
        second_tanh = jnp.tanh(pre)
        second[s] = second_tanh
        second_bf = (second_tanh + first_act).astype(BF16)
        out = lax.dot_general(heads[s], second_bf, NN, preferred_element_type=F32)
        for slot in range(slots):
            at = slice(slot * walkers, (slot + 1) * walkers)
            send[pl.ds(s * 2 * slots + slot, 1), :] = jnp.tanh(out[0:1, at])
            send[pl.ds((s * 2 + 1) * slots + slot, 1), :] = out[1:2, at]


def invert_transposed(spread, gathered, slots, walkers):
    column = lax.broadcasted_iota(jnp.int32, (slots, walkers), 0)
    rows = []
    for j in range(slots):
        squashed = gathered[pl.ds(j, slots, stride=2 * slots), :]
        rows.append(jnp.where(column == j, 1.0, 0.0) + spread * squashed)
    for p in range(slots):
        factor = 1.0 / rows[p][p : p + 1, :]
        pivot = jnp.where(column == p, factor, rows[p] * factor)
        for r in range(slots):
            if r != p:
                rows[r] = jnp.where(column == p, 0.0, rows[r]) - rows[r][p : p + 1, :] * pivot
        rows[p] = pivot
    return rows


def backward_kernel(spread, *refs):
    along_x, refs = refs[:XS], refs[XS:]
    others, potential, weights_in, basis, first, second, w_two, w_heads_t = refs[:8]
    outs, (gathered, inverse_t, value, slope, cot, first_bf, inner_one, inner_two) = refs[8 : 8 + YS], refs[8 + YS :]
    send = along_x[0]
    slots, walkers = potential.shape
    states, hidden = w_two.shape[:2]
    rows_number = slots * walkers
    block = send.shape[0]
    me_x, me_core = lax.axis_index("x"), lax.axis_index("core")
    for k in range(XS):
        for at, source in ((me_core, along_x[k]), (1 - me_core, others.at[k])):
            owner = (me_x + XS - k) % XS * 2 + at
            gathered[pl.ds(pl.multiple_of(owner * block, block), block), :] = source[...]

    weights = weights_in[...]
    rows = invert_transposed(spread, gathered, slots, walkers)
    for j in range(slots):
        inverse_t[j] = rows[j]
    pot = potential[...]
    column = lax.broadcasted_iota(jnp.int32, (slots, walkers), 0)
    energies = [jnp.zeros((slots, walkers), F32) for _ in range(slots)]
    for j in range(slots):
        squashed = gathered[pl.ds(2 * slots * j, slots), :]
        amplitude = jnp.where(column == j, 1.0, 0.0) + spread * squashed
        hps = gathered[pl.ds(2 * slots * j + slots, slots), :] + pot * amplitude
        for k in range(slots):
            energies[k] = energies[k] + rows[j] * hps[k : k + 1, :]
    trace = jnp.zeros((1, walkers), F32)
    lane = lax.broadcasted_iota(jnp.int32, (8, walkers), 1)
    sums = jnp.zeros((8, walkers), F32)
    for k in range(slots):
        trace = trace + energies[k][k : k + 1, :]
        total = jnp.sum(energies[k] * weights, axis=1, keepdims=True)
        for half in range(slots // 8):
            sums = jnp.where(lane == half * slots + k, total[half * 8 : half * 8 + 8], sums)
    count = jnp.sum(weights, axis=1, keepdims=True)
    level = jnp.sum(trace * weights, axis=1, keepdims=True)
    center = level / count
    note = jnp.where(lane == 0, level, jnp.where(lane == 1, count, 0.0))

    cot[...] = jnp.zeros(cot.shape, F32)
    for s in range(states):
        own = inverse_t[(me_x * 2 + me_core) * states + s]
        along_own = jnp.zeros((slots, walkers), F32)
        for k in range(slots):
            along_own = along_own + own[k : k + 1, :] * energies[k]
        hps = weights * own
        amp = weights * (2.0 * (trace - center) * own - along_own)
        squashed = send[pl.ds(s * 2 * slots, slots), :]
        bend = spread * (1.0 - squashed * squashed)
        amp = (amp + hps * pot) * bend
        steep = -2.0 * hps * bend
        for slot in range(slots):
            lanes = pl.ds(slot * walkers, walkers)
            cot[s, 0:1, lanes] = amp[slot : slot + 1, :]
            cot[s, 1:2, lanes] = hps[slot : slot + 1, :]
            cot[s, 2:3, lanes] = steep[slot : slot + 1, :]

    def put(target, start, s, array):
        for half in range(hidden // 128):
            at = pl.ds(4 * start + 2 * half + s, array.shape[0], stride=4)
            target[at, :] = array[:, half * 128 : (half + 1) * 128]

    heads = []
    for s in range(states):
        first_act = first[s]
        second_tanh = second[s]
        second_bf = (second_tanh + first_act).astype(BF16)
        first_bf[s] = first_act.astype(BF16)
        bend_one = 1.0 - first_act * first_act
        bend_two = 1.0 - second_tanh * second_tanh
        cot_bf = cot[s].astype(BF16)
        heads.append(lax.dot_general(cot_bf, second_bf, NT, preferred_element_type=F32))
        for t in range(2):
            back_two = lax.dot_general(w_heads_t[s, t], cot_bf, NN, preferred_element_type=F32)
            inner = (back_two * bend_two).astype(BF16)
            inner_two[s, t] = inner
            back_one = back_two + lax.dot_general(w_two[s], inner, NN, preferred_element_type=F32)
            inner_one[s, t] = (back_one * bend_one).astype(BF16)
    for t, target in enumerate((value, slope)):
        spare = 4 * (2 * COSINES - 1)
        target[pl.ds(spare, 4 * BASIS - spare), :] = jnp.zeros((4 * BASIS - spare, 128), F32)
        for s in range(states):
            grad_two = lax.dot_general(first_bf[s], inner_two[s, t], NT, preferred_element_type=F32)
            put(target, BASIS, s, grad_two)
            grad_one = lax.dot_general(basis[...], inner_one[s, t], NT, preferred_element_type=F32)
            put(target, 0, s, grad_one[0 : 2 * COSINES - 1])
            put(target, 2 * COSINES - 1, s, heads[s][2 * t : 2 * t + 2])
    value[pl.ds(4 * (2 * COSINES + 1), 8), :] = sums
    part = value.shape[0] // YS
    y = lax.axis_index("y")
    for k in range(YS):
        at = pl.ds(pl.multiple_of((y + k) % YS * part, part), part)
        outs[k][pl.ds(0, part), :] = value[at, :] - center * slope[at, :]
        outs[k][pl.ds(part, part), :] = slope[at, :]
        outs[k][pl.ds(2 * part, 8), :] = note


def line_kernel(*refs):
    parts, out = refs[:YS], refs[YS]
    part = (parts[0].shape[0] - 8) // 2
    size = part // ZS

    def added(start, length):
        total = parts[0][pl.ds(start, length), :]
        for k in range(1, YS):
            total = total + parts[k][pl.ds(start, length), :]
        return total

    for z in range(ZS):
        out[z, 0:size] = added(z * size, size)
        out[z, size : 2 * size] = added(part + z * size, size)
        out[z, 2 * size : 2 * size + 8] = added(2 * part, 8)


def piece_kernel(parts, out):
    size = out.shape[1]
    total = parts[0]
    for z in range(1, ZS):
        total = total + parts[z]
    note = total[2 * size : 2 * size + 1]
    share = 1.0 / note[:, 1:2]
    mean = note[:, 0:1] * share
    piece = (total[0:size] + mean * total[size : 2 * size]) * share
    for z in range(ZS):
        out[z] = piece


def expand_kernel(*refs):
    parts, (select_in, energy, grad_first, grad_second, grad_heads, summed) = refs[:YS], refs[YS:]
    y = lax.axis_index("y")
    part = parts[0].shape[0]
    for k in range(YS):
        summed[pl.ds(pl.multiple_of((y + YS - k) % YS * part, part), part), :] = parts[k][...]
    select = select_in[...]
    slots = energy.shape[0]
    note = summed[pl.ds(4 * (2 * COSINES + 1), 8), :]
    for half in range(slots // 8):
        energy[pl.ds(half * 8, 8), :] = note[:, half * slots : (half + 1) * slots]
    states = grad_first.shape[1]
    rows = grad_second.shape[0]
    for half in range(2):
        lanes = pl.ds(half * 128, 128)
        for s in range(states):
            value = summed[pl.ds(2 * half + s, BASIS, stride=4), :]
            parts = jnp.concatenate(three_parts(value), axis=0)
            grad_first[:, s, lanes] = lax.dot_general(select, parts, NN, preferred_element_type=F32)
            grad_second[:, s, lanes] = summed[pl.ds(4 * BASIS + 2 * half + s, rows, stride=4), :]
            grad_heads[:, s, lanes] = value[2 * COSINES - 1 : 2 * COSINES + 1]


def call(body, outs, scratch, limit, args, flops, hbm=False):
    place = pltpu.HBM if hbm else pltpu.VMEM
    if hbm:
        args = [pltpu.with_memory_space_constraint(a, pltpu.HBM) for a in args]
    return pl.pallas_call(
        body,
        out_shape=[jax.ShapeDtypeStruct(s, t) for s, t in outs],
        in_specs=[pl.BlockSpec(memory_space=place)] * len(args),
        out_specs=[pl.BlockSpec(memory_space=pltpu.VMEM)] * len(outs),
        scratch_shapes=[pltpu.VMEM(*s) if isinstance(s, tuple) else s for s in scratch],
        compiler_params=pltpu.CompilerParams(vmem_limit_bytes=limit << 20),
        cost_estimate=pl.CostEstimate(flops=flops, bytes_accessed=1 << 20, transcendentals=0),
    )(*args)


def along(axis, array, shift):
    size = lax.axis_size(axis)
    return lax.ppermute(array, axis, [(d, (d + shift) % size) for d in range(size)])


def shards(positions, recip, moire_coef, counts, w_first, w_second, w_heads):
    electrons, slots, walkers = positions.shape[1:]
    features, states, hidden = w_first.shape
    rows = slots * walkers
    groups = lax.axis_size(("x", "core"))
    spread = 0.75 / slots
    total = 4 * (BASIS + hidden)
    work = 2 * states * rows * hidden * hidden
    args = (positions, recip, moire_coef[None], counts[None], w_first, w_second, w_heads)
    send, potential, basis, first, second, weights, select, w_two, w_heads_t = call(
        forward_kernel,
        [((4 * slots, walkers), F32), ((slots, walkers), F32), ((BASIS, rows), BF16),
         ((states, hidden, rows), F32), ((states, hidden, rows), F32), ((1, walkers), F32),
         ((features, 3 * BASIS), BF16), ((states, hidden, hidden), BF16), ((states, 2, hidden, 16), BF16)],
        [(a.shape, a.dtype) for a in args] + [pltpu.SemaphoreType.DMA((len(args),))]
        + [((4, electrons, slots, walkers), F32), ((slots * BASIS, walkers), F32),
           ((states, hidden, 3 * BASIS), BF16), ((states, hidden, hidden), BF16), ((3 * BASIS, rows), BF16)],
        40, args, 2 * work, hbm=True)
    along_x = [send] + [along("x", send, k) for k in range(1, XS)]
    others = along("core", jnp.stack(along_x), 1)

    def backward_body(*refs):
        backward_kernel(spread, *refs)

    part = total // YS
    size = part // ZS
    parts = call(
        backward_body,
        [((2 * part + 8, 128), F32)] * YS,
        [((groups * 4 * slots, walkers), F32), ((slots, slots, walkers), F32), ((total, 128), F32),
         ((total, 128), F32), ((states, 16, rows), F32), ((states, hidden, rows), BF16),
         ((states, 2, hidden, rows), BF16), ((states, 2, hidden, rows), BF16)],
        24, (*along_x, others, potential, weights, basis, first, second, w_two, w_heads_t), 6 * work)
    parts = [parts[0]] + [along("y", parts[k], k) for k in range(1, YS)]
    lines, = call(line_kernel, [((ZS, 2 * size + 8, 128), F32)], [], 4, parts, 1 << 20)
    lines = lax.all_to_all(lines, "z", 0, 0, tiled=True)
    pieces, = call(piece_kernel, [((ZS, size, 128), F32)], [], 4, (lines,), 1 << 20)
    summed = lax.all_to_all(pieces, "z", 0, 0, tiled=True).reshape(part, 128)
    parts = [summed] + [along("y", summed, k) for k in range(1, YS)]
    return call(
        expand_kernel,
        [((slots, slots), F32), (w_first.shape, F32), (w_second.shape, F32), (w_heads.shape, F32)],
        [((total, 128), F32)], 8, (*parts, select), 1 << 20)


def solution(mesh):
    mesh = Mesh(mesh.devices.reshape(XS, 2, YS, ZS), ("x", "core", "y", "z"))
    state, walker = ("x", "core"), ("y", "z")
    in_specs = (
        P(None, None, None, walker),
        P(),
        P(),
        P(walker),
        P(None, state, None),
        P(None, state, None),
        P(None, state, None),
    )
    out_specs = (P(), P(None, state, None), P(None, state, None), P(None, state, None))
    return jax.shard_map(shards, mesh=mesh, in_specs=in_specs, out_specs=out_specs, check_vma=False)
```

time: 103 us -> 90.1 us (0.87)
  blocking collectives: 78.2 us -> 32.2 us
  waiting for transfers between devices: 0 us -> 26.9 us
  starting transfers between devices: 0 us -> 14.4 us
  local copies, waits for them, and re-layouts: 4.86 us -> 0 us
  Pallas kernels: 18.9 us -> 15.8 us
    all_to_all x4 -> x2, blocking collectives: 78.2 us -> 32.2 us  [the longest x1 20.4 us: shards(): lines = lax.all_to_all(lines, 'z', 0, 0, tiled=True)]
    ppermute x0 -> x10, waiting for transfers between devices: none -> 26.9 us  [along(): lax.ppermute(array, axis, [(d, (d + shift) % size) for d in range(size)])]
    ppermute x0 -> x10, starting transfers between devices: none -> 14.4 us  [along(): lax.ppermute(array, axis, [(d, (d + shift) % size) for d in range(size)])]
    unnamed x11 -> x0, local copies, waits for them, and re-layouts: 3.7 us -> none
    pallas_call x4 -> x5, Pallas kernels: 18.9 us -> 15.8 us  [call(): pl.pallas_call(body, out_shape=[jax.ShapeDtypeStruct(s, t) for s, t in ou...]
    transpose x1 -> x0, local copies, waits for them, and re-layouts: 1.1 us -> none  [shards(): w_two = jnp.moveaxis(w_second, 1, 0)]
  transfers between devices with their start and end apart: 0 -> 10, of which waited for: 0 -> 8; matrix products, arithmetic and copies ran while one was open for 0% -> 0% of each run, Pallas kernels for 0% -> 0%
where the time goes in v2:
time: 90.1 us; the launch traced here: 89.9 us
  blocking collectives  32.2 us (36%)
  waiting for transfers between devices  26.9 us (30%)
  Pallas kernels  15.8 us (18%)
  starting transfers between devices  14.4 us (16%)
    ppermute x10, waiting for transfers between devices, along(): lax.ppermute(array, axis, [(d, (d + shift) % size) for d in range(size)])  26.9 us
    all_to_all x1, blocking collectives, shards(): lines = lax.all_to_all(lines, 'z', 0, 0, tiled=True)  20.4 us
    pallas_call x5, Pallas kernels, call(): pl.pallas_call(body, out_shape=[jax.ShapeDtypeStruct(s, t) for s, t in ou...  15.8 us
    ppermute x10, starting transfers between devices, along(): lax.ppermute(array, axis, [(d, (d + shift) % size) for d in range(size)])  14.4 us
    all_to_all x1, blocking collectives, shards(): summed = lax.all_to_all(pieces, 'z', 0, 0, tiled=True).reshape(part, 128)  11.8 us
  transfers between devices with their start and end apart: 10, of which 8 were waited for; matrix products, arithmetic and copies ran while one was open for 0% of the time, Pallas kernels for 0%

profile of v2, /device:TPU:32, one launch (start us, length us, event | category | flops | bytes accessed | tf_op | source)
XLA Modules:
  0.0 89.9 jit_solution(17309032264022429573)
XLA Ops:
  0.6 6.8 %shard_map.102 = (f32[64,128]{1,0:T(8,128)S(1)}, f32[16,128]{1,0:T(8,128)S(1)}, bf16[64,2048]{1,0:T(8,128)(2,1)S(1)}, f32[2,256,2048]{2,1,0:T(8,128)S(1)}, f32[2...) custom-call(f32[2,30,16,128]{3,2,1,0:T(8,128)} %pos_in.1, ...), custom_call_target="tpu_custom_call" | custom-call | flops 1073741824 | bytes 1048576 | tf_op jit(solution)/shard_map/pallas_call | solution.py:364
  7.5 2.8 %collective-permute-start.2 = (f32[64,128]{1,0:T(8,128)S(1)}, f32[64,128]{1,0:T(8,128)S(1)}, u32[]{:S(2)}, u32[]{:S(2)}) collective-permute-start(f32[64,128]{1,0:T(8,128)S(1)} %get-tuple-element.17.refs_0_), channel_id=1, source_target_pairs={{0,192},{64,0},{128,64},{192,128},{1,193},{65,1},{129,65},{193,129... | collective-permute-start | bytes 98312 | tf_op jit(solution)/shard_map/ppermute | solution.py:377
  10.3 0.8 collective-permute-start.1
  11.1 0.9 collective-permute-start
  12.0 0.0 collective-permute-done.2.refs_3_
  12.0 3.7 %collective-permute-done.1.refs_2_ = f32[64,128]{1,0:T(8,128)S(1)} collective-permute-done((f32[64,128]{1,0:T(8,128)S(1)}, f32[64,128]{1,0:T(8,128)S(1)}, u32[]{:S(2)}, u32[]{:S(2)}) %collective-permute-start.1) | collective-permute-done | bytes 32800 | tf_op jit(solution)/shard_map/ppermute | solution.py:377
  15.7 0.5 collective-permute-done.refs_1_
  16.3 0.3 collective-permute-start.3
  16.5 1.3 %collective-permute-done.3.refs_4_ = f32[4,64,128]{2,1,0:T(8,128)S(1)} collective-permute-done((f32[4,64,128]{2,1,0:T(8,128)S(1)}, f32[4,64,128]{2,1,0:T(8,128)S(1)}, u32[]{:S(2)}, u32[]{:S(2)}) %collective-permute-start.3) | collective-permute-done | bytes 131104 | tf_op jit(solution)/shard_map/ppermute | solution.py:377
  17.9 7.1 %shard_map.103 = (f32[648,128]{1,0:T(8,128)S(1)}, f32[648,128]{1,0:T(8,128)S(1)}, f32[648,128]{1,0:T(8,128)S(1)}, f32[648,128]{1,0:T(8,128)S(1)}) custom-call(f32[64,128]{1,0:T(8,128)S(1)} %get-tuple-element.17.refs_0_, f32[64,128]{1,0:T(8,128)S(1)} %collective-permute-done.refs_1_, f32[64,128]{1,0:T(8,128)S(1)} %collective-permute-done.1.refs_2_, ...), custom_call_target="tpu_custom_call" | custom-call | flops 3221225472 | bytes 1048576 | tf_op jit(solution)/shard_map/pallas_call | solution.py:364
  25.0 1.7 %collective-permute-start.4 = (f32[648,128]{1,0:T(8,128)S(1)}, f32[648,128]{1,0:T(8,128)S(1)}, u32[]{:S(2)}, u32[]{:S(2)}) collective-permute-start(f32[648,128]{1,0:T(8,128)S(1)} %get-tuple-element.26), channel_id=1, source_target_pairs={{0,8},{8,16},{16,24},{24,0},{1,9},{9,17},{17,25},{25,1},{2,10},{10... | collective-permute-start | bytes 995336 | tf_op jit(solution)/shard_map/ppermute | solution.py:377
  26.6 2.9 %collective-permute-start.5 = (f32[648,128]{1,0:T(8,128)S(1)}, f32[648,128]{1,0:T(8,128)S(1)}, u32[]{:S(2)}, u32[]{:S(2)}) collective-permute-start(f32[648,128]{1,0:T(8,128)S(1)} %get-tuple-element.27), channel_id=1, source_target_pairs={{0,16},{8,24},{16,0},{24,8},{1,17},{9,25},{17,1},{25,9},{2,18},{10... | collective-permute-start | bytes 995336 | tf_op jit(solution)/shard_map/ppermute | solution.py:377
  29.5 1.3 %collective-permute-start.6 = (f32[648,128]{1,0:T(8,128)S(1)}, f32[648,128]{1,0:T(8,128)S(1)}, u32[]{:S(2)}, u32[]{:S(2)}) collective-permute-start(f32[648,128]{1,0:T(8,128)S(1)} %get-tuple-element.28), channel_id=1, source_target_pairs={{0,24},{8,0},{16,8},{24,16},{1,25},{9,1},{17,9},{25,17},{2,26},{10... | collective-permute-start | bytes 995336 | tf_op jit(solution)/shard_map/ppermute | solution.py:377
  30.9 5.3 %collective-permute-done.4.refs_1_ = f32[648,128]{1,0:T(8,128)S(1)} collective-permute-done((f32[648,128]{1,0:T(8,128)S(1)}, f32[648,128]{1,0:T(8,128)S(1)}, u32[]{:S(2)}, u32[]{:S(2)}) %collective-permute-start.4) | collective-permute-done | bytes 331808 | tf_op jit(solution)/shard_map/ppermute | solution.py:377
  36.2 8.3 %collective-permute-done.5.refs_2_ = f32[648,128]{1,0:T(8,128)S(1)} collective-permute-done((f32[648,128]{1,0:T(8,128)S(1)}, f32[648,128]{1,0:T(8,128)S(1)}, u32[]{:S(2)}, u32[]{:S(2)}) %collective-permute-start.5) | collective-permute-done | bytes 331808 | tf_op jit(solution)/shard_map/ppermute | solution.py:377
  44.4 0.0 collective-permute-done.6.refs_3_
  44.4 0.1 shard_map.104
  44.6 20.4 %all_to_all.10.parts = f32[8,88,128]{2,1,0:T(8,128)S(1)} all-to-all(f32[8,88,128]{2,1,0:T(8,128)S(1)} %shard_map.104), channel_id=1, replica_groups=mesh['x'=4,'core'=2,'y'=4,'z'=8] {'z'}, dimensions={0} | all-to-all | bytes 720896 | tf_op jit(solution)/shard_map/all_to_all | solution.py:415
  64.9 0.1 shard_map.105
  65.1 11.8 %all_to_all.11 = f32[8,40,128]{2,1,0:T(8,128)S(1)} all-to-all(f32[8,40,128]{2,1,0:T(8,128)S(1)} %shard_map.105), channel_id=1, replica_groups=mesh['x'=4,'core'=2,'y'=4,'z'=8] {'z'}, dimensions={0} | all-to-all | bytes 327680 | tf_op jit(solution)/shard_map/all_to_all | solution.py:417
  76.9 2.9 %collective-permute-start.9 = (f32[320,128]{1,0:T(8,128)S(1)}, f32[320,128]{1,0:T(8,128)S(1)}, u32[]{:S(2)}, u32[]{:S(2)}) collective-permute-start(f32[320,128]{1,0:T(8,128)S(1)} %bitcast.7), channel_id=1, source_target_pairs={{0,24},{8,0},{16,8},{24,16},{1,25},{9,1},{17,9},{25,17},{2,26},{10... | collective-permute-start | bytes 491528 | tf_op jit(solution)/shard_map/ppermute | solution.py:377
  79.8 0.4 collective-permute-start.8
  80.2 0.4 collective-permute-start.7
  80.6 3.9 %collective-permute-done.9.refs_3_ = f32[320,128]{1,0:T(8,128)S(1)} collective-permute-done((f32[320,128]{1,0:T(8,128)S(1)}, f32[320,128]{1,0:T(8,128)S(1)}, u32[]{:S(2)}, u32[]{:S(2)}) %collective-permute-start.9) | collective-permute-done | bytes 163872 | tf_op jit(solution)/shard_map/ppermute | solution.py:377
  84.5 2.1 %collective-permute-done.8.refs_2_ = f32[320,128]{1,0:T(8,128)S(1)} collective-permute-done((f32[320,128]{1,0:T(8,128)S(1)}, f32[320,128]{1,0:T(8,128)S(1)}, u32[]{:S(2)}, u32[]{:S(2)}) %collective-permute-start.8) | collective-permute-done | bytes 163872 | tf_op jit(solution)/shard_map/ppermute | solution.py:377
  86.7 1.7 %collective-permute-done.7.refs_1_ = f32[320,128]{1,0:T(8,128)S(1)} collective-permute-done((f32[320,128]{1,0:T(8,128)S(1)}, f32[320,128]{1,0:T(8,128)S(1)}, u32[]{:S(2)}, u32[]{:S(2)}) %collective-permute-start.7) | collective-permute-done | bytes 163872 | tf_op jit(solution)/shard_map/ppermute | solution.py:377
  88.3 1.6 %shard_map.106 = (f32[16,16]{1,0:T(8,128)}, f32[256,2,256]{2,1,0:T(2,128)}, f32[256,2,256]{2,1,0:T(2,128)}, f32[2,2,256]{2,1,0:T(2,128)}) custom-call(f32[320,128]{1,0:T(8,128)S(1)} %bitcast.10, f32[320,128]{1,0:T(8,128)S(1)} %collective-permute-done.7.refs_1_, f32[320,128]{1,0:T(8,128)S(1)} %collective-permute-done.8.refs_2_, ...), custom_call_target="tpu_custom_call" | custom-call | flops 1048576 | bytes 1048576 | tf_op jit(solution)/shard_map/pallas_call | solution.py:364
  (1 shorter events, 0.0 us)
Async XLA Ops:
  7.5 4.5 %collective-permute-start.2 = (f32[64,128]{1,0:T(8,128)S(1)}, f32[64,128]{1,0:T(8,128)S(1)}, u32[]{:S(2)}, u32[]{:S(2)}) collective-permute-start(f32[64,128]{1,0:T(8,128)S(1)} %get-tuple-element.17.refs_0_), channel_id=1, source_target_pairs={{0,192},{64,0},{128,64},{192,128},{1,193},{65,1},{129,65},{193,129... | collective-permute-start | bytes 98312 | tf_op jit(solution)/shard_map/ppermute | solution.py:377
  10.3 5.4 %collective-permute-start.1 = (f32[64,128]{1,0:T(8,128)S(1)}, f32[64,128]{1,0:T(8,128)S(1)}, u32[]{:S(2)}, u32[]{:S(2)}) collective-permute-start(f32[64,128]{1,0:T(8,128)S(1)} %get-tuple-element.17.refs_0_), channel_id=1, source_target_pairs={{0,128},{64,192},{128,0},{192,64},{1,129},{65,193},{129,1},{193,65... | collective-permute-start | bytes 98312 | tf_op jit(solution)/shard_map/ppermute | solution.py:377
  11.1 5.1 %collective-permute-start = (f32[64,128]{1,0:T(8,128)S(1)}, f32[64,128]{1,0:T(8,128)S(1)}, u32[]{:S(2)}, u32[]{:S(2)}) collective-permute-start(f32[64,128]{1,0:T(8,128)S(1)} %get-tuple-element.17.refs_0_), channel_id=1, source_target_pairs={{0,64},{64,128},{128,192},{192,0},{1,65},{65,129},{129,193},{193,1... | collective-permute-start | bytes 98312 | tf_op jit(solution)/shard_map/ppermute | solution.py:377
  16.3 1.6 %collective-permute-start.3 = (f32[4,64,128]{2,1,0:T(8,128)S(1)}, f32[4,64,128]{2,1,0:T(8,128)S(1)}, u32[]{:S(2)}, u32[]{:S(2)}) collective-permute-start(f32[4,64,128]{2,1,0:T(8,128)S(1)} %pad_maximum_fusion), channel_id=1, source_target_pairs={{0,32},{32,0},{1,33},{33,1},{2,34},{34,2},{3,35},{35,3},{4,36},{36... | collective-permute-start | bytes 393224 | tf_op jit(solution)/shard_map/ppermute | solution.py:377
  25.0 11.2 %collective-permute-start.4 = (f32[648,128]{1,0:T(8,128)S(1)}, f32[648,128]{1,0:T(8,128)S(1)}, u32[]{:S(2)}, u32[]{:S(2)}) collective-permute-start(f32[648,128]{1,0:T(8,128)S(1)} %get-tuple-element.26), channel_id=1, source_target_pairs={{0,8},{8,16},{16,24},{24,0},{1,9},{9,17},{17,25},{25,1},{2,10},{10... | collective-permute-start | bytes 995336 | tf_op jit(solution)/shard_map/ppermute | solution.py:377
  26.6 17.8 %collective-permute-start.5 = (f32[648,128]{1,0:T(8,128)S(1)}, f32[648,128]{1,0:T(8,128)S(1)}, u32[]{:S(2)}, u32[]{:S(2)}) collective-permute-start(f32[648,128]{1,0:T(8,128)S(1)} %get-tuple-element.27), channel_id=1, source_target_pairs={{0,16},{8,24},{16,0},{24,8},{1,17},{9,25},{17,1},{25,9},{2,18},{10... | collective-permute-start | bytes 995336 | tf_op jit(solution)/shard_map/ppermute | solution.py:377
  29.5 14.9 %collective-permute-start.6 = (f32[648,128]{1,0:T(8,128)S(1)}, f32[648,128]{1,0:T(8,128)S(1)}, u32[]{:S(2)}, u32[]{:S(2)}) collective-permute-start(f32[648,128]{1,0:T(8,128)S(1)} %get-tuple-element.28), channel_id=1, source_target_pairs={{0,24},{8,0},{16,8},{24,16},{1,25},{9,1},{17,9},{25,17},{2,26},{10... | collective-permute-start | bytes 995336 | tf_op jit(solution)/shard_map/ppermute | solution.py:377
  76.9 7.6 %collective-permute-start.9 = (f32[320,128]{1,0:T(8,128)S(1)}, f32[320,128]{1,0:T(8,128)S(1)}, u32[]{:S(2)}, u32[]{:S(2)}) collective-permute-start(f32[320,128]{1,0:T(8,128)S(1)} %bitcast.7), channel_id=1, source_target_pairs={{0,24},{8,0},{16,8},{24,16},{1,25},{9,1},{17,9},{25,17},{2,26},{10... | collective-permute-start | bytes 491528 | tf_op jit(solution)/shard_map/ppermute | solution.py:377
  79.8 6.9 %collective-permute-start.8 = (f32[320,128]{1,0:T(8,128)S(1)}, f32[320,128]{1,0:T(8,128)S(1)}, u32[]{:S(2)}, u32[]{:S(2)}) collective-permute-start(f32[320,128]{1,0:T(8,128)S(1)} %bitcast.8), channel_id=1, source_target_pairs={{0,16},{8,24},{16,0},{24,8},{1,17},{9,25},{17,1},{25,9},{2,18},{10... | collective-permute-start | bytes 491528 | tf_op jit(solution)/shard_map/ppermute | solution.py:377
  80.2 8.2 %collective-permute-start.7 = (f32[320,128]{1,0:T(8,128)S(1)}, f32[320,128]{1,0:T(8,128)S(1)}, u32[]{:S(2)}, u32[]{:S(2)}) collective-permute-start(f32[320,128]{1,0:T(8,128)S(1)} %bitcast.9), channel_id=1, source_target_pairs={{0,8},{8,16},{16,24},{24,0},{1,9},{9,17},{17,25},{25,1},{2,10},{10... | collective-permute-start | bytes 491528 | tf_op jit(solution)/shard_map/ppermute | solution.py:377

commit v3 on v2

--- a/solution.py
+++ b/solution.py
@@ -170,9 +170,7 @@
         value = w_heads_raw[:, s, :].astype(F32)
         value = jnp.concatenate([value, jnp.zeros((16 - value.shape[0], value.shape[1]), F32)], axis=0)
         heads.append(value.astype(BF16))
-        w_heads_t[s, 0] = value.T.astype(BF16)
-        value = jnp.concatenate([jnp.zeros((2, value.shape[1]), F32), value[0:1], jnp.zeros((13, value.shape[1]), F32)], axis=0)
-        w_heads_t[s, 1] = value.T.astype(BF16)
+        w_heads_t[s] = value.T.astype(BF16)
 
     for s in range(states):
         pre = lax.dot_general(w_eff[s], basis_three[...], NN, preferred_element_type=F32)
@@ -205,18 +203,14 @@
     return rows
 
 
-def backward_kernel(spread, *refs):
-    along_x, refs = refs[:XS], refs[XS:]
-    others, potential, weights_in, basis, first, second, w_two, w_heads_t = refs[:8]
-    outs, (gathered, inverse_t, value, slope, cot, first_bf, inner_one, inner_two) = refs[8 : 8 + YS], refs[8 + YS :]
-    send = along_x[0]
+def energy_kernel(spread, *refs):
+    near, (others, potential, weights_in, message, sums, d_amp, d_hps, gathered, inverse_t) = refs[:XS], refs[XS:]
     slots, walkers = potential.shape
-    states, hidden = w_two.shape[:2]
-    rows_number = slots * walkers
-    block = send.shape[0]
+    states = d_amp.shape[0]
+    block = near[0].shape[0]
     me_x, me_core = lax.axis_index("x"), lax.axis_index("core")
     for k in range(XS):
-        for at, source in ((me_core, along_x[k]), (1 - me_core, others.at[k])):
+        for at, source in ((me_core, near[k]), (1 - me_core, others.at[k])):
             owner = (me_x + XS - k) % XS * 2 + at
             gathered[pl.ds(pl.multiple_of(owner * block, block), block), :] = source[...]
 
@@ -235,126 +229,112 @@
             energies[k] = energies[k] + rows[j] * hps[k : k + 1, :]
     trace = jnp.zeros((1, walkers), F32)
     lane = lax.broadcasted_iota(jnp.int32, (8, walkers), 1)
-    sums = jnp.zeros((8, walkers), F32)
+    note = jnp.zeros((8, walkers), F32)
     for k in range(slots):
         trace = trace + energies[k][k : k + 1, :]
         total = jnp.sum(energies[k] * weights, axis=1, keepdims=True)
         for half in range(slots // 8):
-            sums = jnp.where(lane == half * slots + k, total[half * 8 : half * 8 + 8], sums)
+            note = jnp.where(lane == half * slots + k, total[half * 8 : half * 8 + 8], note)
     count = jnp.sum(weights, axis=1, keepdims=True)
     level = jnp.sum(trace * weights, axis=1, keepdims=True)
-    center = level / count
+    sums[...] = note
+    lane = lane[0:1]
     note = jnp.where(lane == 0, level, jnp.where(lane == 1, count, 0.0))
-
-    cot[...] = jnp.zeros(cot.shape, F32)
+    for d in range(message.shape[0]):
+        message[d] = note
     for s in range(states):
         own = inverse_t[(me_x * 2 + me_core) * states + s]
         along_own = jnp.zeros((slots, walkers), F32)
         for k in range(slots):
             along_own = along_own + own[k : k + 1, :] * energies[k]
-        hps = weights * own
-        amp = weights * (2.0 * (trace - center) * own - along_own)
+        d_amp[s] = weights * (2.0 * trace * own - along_own)
+        d_hps[s] = weights * own
+
+
+def backward_kernel(spread, *refs):
+    (messages, d_amp, d_hps, sums, send, potential, basis, first, second, w_two, w_heads_t), outs, (
+        out, cot, first_bf, inner_one, inner_two) = refs[:11], refs[11 : 11 + YS], refs[11 + YS :]
+    states, slots, walkers = d_amp.shape
+    hidden = w_two.shape[1]
+    total = jnp.sum(messages[...], axis=0)
+    share = 1.0 / total[:, 1:2]
+    mean = total[:, 0:1] * share
+    pot = potential[...]
+    cot[...] = jnp.zeros(cot.shape, F32)
+    for s in range(states):
         squashed = send[pl.ds(s * 2 * slots, slots), :]
-        bend = spread * (1.0 - squashed * squashed)
-        amp = (amp + hps * pot) * bend
-        steep = -2.0 * hps * bend
+        hps = d_hps[s] * share
+        amp = (d_amp[s] - 2.0 * mean * d_hps[s]) * share
+        amp = (amp + hps * pot) * (spread * (1.0 - squashed * squashed))
         for slot in range(slots):
             lanes = pl.ds(slot * walkers, walkers)
             cot[s, 0:1, lanes] = amp[slot : slot + 1, :]
             cot[s, 1:2, lanes] = hps[slot : slot + 1, :]
-            cot[s, 2:3, lanes] = steep[slot : slot + 1, :]
-
-    def put(target, start, s, array):
+
+    def put(start, s, array):
         for half in range(hidden // 128):
             at = pl.ds(4 * start + 2 * half + s, array.shape[0], stride=4)
-            target[at, :] = array[:, half * 128 : (half + 1) * 128]
-
-    heads = []
+            out[at, :] = array[:, half * 128 : (half + 1) * 128]
+
+    spare = 4 * (2 * COSINES - 1)
+    out[pl.ds(spare, 4 * BASIS - spare), :] = jnp.zeros((4 * BASIS - spare, 128), F32)
     for s in range(states):
         first_act = first[s]
         second_tanh = second[s]
         second_bf = (second_tanh + first_act).astype(BF16)
         first_bf[s] = first_act.astype(BF16)
-        bend_one = 1.0 - first_act * first_act
-        bend_two = 1.0 - second_tanh * second_tanh
         cot_bf = cot[s].astype(BF16)
-        heads.append(lax.dot_general(cot_bf, second_bf, NT, preferred_element_type=F32))
-        for t in range(2):
-            back_two = lax.dot_general(w_heads_t[s, t], cot_bf, NN, preferred_element_type=F32)
-            inner = (back_two * bend_two).astype(BF16)
-            inner_two[s, t] = inner
-            back_one = back_two + lax.dot_general(w_two[s], inner, NN, preferred_element_type=F32)
-            inner_one[s, t] = (back_one * bend_one).astype(BF16)
-    for t, target in enumerate((value, slope)):
-        spare = 4 * (2 * COSINES - 1)
-        target[pl.ds(spare, 4 * BASIS - spare), :] = jnp.zeros((4 * BASIS - spare, 128), F32)
-        for s in range(states):
-            grad_two = lax.dot_general(first_bf[s], inner_two[s, t], NT, preferred_element_type=F32)
-            put(target, BASIS, s, grad_two)
-            grad_one = lax.dot_general(basis[...], inner_one[s, t], NT, preferred_element_type=F32)
-            put(target, 0, s, grad_one[0 : 2 * COSINES - 1])
-            put(target, 2 * COSINES - 1, s, heads[s][2 * t : 2 * t + 2])
-    value[pl.ds(4 * (2 * COSINES + 1), 8), :] = sums
-    part = value.shape[0] // YS
+        heads = lax.dot_general(cot_bf, second_bf, NT, preferred_element_type=F32)
+        put(2 * COSINES - 1, s, heads[0:2])
+        back_two = lax.dot_general(w_heads_t[s], cot_bf, NN, preferred_element_type=F32)
+        inner = (back_two * (1.0 - second_tanh * second_tanh)).astype(BF16)
+        inner_two[s] = inner
+        back_one = back_two + lax.dot_general(w_two[s], inner, NN, preferred_element_type=F32)
+        inner_one[s] = (back_one * (1.0 - first_act * first_act)).astype(BF16)
+    for s in range(states):
+        put(BASIS, s, lax.dot_general(first_bf[s], inner_two[s], NT, preferred_element_type=F32))
+        grad_one = lax.dot_general(basis[...], inner_one[s], NT, preferred_element_type=F32)
+        put(0, s, grad_one[0 : 2 * COSINES - 1])
+    out[pl.ds(4 * (2 * COSINES + 1), 8), :] = sums[...] * share
+    part = out.shape[0] // YS
     y = lax.axis_index("y")
     for k in range(YS):
-        at = pl.ds(pl.multiple_of((y + k) % YS * part, part), part)
-        outs[k][pl.ds(0, part), :] = value[at, :] - center * slope[at, :]
-        outs[k][pl.ds(part, part), :] = slope[at, :]
-        outs[k][pl.ds(2 * part, 8), :] = note
+        outs[k][...] = out[pl.ds(pl.multiple_of((y + k) % YS * part, part), part), :]
 
 
 def line_kernel(*refs):
     parts, out = refs[:YS], refs[YS]
-    part = (parts[0].shape[0] - 8) // 2
-    size = part // ZS
-
-    def added(start, length):
-        total = parts[0][pl.ds(start, length), :]
-        for k in range(1, YS):
-            total = total + parts[k][pl.ds(start, length), :]
-        return total
-
-    for z in range(ZS):
-        out[z, 0:size] = added(z * size, size)
-        out[z, size : 2 * size] = added(part + z * size, size)
-        out[z, 2 * size : 2 * size + 8] = added(2 * part, 8)
+    total = parts[0][...]
+    for k in range(1, YS):
+        total = total + parts[k][...]
+    out[...] = total
 
 
 def piece_kernel(parts, out):
-    size = out.shape[1]
-    total = parts[0]
+    piece = parts[0]
     for z in range(1, ZS):
-        total = total + parts[z]
-    note = total[2 * size : 2 * size + 1]
-    share = 1.0 / note[:, 1:2]
-    mean = note[:, 0:1] * share
-    piece = (total[0:size] + mean * total[size : 2 * size]) * share
+        piece = piece + parts[z]
     for z in range(ZS):
         out[z] = piece
 
 
 def expand_kernel(*refs):
-    parts, (select_in, energy, grad_first, grad_second, grad_heads, summed) = refs[:YS], refs[YS:]
+    parts, (select, energy, grad_first, grad_second, grad_heads, summed) = refs[:YS], refs[YS:]
     y = lax.axis_index("y")
     part = parts[0].shape[0]
     for k in range(YS):
         summed[pl.ds(pl.multiple_of((y + YS - k) % YS * part, part), part), :] = parts[k][...]
-    select = select_in[...]
     slots = energy.shape[0]
     note = summed[pl.ds(4 * (2 * COSINES + 1), 8), :]
     for half in range(slots // 8):
         energy[pl.ds(half * 8, 8), :] = note[:, half * slots : (half + 1) * slots]
-    states = grad_first.shape[1]
-    rows = grad_second.shape[0]
-    for half in range(2):
-        lanes = pl.ds(half * 128, 128)
-        for s in range(states):
-            value = summed[pl.ds(2 * half + s, BASIS, stride=4), :]
-            parts = jnp.concatenate(three_parts(value), axis=0)
-            grad_first[:, s, lanes] = lax.dot_general(select, parts, NN, preferred_element_type=F32)
-            grad_second[:, s, lanes] = summed[pl.ds(4 * BASIS + 2 * half + s, rows, stride=4), :]
-            grad_heads[:, s, lanes] = value[2 * COSINES - 1 : 2 * COSINES + 1]
+    for at in range(4):
+        value = summed[pl.ds(at, BASIS, stride=4), :]
+        parts = jnp.concatenate(three_parts(value), axis=0)
+        rows = lax.dot_general(select[...], parts, NN, preferred_element_type=F32)
+        grad_first[pl.ds(at, rows.shape[0], stride=4), :] = rows
+    grad_second[...] = summed[pl.ds(4 * BASIS, grad_second.shape[0]), :]
+    grad_heads[...] = summed[pl.ds(4 * (2 * COSINES - 1), grad_heads.shape[0]), :]
 
 
 def call(body, outs, scratch, limit, args, flops, hbm=False):
@@ -381,7 +361,7 @@
     electrons, slots, walkers = positions.shape[1:]
     features, states, hidden = w_first.shape
     rows = slots * walkers
-    groups = lax.axis_size(("x", "core"))
+    groups, shares = lax.axis_size(("x", "core")), lax.axis_size(("y", "z"))
     spread = 0.75 / slots
     total = 4 * (BASIS + hidden)
     work = 2 * states * rows * hidden * hidden
@@ -390,36 +370,47 @@
         forward_kernel,
         [((4 * slots, walkers), F32), ((slots, walkers), F32), ((BASIS, rows), BF16),
          ((states, hidden, rows), F32), ((states, hidden, rows), F32), ((1, walkers), F32),
-         ((features, 3 * BASIS), BF16), ((states, hidden, hidden), BF16), ((states, 2, hidden, 16), BF16)],
+         ((features, 3 * BASIS), BF16), ((states, hidden, hidden), BF16), ((states, hidden, 16), BF16)],
         [(a.shape, a.dtype) for a in args] + [pltpu.SemaphoreType.DMA((len(args),))]
         + [((4, electrons, slots, walkers), F32), ((slots * BASIS, walkers), F32),
            ((states, hidden, 3 * BASIS), BF16), ((states, hidden, hidden), BF16), ((3 * BASIS, rows), BF16)],
         40, args, 2 * work, hbm=True)
-    along_x = [send] + [along("x", send, k) for k in range(1, XS)]
-    others = along("core", jnp.stack(along_x), 1)
+    near = [send] + [along("x", send, k) for k in range(1, XS)]
+    others = along("core", jnp.stack(near), 1)
+
+    def energy_body(*refs):
+        energy_kernel(spread, *refs)
 
     def backward_body(*refs):
         backward_kernel(spread, *refs)
 
+    message, sums, d_amp, d_hps = call(
+        energy_body,
+        [((shares, 1, walkers), F32), ((8, walkers), F32), ((states, slots, walkers), F32),
+         ((states, slots, walkers), F32)],
+        [((groups * 4 * slots, walkers), F32), ((slots, slots, walkers), F32)],
+        4, (*near, others, potential, weights), 1 << 20)
+    messages = lax.all_to_all(message, ("y", "z"), 0, 0, tiled=True)
     part = total // YS
     size = part // ZS
     parts = call(
         backward_body,
-        [((2 * part + 8, 128), F32)] * YS,
-        [((groups * 4 * slots, walkers), F32), ((slots, slots, walkers), F32), ((total, 128), F32),
-         ((total, 128), F32), ((states, 16, rows), F32), ((states, hidden, rows), BF16),
-         ((states, 2, hidden, rows), BF16), ((states, 2, hidden, rows), BF16)],
-        24, (*along_x, others, potential, weights, basis, first, second, w_two, w_heads_t), 6 * work)
+        [((part, 128), F32)] * YS,
+        [((total, 128), F32), ((states, 16, rows), F32), ((states, hidden, rows), BF16),
+         ((states, hidden, rows), BF16), ((states, hidden, rows), BF16)],
+        20, (messages, d_amp, d_hps, sums, send, potential, basis, first, second, w_two, w_heads_t), 3 * work)
     parts = [parts[0]] + [along("y", parts[k], k) for k in range(1, YS)]
-    lines, = call(line_kernel, [((ZS, 2 * size + 8, 128), F32)], [], 4, parts, 1 << 20)
-    lines = lax.all_to_all(lines, "z", 0, 0, tiled=True)
+    line, = call(line_kernel, [((part, 128), F32)], [], 4, parts, 1 << 20)
+    lines = lax.all_to_all(line.reshape(ZS, size, 128), "z", 0, 0, tiled=True)
     pieces, = call(piece_kernel, [((ZS, size, 128), F32)], [], 4, (lines,), 1 << 20)
     summed = lax.all_to_all(pieces, "z", 0, 0, tiled=True).reshape(part, 128)
     parts = [summed] + [along("y", summed, k) for k in range(1, YS)]
-    return call(
+    energy_matrix, *grads = call(
         expand_kernel,
-        [((slots, slots), F32), (w_first.shape, F32), (w_second.shape, F32), (w_heads.shape, F32)],
+        [((slots, slots), F32)] + [((4 * w.shape[0], 128), F32) for w in (w_first, w_second, w_heads)],
         [((total, 128), F32)], 8, (*parts, select), 1 << 20)
+    grads = [g.reshape(-1, hidden // 128, states, 128).transpose(0, 2, 1, 3).reshape(-1, states, hidden) for g in grads]
+    return (energy_matrix, *grads)
 
 
 def solution(mesh):

time: 90.1 us -> 88.3 us (0.980)
  blocking collectives: 32.2 us -> 43.4 us
  waiting for transfers between devices: 26.9 us -> 19.3 us
  Pallas kernels: 15.8 us -> 12.6 us
  starting transfers between devices: 14.4 us -> 12.1 us
    all_to_all x1 -> x2, blocking collectives: 20.4 us -> 31.6 us  [the longest x1 19.8 us: shards(): messages = lax.all_to_all(message, ('y', 'z'), 0, 0, tiled=True)]
    ppermute x10, waiting for transfers between devices: 26.9 us -> 19.3 us  [along(): lax.ppermute(array, axis, [(d, (d + shift) % size) for d in range(size)])]
    pallas_call x5 -> x6, Pallas kernels: 15.8 us -> 12.6 us  [call(): pl.pallas_call(body, out_shape=[jax.ShapeDtypeStruct(s, t) for s, t in ou...]
    ppermute x10, starting transfers between devices: 14.4 us -> 12.1 us  [along(): lax.ppermute(array, axis, [(d, (d + shift) % size) for d in range(size)])]
where the time goes in v3:
time: 88.3 us; the launch traced here: 88 us
  blocking collectives  43.4 us (49%)
  waiting for transfers between devices  19.3 us (22%)
  Pallas kernels  12.6 us (14%)
  starting transfers between devices  12.1 us (14%)
    all_to_all x1, blocking collectives, shards(): messages = lax.all_to_all(message, ('y', 'z'), 0, 0, tiled=True)  19.8 us
    ppermute x10, waiting for transfers between devices, along(): lax.ppermute(array, axis, [(d, (d + shift) % size) for d in range(size)])  19.3 us
    pallas_call x6, Pallas kernels, call(): pl.pallas_call(body, out_shape=[jax.ShapeDtypeStruct(s, t) for s, t in ou...  12.6 us
    ppermute x10, starting transfers between devices, along(): lax.ppermute(array, axis, [(d, (d + shift) % size) for d in range(size)])  12.1 us
    all_to_all x1, blocking collectives, shards(): summed = lax.all_to_all(pieces, 'z', 0, 0, tiled=True).reshape(part, 128)  11.8 us
    all_to_all x1, blocking collectives, shards(): lines = lax.all_to_all(line.reshape(ZS, size, 128), 'z', 0, 0, tiled=True)  11.8 us
  transfers between devices with their start and end apart: 10, of which 8 were waited for; matrix products, arithmetic and copies ran while one was open for 0% of the time, Pallas kernels for 0%

profile of v3, /device:TPU:32, one launch (start us, length us, event | category | flops | bytes accessed | tf_op | source)
XLA Modules:
  0.0 88.0 jit_solution(12625245398722359316)
XLA Ops:
  0.6 6.8 %shard_map.102 = (f32[64,128]{1,0:T(8,128)S(1)}, f32[16,128]{1,0:T(8,128)S(1)}, bf16[64,2048]{1,0:T(8,128)(2,1)S(1)}, f32[2,256,2048]{2,1,0:T(8,128)S(1)}, f32[2...) custom-call(f32[2,30,16,128]{3,2,1,0:T(8,128)} %pos_in.1, ...), custom_call_target="tpu_custom_call" | custom-call | flops 1073741824 | bytes 1048576 | tf_op jit(solution)/shard_map/pallas_call | solution.py:344
  7.5 2.8 %collective-permute-start.2 = (f32[64,128]{1,0:T(8,128)S(1)}, f32[64,128]{1,0:T(8,128)S(1)}, u32[]{:S(2)}, u32[]{:S(2)}) collective-permute-start(f32[64,128]{1,0:T(8,128)S(1)} %get-tuple-element.25.refs_0_.refs_4_), channel_id=1, source_target_pairs={{0,192},{64,0},{128,64},{192,128},{1,193},{65,1},{129,65},{193,129... | collective-permute-start | bytes 98312 | tf_op jit(solution)/shard_map/ppermute | solution.py:357
  10.3 0.8 collective-permute-start.1
  11.1 0.9 %collective-permute-start = (f32[64,128]{1,0:T(8,128)S(1)}, f32[64,128]{1,0:T(8,128)S(1)}, u32[]{:S(2)}, u32[]{:S(2)}) collective-permute-start(f32[64,128]{1,0:T(8,128)S(1)} %get-tuple-element.25.refs_0_.refs_4_), channel_id=1, source_target_pairs={{0,64},{64,128},{128,192},{192,0},{1,65},{65,129},{129,193},{193,1... | collective-permute-start | bytes 98312 | tf_op jit(solution)/shard_map/ppermute | solution.py:357
  12.0 0.0 collective-permute-done.2.refs_3_
  12.0 3.7 %collective-permute-done.1.refs_2_ = f32[64,128]{1,0:T(8,128)S(1)} collective-permute-done((f32[64,128]{1,0:T(8,128)S(1)}, f32[64,128]{1,0:T(8,128)S(1)}, u32[]{:S(2)}, u32[]{:S(2)}) %collective-permute-start.1) | collective-permute-done | bytes 32800 | tf_op jit(solution)/shard_map/ppermute | solution.py:357
  15.7 0.5 collective-permute-done.refs_1_
  16.2 0.1 collective-permute-start.3
  16.3 1.3 %collective-permute-done.3.refs_4_ = f32[4,64,128]{2,1,0:T(8,128)S(1)} collective-permute-done((f32[4,64,128]{2,1,0:T(8,128)S(1)}, f32[4,64,128]{2,1,0:T(8,128)S(1)}, u32[]{:S(2)}, u32[]{:S(2)}) %collective-permute-start.3) | collective-permute-done | bytes 131104 | tf_op jit(solution)/shard_map/ppermute | solution.py:357
  17.7 0.7 shard_map.103
  18.3 19.8 %all_to_all.15.refs_0_ = f32[32,1,128]{2,1,0:T(1,128)S(1)} all-to-all(f32[32,1,128]{2,1,0:T(1,128)S(1)} %get-tuple-element.28), channel_id=1, replica_groups=mesh['x'=4,'core'=2,'y'=4,'z'=8] {'y','z'}, dimensions={0} | all-to-all | bytes 32768 | tf_op jit(solution)/shard_map/all_to_all | solution.py:393
  38.1 3.8 %shard_map.104 = (f32[320,128]{1,0:T(8,128)S(1)}, f32[320,128]{1,0:T(8,128)S(1)}, f32[320,128]{1,0:T(8,128)S(1)}, f32[320,128]{1,0:T(8,128)S(1)}) custom-call(f32[32,1,128]{2,1,0:T(1,128)S(1)} %all_to_all.15.refs_0_, f32[2,16,128]{2,1,0:T(8,128)S(1)} %get-tuple-element.29.refs_1_, f32[2,16,128]{2,1,0:T(8,128)S(1)} %get-tuple-element.30.refs_2_, ...), custom_call_target="tpu_custom_call" | custom-call | flops 1610612736 | bytes 1048576 | tf_op jit(solution)/shard_map/pallas_call | solution.py:344
  41.9 0.7 collective-permute-start.4
  42.6 2.0 %collective-permute-start.5 = (f32[320,128]{1,0:T(8,128)S(1)}, f32[320,128]{1,0:T(8,128)S(1)}, u32[]{:S(2)}, u32[]{:S(2)}) collective-permute-start(f32[320,128]{1,0:T(8,128)S(1)} %get-tuple-element.39), channel_id=1, source_target_pairs={{0,16},{8,24},{16,0},{24,8},{1,17},{9,25},{17,1},{25,9},{2,18},{10... | collective-permute-start | bytes 491528 | tf_op jit(solution)/shard_map/ppermute | solution.py:357
  44.6 1.2 %collective-permute-start.6 = (f32[320,128]{1,0:T(8,128)S(1)}, f32[320,128]{1,0:T(8,128)S(1)}, u32[]{:S(2)}, u32[]{:S(2)}) collective-permute-start(f32[320,128]{1,0:T(8,128)S(1)} %get-tuple-element.40), channel_id=1, source_target_pairs={{0,24},{8,0},{16,8},{24,16},{1,25},{9,1},{17,9},{25,17},{2,26},{10... | collective-permute-start | bytes 491528 | tf_op jit(solution)/shard_map/ppermute | solution.py:357
  45.9 5.6 %collective-permute-done.4.refs_1_ = f32[320,128]{1,0:T(8,128)S(1)} collective-permute-done((f32[320,128]{1,0:T(8,128)S(1)}, f32[320,128]{1,0:T(8,128)S(1)}, u32[]{:S(2)}, u32[]{:S(2)}) %collective-permute-start.4) | collective-permute-done | bytes 163872 | tf_op jit(solution)/shard_map/ppermute | solution.py:357
  51.5 0.0 collective-permute-done.5.refs_2_
  51.5 0.6 collective-permute-done.6.refs_3_
  52.1 0.1 shard_map.105
  52.1 11.8 %all_to_all.16.parts = f32[8,40,128]{2,1,0:T(8,128)S(1)} all-to-all(f32[8,40,128]{2,1,0:T(8,128)S(1)} %bitcast.27), channel_id=1, replica_groups=mesh['x'=4,'core'=2,'y'=4,'z'=8] {'z'}, dimensions={0} | all-to-all | bytes 327680 | tf_op jit(solution)/shard_map/all_to_all | solution.py:404
  63.9 11.8 %all_to_all.17 = f32[8,40,128]{2,1,0:T(8,128)S(1)} all-to-all(f32[8,40,128]{2,1,0:T(8,128)S(1)} %shard_map.106), channel_id=1, replica_groups=mesh['x'=4,'core'=2,'y'=4,'z'=8] {'z'}, dimensions={0} | all-to-all | bytes 327680 | tf_op jit(solution)/shard_map/all_to_all | solution.py:406
  75.8 2.7 %collective-permute-start.9 = (f32[320,128]{1,0:T(8,128)S(1)}, f32[320,128]{1,0:T(8,128)S(1)}, u32[]{:S(2)}, u32[]{:S(2)}) collective-permute-start(f32[320,128]{1,0:T(8,128)S(1)} %bitcast.23), channel_id=1, source_target_pairs={{0,24},{8,0},{16,8},{24,16},{1,25},{9,1},{17,9},{25,17},{2,26},{10... | collective-permute-start | bytes 491528 | tf_op jit(solution)/shard_map/ppermute | solution.py:357
  78.4 0.0 collective-permute-start.8
  78.4 0.8 collective-permute-start.7
  79.3 3.8 %collective-permute-done.9.refs_3_ = f32[320,128]{1,0:T(8,128)S(1)} collective-permute-done((f32[320,128]{1,0:T(8,128)S(1)}, f32[320,128]{1,0:T(8,128)S(1)}, u32[]{:S(2)}, u32[]{:S(2)}) %collective-permute-start.9) | collective-permute-done | bytes 163872 | tf_op jit(solution)/shard_map/ppermute | solution.py:357
  83.0 2.3 %collective-permute-done.8.refs_2_ = f32[320,128]{1,0:T(8,128)S(1)} collective-permute-done((f32[320,128]{1,0:T(8,128)S(1)}, f32[320,128]{1,0:T(8,128)S(1)}, u32[]{:S(2)}, u32[]{:S(2)}) %collective-permute-start.8) | collective-permute-done | bytes 163872 | tf_op jit(solution)/shard_map/ppermute | solution.py:357
  85.3 1.4 %collective-permute-done.7.refs_1_ = f32[320,128]{1,0:T(8,128)S(1)} collective-permute-done((f32[320,128]{1,0:T(8,128)S(1)}, f32[320,128]{1,0:T(8,128)S(1)}, u32[]{:S(2)}, u32[]{:S(2)}) %collective-permute-start.7) | collective-permute-done | bytes 163872 | tf_op jit(solution)/shard_map/ppermute | solution.py:357
  86.7 1.3 %shard_map.107 = (f32[16,16]{1,0:T(8,128)}, f32[1024,128]{1,0:T(8,128)}, f32[1024,128]{1,0:T(8,128)}, f32[8,128]{1,0:T(8,128)}) custom-call(f32[320,128]{1,0:T(8,128)S(1)} %bitcast.26, f32[320,128]{1,0:T(8,128)S(1)} %collective-permute-done.7.refs_1_, f32[320,128]{1,0:T(8,128)S(1)} %collective-permute-done.8.refs_2_, ...), custom_call_target="tpu_custom_call" | custom-call | flops 1048576 | bytes 1048576 | tf_op jit(solution)/shard_map/pallas_call | solution.py:344
  (2 shorter events, 0.0 us)
Async XLA Ops:
  7.5 4.5 %collective-permute-start.2 = (f32[64,128]{1,0:T(8,128)S(1)}, f32[64,128]{1,0:T(8,128)S(1)}, u32[]{:S(2)}, u32[]{:S(2)}) collective-permute-start(f32[64,128]{1,0:T(8,128)S(1)} %get-tuple-element.25.refs_0_.refs_4_), channel_id=1, source_target_pairs={{0,192},{64,0},{128,64},{192,128},{1,193},{65,1},{129,65},{193,129... | collective-permute-start | bytes 98312 | tf_op jit(solution)/shard_map/ppermute | solution.py:357
  10.3 5.4 %collective-permute-start.1 = (f32[64,128]{1,0:T(8,128)S(1)}, f32[64,128]{1,0:T(8,128)S(1)}, u32[]{:S(2)}, u32[]{:S(2)}) collective-permute-start(f32[64,128]{1,0:T(8,128)S(1)} %get-tuple-element.25.refs_0_.refs_4_), channel_id=1, source_target_pairs={{0,128},{64,192},{128,0},{192,64},{1,129},{65,193},{129,1},{193,65... | collective-permute-start | bytes 98312 | tf_op jit(solution)/shard_map/ppermute | solution.py:357
  11.1 5.1 %collective-permute-start = (f32[64,128]{1,0:T(8,128)S(1)}, f32[64,128]{1,0:T(8,128)S(1)}, u32[]{:S(2)}, u32[]{:S(2)}) collective-permute-start(f32[64,128]{1,0:T(8,128)S(1)} %get-tuple-element.25.refs_0_.refs_4_), channel_id=1, source_target_pairs={{0,64},{64,128},{128,192},{192,0},{1,65},{65,129},{129,193},{193,1... | collective-permute-start | bytes 98312 | tf_op jit(solution)/shard_map/ppermute | solution.py:357
  16.2 1.4 %collective-permute-start.3 = (f32[4,64,128]{2,1,0:T(8,128)S(1)}, f32[4,64,128]{2,1,0:T(8,128)S(1)}, u32[]{:S(2)}, u32[]{:S(2)}) collective-permute-start(f32[4,64,128]{2,1,0:T(8,128)S(1)} %pad_maximum_fusion), channel_id=1, source_target_pairs={{0,32},{32,0},{1,33},{33,1},{2,34},{34,2},{3,35},{35,3},{4,36},{36... | collective-permute-start | bytes 393224 | tf_op jit(solution)/shard_map/ppermute | solution.py:357
  41.9 9.6 %collective-permute-start.4 = (f32[320,128]{1,0:T(8,128)S(1)}, f32[320,128]{1,0:T(8,128)S(1)}, u32[]{:S(2)}, u32[]{:S(2)}) collective-permute-start(f32[320,128]{1,0:T(8,128)S(1)} %get-tuple-element.38), channel_id=1, source_target_pairs={{0,8},{8,16},{16,24},{24,0},{1,9},{9,17},{17,25},{25,1},{2,10},{10... | collective-permute-start | bytes 491528 | tf_op jit(solution)/shard_map/ppermute | solution.py:357
  42.6 8.9 %collective-permute-start.5 = (f32[320,128]{1,0:T(8,128)S(1)}, f32[320,128]{1,0:T(8,128)S(1)}, u32[]{:S(2)}, u32[]{:S(2)}) collective-permute-start(f32[320,128]{1,0:T(8,128)S(1)} %get-tuple-element.39), channel_id=1, source_target_pairs={{0,16},{8,24},{16,0},{24,8},{1,17},{9,25},{17,1},{25,9},{2,18},{10... | collective-permute-start | bytes 491528 | tf_op jit(solution)/shard_map/ppermute | solution.py:357
  44.6 7.5 %collective-permute-start.6 = (f32[320,128]{1,0:T(8,128)S(1)}, f32[320,128]{1,0:T(8,128)S(1)}, u32[]{:S(2)}, u32[]{:S(2)}) collective-permute-start(f32[320,128]{1,0:T(8,128)S(1)} %get-tuple-element.40), channel_id=1, source_target_pairs={{0,24},{8,0},{16,8},{24,16},{1,25},{9,1},{17,9},{25,17},{2,26},{10... | collective-permute-start | bytes 491528 | tf_op jit(solution)/shard_map/ppermute | solution.py:357
  75.8 7.3 %collective-permute-start.9 = (f32[320,128]{1,0:T(8,128)S(1)}, f32[320,128]{1,0:T(8,128)S(1)}, u32[]{:S(2)}, u32[]{:S(2)}) collective-permute-start(f32[320,128]{1,0:T(8,128)S(1)} %bitcast.23), channel_id=1, source_target_pairs={{0,24},{8,0},{16,8},{24,16},{1,25},{9,1},{17,9},{25,17},{2,26},{10... | collective-permute-start | bytes 491528 | tf_op jit(solution)/shard_map/ppermute | solution.py:357
  78.4 6.9 %collective-permute-start.8 = (f32[320,128]{1,0:T(8,128)S(1)}, f32[320,128]{1,0:T(8,128)S(1)}, u32[]{:S(2)}, u32[]{:S(2)}) collective-permute-start(f32[320,128]{1,0:T(8,128)S(1)} %bitcast.24), channel_id=1, source_target_pairs={{0,16},{8,24},{16,0},{24,8},{1,17},{9,25},{17,1},{25,9},{2,18},{10... | collective-permute-start | bytes 491528 | tf_op jit(solution)/shard_map/ppermute | solution.py:357
  78.4 8.3 %collective-permute-start.7 = (f32[320,128]{1,0:T(8,128)S(1)}, f32[320,128]{1,0:T(8,128)S(1)}, u32[]{:S(2)}, u32[]{:S(2)}) collective-permute-start(f32[320,128]{1,0:T(8,128)S(1)} %bitcast.25), channel_id=1, source_target_pairs={{0,8},{8,16},{16,24},{24,0},{1,9},{9,17},{17,25},{25,1},{2,10},{10... | collective-permute-start | bytes 491528 | tf_op jit(solution)/shard_map/ppermute | solution.py:357

commit v4 on v3

--- a/solution.py
+++ b/solution.py
@@ -120,7 +120,7 @@
                 return tuple(t + p for t, p in zip(totals, parts, strict=True))
 
             number = 12 * len(firsts) + (12 if alone else 0)
-            totals = lax.fori_loop(0, electrons, add, (zero,) * number, unroll=2)
+            totals = lax.fori_loop(0, electrons, add, (zero,) * number, unroll=6)
             for i, m in enumerate(firsts):
                 for n in (1, 2, 3):
                     cc, ss, sc, cs = totals[12 * i + 4 * (n - 1) : 12 * i + 4 * n]
@@ -291,10 +291,9 @@
         inner_two[s] = inner
         back_one = back_two + lax.dot_general(w_two[s], inner, NN, preferred_element_type=F32)
         inner_one[s] = (back_one * (1.0 - first_act * first_act)).astype(BF16)
-    for s in range(states):
-        put(BASIS, s, lax.dot_general(first_bf[s], inner_two[s], NT, preferred_element_type=F32))
         grad_one = lax.dot_general(basis[...], inner_one[s], NT, preferred_element_type=F32)
         put(0, s, grad_one[0 : 2 * COSINES - 1])
+        put(BASIS, s, lax.dot_general(first_bf[s], inner_two[s], NT, preferred_element_type=F32))
     out[pl.ds(4 * (2 * COSINES + 1), 8), :] = sums[...] * share
     part = out.shape[0] // YS
     y = lax.axis_index("y")

time: 88.3 us -> 87.7 us (level)
  no operation moved by 1% of the time
where the time goes in v4:
time: 87.7 us; the launch traced here: 87.5 us
  blocking collectives  43.4 us (49%)
  waiting for transfers between devices  19.3 us (22%)
  Pallas kernels  12.1 us (14%)
  starting transfers between devices  12.1 us (14%)
    all_to_all x1, blocking collectives, shards(): messages = lax.all_to_all(message, ('y', 'z'), 0, 0, tiled=True)  19.8 us
    ppermute x10, waiting for transfers between devices, along(): lax.ppermute(array, axis, [(d, (d + shift) % size) for d in range(size)])  19.3 us
    ppermute x10, starting transfers between devices, along(): lax.ppermute(array, axis, [(d, (d + shift) % size) for d in range(size)])  12.1 us
    pallas_call x6, Pallas kernels, call(): pl.pallas_call(body, out_shape=[jax.ShapeDtypeStruct(s, t) for s, t in ou...  12.1 us
    all_to_all x1, blocking collectives, shards(): summed = lax.all_to_all(pieces, 'z', 0, 0, tiled=True).reshape(part, 128)  11.8 us
    all_to_all x1, blocking collectives, shards(): lines = lax.all_to_all(line.reshape(ZS, size, 128), 'z', 0, 0, tiled=True)  11.8 us
  transfers between devices with their start and end apart: 10, of which 8 were waited for; matrix products, arithmetic and copies ran while one was open for 0% of the time, Pallas kernels for 0%

profile of v4, /device:TPU:32, one launch (start us, length us, event | category | flops | bytes accessed | tf_op | source)
XLA Modules:
  0.0 87.5 jit_solution(15984351386614849796)
XLA Ops:
  0.6 6.5 %shard_map.102 = (f32[64,128]{1,0:T(8,128)S(1)}, f32[16,128]{1,0:T(8,128)S(1)}, bf16[64,2048]{1,0:T(8,128)(2,1)S(1)}, f32[2,256,2048]{2,1,0:T(8,128)S(1)}, f32[2...) custom-call(f32[2,30,16,128]{3,2,1,0:T(8,128)} %pos_in.1, ...), custom_call_target="tpu_custom_call" | custom-call | flops 1073741824 | bytes 1048576 | tf_op jit(solution)/shard_map/pallas_call | solution.py:343
  7.1 2.8 %collective-permute-start.2 = (f32[64,128]{1,0:T(8,128)S(1)}, f32[64,128]{1,0:T(8,128)S(1)}, u32[]{:S(2)}, u32[]{:S(2)}) collective-permute-start(f32[64,128]{1,0:T(8,128)S(1)} %get-tuple-element.25.refs_0_.refs_4_), channel_id=1, source_target_pairs={{0,192},{64,0},{128,64},{192,128},{1,193},{65,1},{129,65},{193,129... | collective-permute-start | bytes 98312 | tf_op jit(solution)/shard_map/ppermute | solution.py:356
  10.0 0.8 collective-permute-start.1
  10.8 0.9 %collective-permute-start = (f32[64,128]{1,0:T(8,128)S(1)}, f32[64,128]{1,0:T(8,128)S(1)}, u32[]{:S(2)}, u32[]{:S(2)}) collective-permute-start(f32[64,128]{1,0:T(8,128)S(1)} %get-tuple-element.25.refs_0_.refs_4_), channel_id=1, source_target_pairs={{0,64},{64,128},{128,192},{192,0},{1,65},{65,129},{129,193},{193,1... | collective-permute-start | bytes 98312 | tf_op jit(solution)/shard_map/ppermute | solution.py:356
  11.6 0.0 collective-permute-done.2.refs_3_
  11.6 3.7 %collective-permute-done.1.refs_2_ = f32[64,128]{1,0:T(8,128)S(1)} collective-permute-done((f32[64,128]{1,0:T(8,128)S(1)}, f32[64,128]{1,0:T(8,128)S(1)}, u32[]{:S(2)}, u32[]{:S(2)}) %collective-permute-start.1) | collective-permute-done | bytes 32800 | tf_op jit(solution)/shard_map/ppermute | solution.py:356
  15.4 0.5 collective-permute-done.refs_1_
  15.9 0.1 collective-permute-start.3
  16.0 1.3 %collective-permute-done.3.refs_4_ = f32[4,64,128]{2,1,0:T(8,128)S(1)} collective-permute-done((f32[4,64,128]{2,1,0:T(8,128)S(1)}, f32[4,64,128]{2,1,0:T(8,128)S(1)}, u32[]{:S(2)}, u32[]{:S(2)}) %collective-permute-start.3) | collective-permute-done | bytes 131104 | tf_op jit(solution)/shard_map/ppermute | solution.py:356
  17.3 0.7 shard_map.103
  18.0 19.8 %all_to_all.15.refs_0_ = f32[32,1,128]{2,1,0:T(1,128)S(1)} all-to-all(f32[32,1,128]{2,1,0:T(1,128)S(1)} %get-tuple-element.28), channel_id=1, replica_groups=mesh['x'=4,'core'=2,'y'=4,'z'=8] {'y','z'}, dimensions={0} | all-to-all | bytes 32768 | tf_op jit(solution)/shard_map/all_to_all | solution.py:392
  37.8 3.6 %shard_map.104 = (f32[320,128]{1,0:T(8,128)S(1)}, f32[320,128]{1,0:T(8,128)S(1)}, f32[320,128]{1,0:T(8,128)S(1)}, f32[320,128]{1,0:T(8,128)S(1)}) custom-call(f32[32,1,128]{2,1,0:T(1,128)S(1)} %all_to_all.15.refs_0_, f32[2,16,128]{2,1,0:T(8,128)S(1)} %get-tuple-element.29.refs_1_, f32[2,16,128]{2,1,0:T(8,128)S(1)} %get-tuple-element.30.refs_2_, ...), custom_call_target="tpu_custom_call" | custom-call | flops 1610612736 | bytes 1048576 | tf_op jit(solution)/shard_map/pallas_call | solution.py:343
  41.4 0.7 collective-permute-start.4
  42.1 2.0 %collective-permute-start.5 = (f32[320,128]{1,0:T(8,128)S(1)}, f32[320,128]{1,0:T(8,128)S(1)}, u32[]{:S(2)}, u32[]{:S(2)}) collective-permute-start(f32[320,128]{1,0:T(8,128)S(1)} %get-tuple-element.39), channel_id=1, source_target_pairs={{0,16},{8,24},{16,0},{24,8},{1,17},{9,25},{17,1},{25,9},{2,18},{10... | collective-permute-start | bytes 491528 | tf_op jit(solution)/shard_map/ppermute | solution.py:356
  44.1 1.2 %collective-permute-start.6 = (f32[320,128]{1,0:T(8,128)S(1)}, f32[320,128]{1,0:T(8,128)S(1)}, u32[]{:S(2)}, u32[]{:S(2)}) collective-permute-start(f32[320,128]{1,0:T(8,128)S(1)} %get-tuple-element.40), channel_id=1, source_target_pairs={{0,24},{8,0},{16,8},{24,16},{1,25},{9,1},{17,9},{25,17},{2,26},{10... | collective-permute-start | bytes 491528 | tf_op jit(solution)/shard_map/ppermute | solution.py:356
  45.3 5.6 %collective-permute-done.4.refs_1_ = f32[320,128]{1,0:T(8,128)S(1)} collective-permute-done((f32[320,128]{1,0:T(8,128)S(1)}, f32[320,128]{1,0:T(8,128)S(1)}, u32[]{:S(2)}, u32[]{:S(2)}) %collective-permute-start.4) | collective-permute-done | bytes 163872 | tf_op jit(solution)/shard_map/ppermute | solution.py:356
  51.0 0.0 collective-permute-done.5.refs_2_
  51.0 0.6 collective-permute-done.6.refs_3_
  51.6 0.1 shard_map.105
  51.6 11.8 %all_to_all.16.parts = f32[8,40,128]{2,1,0:T(8,128)S(1)} all-to-all(f32[8,40,128]{2,1,0:T(8,128)S(1)} %bitcast.27), channel_id=1, replica_groups=mesh['x'=4,'core'=2,'y'=4,'z'=8] {'z'}, dimensions={0} | all-to-all | bytes 327680 | tf_op jit(solution)/shard_map/all_to_all | solution.py:403
  63.4 11.8 %all_to_all.17 = f32[8,40,128]{2,1,0:T(8,128)S(1)} all-to-all(f32[8,40,128]{2,1,0:T(8,128)S(1)} %shard_map.106), channel_id=1, replica_groups=mesh['x'=4,'core'=2,'y'=4,'z'=8] {'z'}, dimensions={0} | all-to-all | bytes 327680 | tf_op jit(solution)/shard_map/all_to_all | solution.py:405
  75.2 2.7 %collective-permute-start.9 = (f32[320,128]{1,0:T(8,128)S(1)}, f32[320,128]{1,0:T(8,128)S(1)}, u32[]{:S(2)}, u32[]{:S(2)}) collective-permute-start(f32[320,128]{1,0:T(8,128)S(1)} %bitcast.23), channel_id=1, source_target_pairs={{0,24},{8,0},{16,8},{24,16},{1,25},{9,1},{17,9},{25,17},{2,26},{10... | collective-permute-start | bytes 491528 | tf_op jit(solution)/shard_map/ppermute | solution.py:356
  77.9 0.0 collective-permute-start.8
  77.9 0.8 collective-permute-start.7
  78.7 3.8 %collective-permute-done.9.refs_3_ = f32[320,128]{1,0:T(8,128)S(1)} collective-permute-done((f32[320,128]{1,0:T(8,128)S(1)}, f32[320,128]{1,0:T(8,128)S(1)}, u32[]{:S(2)}, u32[]{:S(2)}) %collective-permute-start.9) | collective-permute-done | bytes 163872 | tf_op jit(solution)/shard_map/ppermute | solution.py:356
  82.5 2.3 %collective-permute-done.8.refs_2_ = f32[320,128]{1,0:T(8,128)S(1)} collective-permute-done((f32[320,128]{1,0:T(8,128)S(1)}, f32[320,128]{1,0:T(8,128)S(1)}, u32[]{:S(2)}, u32[]{:S(2)}) %collective-permute-start.8) | collective-permute-done | bytes 163872 | tf_op jit(solution)/shard_map/ppermute | solution.py:356
  84.8 1.4 %collective-permute-done.7.refs_1_ = f32[320,128]{1,0:T(8,128)S(1)} collective-permute-done((f32[320,128]{1,0:T(8,128)S(1)}, f32[320,128]{1,0:T(8,128)S(1)}, u32[]{:S(2)}, u32[]{:S(2)}) %collective-permute-start.7) | collective-permute-done | bytes 163872 | tf_op jit(solution)/shard_map/ppermute | solution.py:356
  86.2 1.3 %shard_map.107 = (f32[16,16]{1,0:T(8,128)}, f32[1024,128]{1,0:T(8,128)}, f32[1024,128]{1,0:T(8,128)}, f32[8,128]{1,0:T(8,128)}) custom-call(f32[320,128]{1,0:T(8,128)S(1)} %bitcast.26, f32[320,128]{1,0:T(8,128)S(1)} %collective-permute-done.7.refs_1_, f32[320,128]{1,0:T(8,128)S(1)} %collective-permute-done.8.refs_2_, ...), custom_call_target="tpu_custom_call" | custom-call | flops 1048576 | bytes 1048576 | tf_op jit(solution)/shard_map/pallas_call | solution.py:343
  (2 shorter events, 0.0 us)
Async XLA Ops:
  7.1 4.5 %collective-permute-start.2 = (f32[64,128]{1,0:T(8,128)S(1)}, f32[64,128]{1,0:T(8,128)S(1)}, u32[]{:S(2)}, u32[]{:S(2)}) collective-permute-start(f32[64,128]{1,0:T(8,128)S(1)} %get-tuple-element.25.refs_0_.refs_4_), channel_id=1, source_target_pairs={{0,192},{64,0},{128,64},{192,128},{1,193},{65,1},{129,65},{193,129... | collective-permute-start | bytes 98312 | tf_op jit(solution)/shard_map/ppermute | solution.py:356
  10.0 5.4 %collective-permute-start.1 = (f32[64,128]{1,0:T(8,128)S(1)}, f32[64,128]{1,0:T(8,128)S(1)}, u32[]{:S(2)}, u32[]{:S(2)}) collective-permute-start(f32[64,128]{1,0:T(8,128)S(1)} %get-tuple-element.25.refs_0_.refs_4_), channel_id=1, source_target_pairs={{0,128},{64,192},{128,0},{192,64},{1,129},{65,193},{129,1},{193,65... | collective-permute-start | bytes 98312 | tf_op jit(solution)/shard_map/ppermute | solution.py:356
  10.8 5.1 %collective-permute-start = (f32[64,128]{1,0:T(8,128)S(1)}, f32[64,128]{1,0:T(8,128)S(1)}, u32[]{:S(2)}, u32[]{:S(2)}) collective-permute-start(f32[64,128]{1,0:T(8,128)S(1)} %get-tuple-element.25.refs_0_.refs_4_), channel_id=1, source_target_pairs={{0,64},{64,128},{128,192},{192,0},{1,65},{65,129},{129,193},{193,1... | collective-permute-start | bytes 98312 | tf_op jit(solution)/shard_map/ppermute | solution.py:356
  15.9 1.4 %collective-permute-start.3 = (f32[4,64,128]{2,1,0:T(8,128)S(1)}, f32[4,64,128]{2,1,0:T(8,128)S(1)}, u32[]{:S(2)}, u32[]{:S(2)}) collective-permute-start(f32[4,64,128]{2,1,0:T(8,128)S(1)} %pad_maximum_fusion), channel_id=1, source_target_pairs={{0,32},{32,0},{1,33},{33,1},{2,34},{34,2},{3,35},{35,3},{4,36},{36... | collective-permute-start | bytes 393224 | tf_op jit(solution)/shard_map/ppermute | solution.py:356
  41.4 9.6 %collective-permute-start.4 = (f32[320,128]{1,0:T(8,128)S(1)}, f32[320,128]{1,0:T(8,128)S(1)}, u32[]{:S(2)}, u32[]{:S(2)}) collective-permute-start(f32[320,128]{1,0:T(8,128)S(1)} %get-tuple-element.38), channel_id=1, source_target_pairs={{0,8},{8,16},{16,24},{24,0},{1,9},{9,17},{17,25},{25,1},{2,10},{10... | collective-permute-start | bytes 491528 | tf_op jit(solution)/shard_map/ppermute | solution.py:356
  42.1 8.9 %collective-permute-start.5 = (f32[320,128]{1,0:T(8,128)S(1)}, f32[320,128]{1,0:T(8,128)S(1)}, u32[]{:S(2)}, u32[]{:S(2)}) collective-permute-start(f32[320,128]{1,0:T(8,128)S(1)} %get-tuple-element.39), channel_id=1, source_target_pairs={{0,16},{8,24},{16,0},{24,8},{1,17},{9,25},{17,1},{25,9},{2,18},{10... | collective-permute-start | bytes 491528 | tf_op jit(solution)/shard_map/ppermute | solution.py:356
  44.1 7.5 %collective-permute-start.6 = (f32[320,128]{1,0:T(8,128)S(1)}, f32[320,128]{1,0:T(8,128)S(1)}, u32[]{:S(2)}, u32[]{:S(2)}) collective-permute-start(f32[320,128]{1,0:T(8,128)S(1)} %get-tuple-element.40), channel_id=1, source_target_pairs={{0,24},{8,0},{16,8},{24,16},{1,25},{9,1},{17,9},{25,17},{2,26},{10... | collective-permute-start | bytes 491528 | tf_op jit(solution)/shard_map/ppermute | solution.py:356
  75.2 7.3 %collective-permute-start.9 = (f32[320,128]{1,0:T(8,128)S(1)}, f32[320,128]{1,0:T(8,128)S(1)}, u32[]{:S(2)}, u32[]{:S(2)}) collective-permute-start(f32[320,128]{1,0:T(8,128)S(1)} %bitcast.23), channel_id=1, source_target_pairs={{0,24},{8,0},{16,8},{24,16},{1,25},{9,1},{17,9},{25,17},{2,26},{10... | collective-permute-start | bytes 491528 | tf_op jit(solution)/shard_map/ppermute | solution.py:356
  77.9 6.9 %collective-permute-start.8 = (f32[320,128]{1,0:T(8,128)S(1)}, f32[320,128]{1,0:T(8,128)S(1)}, u32[]{:S(2)}, u32[]{:S(2)}) collective-permute-start(f32[320,128]{1,0:T(8,128)S(1)} %bitcast.24), channel_id=1, source_target_pairs={{0,16},{8,24},{16,0},{24,8},{1,17},{9,25},{17,1},{25,9},{2,18},{10... | collective-permute-start | bytes 491528 | tf_op jit(solution)/shard_map/ppermute | solution.py:356
  77.9 8.3 %collective-permute-start.7 = (f32[320,128]{1,0:T(8,128)S(1)}, f32[320,128]{1,0:T(8,128)S(1)}, u32[]{:S(2)}, u32[]{:S(2)}) collective-permute-start(f32[320,128]{1,0:T(8,128)S(1)} %bitcast.25), channel_id=1, source_target_pairs={{0,8},{8,16},{16,24},{24,0},{1,9},{9,17},{17,25},{25,1},{2,10},{10... | collective-permute-start | bytes 491528 | tf_op jit(solution)/shard_map/ppermute | solution.py:356

commit v5 on v4

--- a/solution.py
+++ b/solution.py
@@ -204,13 +204,14 @@
 
 
 def energy_kernel(spread, *refs):
-    near, (others, potential, weights_in, message, sums, d_amp, d_hps, gathered, inverse_t) = refs[:XS], refs[XS:]
+    near, others = refs[:XS], refs[XS : 2 * XS]
+    potential, weights_in, message, sums, d_amp, d_hps, gathered, inverse_t = refs[2 * XS :]
     slots, walkers = potential.shape
     states = d_amp.shape[0]
     block = near[0].shape[0]
     me_x, me_core = lax.axis_index("x"), lax.axis_index("core")
     for k in range(XS):
-        for at, source in ((me_core, near[k]), (1 - me_core, others.at[k])):
+        for at, source in ((me_core, near[k]), (1 - me_core, others[k])):
             owner = (me_x + XS - k) % XS * 2 + at
             gathered[pl.ds(pl.multiple_of(owner * block, block), block), :] = source[...]
 
@@ -375,7 +376,7 @@
            ((states, hidden, 3 * BASIS), BF16), ((states, hidden, hidden), BF16), ((3 * BASIS, rows), BF16)],
         40, args, 2 * work, hbm=True)
     near = [send] + [along("x", send, k) for k in range(1, XS)]
-    others = along("core", jnp.stack(near), 1)
+    others = [along("core", block, 1) for block in near]
 
     def energy_body(*refs):
         energy_kernel(spread, *refs)
@@ -388,7 +389,7 @@
         [((shares, 1, walkers), F32), ((8, walkers), F32), ((states, slots, walkers), F32),
          ((states, slots, walkers), F32)],
         [((groups * 4 * slots, walkers), F32), ((slots, slots, walkers), F32)],
-        4, (*near, others, potential, weights), 1 << 20)
+        4, (*near, *others, potential, weights), 1 << 20)
     messages = lax.all_to_all(message, ("y", "z"), 0, 0, tiled=True)
     part = total // YS
     size = part // ZS

time: 87.7 us -> 87.5 us (level)
    ppermute x10 -> x13, waiting for transfers between devices: 19.3 us -> 18.6 us  [along(): lax.ppermute(array, axis, [(d, (d + shift) % size) for d in range(size)])]
    ppermute x10 -> x13, starting transfers between devices: 12.1 us -> 12.5 us  [along(): lax.ppermute(array, axis, [(d, (d + shift) % size) for d in range(size)])]
  transfers between devices with their start and end apart: 10 -> 13, of which waited for: 8 -> 9; matrix products, arithmetic and copies ran while one was open for 0% -> 0% of each run, Pallas kernels for 0% -> 0%
where the time goes in v5:
time: 87.5 us; the launch traced here: 87.3 us
  blocking collectives  43.4 us (50%)
  waiting for transfers between devices  18.6 us (21%)
  starting transfers between devices  12.5 us (14%)
  Pallas kernels  12.1 us (14%)
    all_to_all x1, blocking collectives, shards(): messages = lax.all_to_all(message, ('y', 'z'), 0, 0, tiled=True)  19.8 us
    ppermute x13, waiting for transfers between devices, along(): lax.ppermute(array, axis, [(d, (d + shift) % size) for d in range(size)])  18.6 us
    ppermute x13, starting transfers between devices, along(): lax.ppermute(array, axis, [(d, (d + shift) % size) for d in range(size)])  12.5 us
    pallas_call x6, Pallas kernels, call(): pl.pallas_call(body, out_shape=[jax.ShapeDtypeStruct(s, t) for s, t in ou...  12.1 us
    all_to_all x1, blocking collectives, shards(): summed = lax.all_to_all(pieces, 'z', 0, 0, tiled=True).reshape(part, 128)  11.8 us
    all_to_all x1, blocking collectives, shards(): lines = lax.all_to_all(line.reshape(ZS, size, 128), 'z', 0, 0, tiled=True)  11.8 us
  transfers between devices with their start and end apart: 13, of which 9 were waited for; matrix products, arithmetic and copies ran while one was open for 0% of the time, Pallas kernels for 0%

profile of v5, /device:TPU:32, one launch (start us, length us, event | category | flops | bytes accessed | tf_op | source)
XLA Modules:
  0.0 87.3 jit_solution(4646499954689929609)
XLA Ops:
  0.6 6.5 %shard_map.102 = (f32[64,128]{1,0:T(8,128)S(1)}, f32[16,128]{1,0:T(8,128)S(1)}, bf16[64,2048]{1,0:T(8,128)(2,1)S(1)}, f32[2,256,2048]{2,1,0:T(8,128)S(1)}, f32[2...) custom-call(f32[2,30,16,128]{3,2,1,0:T(8,128)} %pos_in.1, ...), custom_call_target="tpu_custom_call" | custom-call | flops 1073741824 | bytes 1048576 | tf_op jit(solution)/shard_map/pallas_call | solution.py:344
  7.1 2.8 %collective-permute-start.2 = (f32[64,128]{1,0:T(8,128)S(1)}, f32[64,128]{1,0:T(8,128)S(1)}, u32[]{:S(2)}, u32[]{:S(2)}) collective-permute-start(f32[64,128]{1,0:T(8,128)S(1)} %get-tuple-element.25.refs_0_.refs_4_), channel_id=1, source_target_pairs={{0,192},{64,0},{128,64},{192,128},{1,193},{65,1},{129,65},{193,129... | collective-permute-start | bytes 98312 | tf_op jit(solution)/shard_map/ppermute | solution.py:357
  10.0 0.8 collective-permute-start.1
  10.8 0.9 %collective-permute-start = (f32[64,128]{1,0:T(8,128)S(1)}, f32[64,128]{1,0:T(8,128)S(1)}, u32[]{:S(2)}, u32[]{:S(2)}) collective-permute-start(f32[64,128]{1,0:T(8,128)S(1)} %get-tuple-element.25.refs_0_.refs_4_), channel_id=1, source_target_pairs={{0,64},{64,128},{128,192},{192,0},{1,65},{65,129},{129,193},{193,1... | collective-permute-start | bytes 98312 | tf_op jit(solution)/shard_map/ppermute | solution.py:357
  11.6 0.0 collective-permute-start.3
  11.6 0.0 collective-permute-done.2.refs_3_
  11.6 0.5 collective-permute-start.6
  12.2 3.2 %collective-permute-done.1.refs_2_ = f32[64,128]{1,0:T(8,128)S(1)} collective-permute-done((f32[64,128]{1,0:T(8,128)S(1)}, f32[64,128]{1,0:T(8,128)S(1)}, u32[]{:S(2)}, u32[]{:S(2)}) %collective-permute-start.1) | collective-permute-done | bytes 32800 | tf_op jit(solution)/shard_map/ppermute | solution.py:357
  15.4 0.0 collective-permute-start.5
  15.4 0.5 collective-permute-done.refs_1_
  15.9 0.0 collective-permute-start.4
  15.9 0.0 collective-permute-done.3.refs_4_
  15.9 0.0 collective-permute-done.6.refs_7_
  15.9 0.7 collective-permute-done.5.refs_6_
  16.6 0.5 collective-permute-done.4.refs_5_
  17.1 0.7 shard_map.103
  17.8 19.8 %all_to_all.15.refs_0_ = f32[32,1,128]{2,1,0:T(1,128)S(1)} all-to-all(f32[32,1,128]{2,1,0:T(1,128)S(1)} %get-tuple-element.28), channel_id=1, replica_groups=mesh['x'=4,'core'=2,'y'=4,'z'=8] {'y','z'}, dimensions={0} | all-to-all | bytes 32768 | tf_op jit(solution)/shard_map/all_to_all | solution.py:393
  37.5 3.6 %shard_map.104 = (f32[320,128]{1,0:T(8,128)S(1)}, f32[320,128]{1,0:T(8,128)S(1)}, f32[320,128]{1,0:T(8,128)S(1)}, f32[320,128]{1,0:T(8,128)S(1)}) custom-call(f32[32,1,128]{2,1,0:T(1,128)S(1)} %all_to_all.15.refs_0_, f32[2,16,128]{2,1,0:T(8,128)S(1)} %get-tuple-element.29.refs_1_, f32[2,16,128]{2,1,0:T(8,128)S(1)} %get-tuple-element.30.refs_2_, ...), custom_call_target="tpu_custom_call" | custom-call | flops 1610612736 | bytes 1048576 | tf_op jit(solution)/shard_map/pallas_call | solution.py:344
  41.1 0.7 collective-permute-start.7
  41.8 2.0 %collective-permute-start.8 = (f32[320,128]{1,0:T(8,128)S(1)}, f32[320,128]{1,0:T(8,128)S(1)}, u32[]{:S(2)}, u32[]{:S(2)}) collective-permute-start(f32[320,128]{1,0:T(8,128)S(1)} %get-tuple-element.39), channel_id=1, source_target_pairs={{0,16},{8,24},{16,0},{24,8},{1,17},{9,25},{17,1},{25,9},{2,18},{10... | collective-permute-start | bytes 491528 | tf_op jit(solution)/shard_map/ppermute | solution.py:357
  43.8 1.2 %collective-permute-start.9 = (f32[320,128]{1,0:T(8,128)S(1)}, f32[320,128]{1,0:T(8,128)S(1)}, u32[]{:S(2)}, u32[]{:S(2)}) collective-permute-start(f32[320,128]{1,0:T(8,128)S(1)} %get-tuple-element.40), channel_id=1, source_target_pairs={{0,24},{8,0},{16,8},{24,16},{1,25},{9,1},{17,9},{25,17},{2,26},{10... | collective-permute-start | bytes 491528 | tf_op jit(solution)/shard_map/ppermute | solution.py:357
  45.1 5.7 %collective-permute-done.7.refs_1_ = f32[320,128]{1,0:T(8,128)S(1)} collective-permute-done((f32[320,128]{1,0:T(8,128)S(1)}, f32[320,128]{1,0:T(8,128)S(1)}, u32[]{:S(2)}, u32[]{:S(2)}) %collective-permute-start.7) | collective-permute-done | bytes 163872 | tf_op jit(solution)/shard_map/ppermute | solution.py:357
  50.7 0.0 collective-permute-done.8.refs_2_
  50.8 0.6 collective-permute-done.9.refs_3_
  51.3 0.1 shard_map.105
  51.4 11.8 %all_to_all.16.parts = f32[8,40,128]{2,1,0:T(8,128)S(1)} all-to-all(f32[8,40,128]{2,1,0:T(8,128)S(1)} %bitcast.23), channel_id=1, replica_groups=mesh['x'=4,'core'=2,'y'=4,'z'=8] {'z'}, dimensions={0} | all-to-all | bytes 327680 | tf_op jit(solution)/shard_map/all_to_all | solution.py:404
  63.2 11.8 %all_to_all.17 = f32[8,40,128]{2,1,0:T(8,128)S(1)} all-to-all(f32[8,40,128]{2,1,0:T(8,128)S(1)} %shard_map.106), channel_id=1, replica_groups=mesh['x'=4,'core'=2,'y'=4,'z'=8] {'z'}, dimensions={0} | all-to-all | bytes 327680 | tf_op jit(solution)/shard_map/all_to_all | solution.py:406
  75.0 2.7 %collective-permute-start.12 = (f32[320,128]{1,0:T(8,128)S(1)}, f32[320,128]{1,0:T(8,128)S(1)}, u32[]{:S(2)}, u32[]{:S(2)}) collective-permute-start(f32[320,128]{1,0:T(8,128)S(1)} %bitcast.19), channel_id=1, source_target_pairs={{0,24},{8,0},{16,8},{24,16},{1,25},{9,1},{17,9},{25,17},{2,26},{10... | collective-permute-start | bytes 491528 | tf_op jit(solution)/shard_map/ppermute | solution.py:357
  77.7 0.0 collective-permute-start.11
  77.7 0.8 collective-permute-start.10
  78.5 3.8 %collective-permute-done.12.refs_3_ = f32[320,128]{1,0:T(8,128)S(1)} collective-permute-done((f32[320,128]{1,0:T(8,128)S(1)}, f32[320,128]{1,0:T(8,128)S(1)}, u32[]{:S(2)}, u32[]{:S(2)}) %collective-permute-start.12) | collective-permute-done | bytes 163872 | tf_op jit(solution)/shard_map/ppermute | solution.py:357
  82.3 2.3 %collective-permute-done.11.refs_2_ = f32[320,128]{1,0:T(8,128)S(1)} collective-permute-done((f32[320,128]{1,0:T(8,128)S(1)}, f32[320,128]{1,0:T(8,128)S(1)}, u32[]{:S(2)}, u32[]{:S(2)}) %collective-permute-start.11) | collective-permute-done | bytes 163872 | tf_op jit(solution)/shard_map/ppermute | solution.py:357
  84.6 1.4 %collective-permute-done.10.refs_1_ = f32[320,128]{1,0:T(8,128)S(1)} collective-permute-done((f32[320,128]{1,0:T(8,128)S(1)}, f32[320,128]{1,0:T(8,128)S(1)}, u32[]{:S(2)}, u32[]{:S(2)}) %collective-permute-start.10) | collective-permute-done | bytes 163872 | tf_op jit(solution)/shard_map/ppermute | solution.py:357
  86.0 1.3 %shard_map.107 = (f32[16,16]{1,0:T(8,128)}, f32[1024,128]{1,0:T(8,128)}, f32[1024,128]{1,0:T(8,128)}, f32[8,128]{1,0:T(8,128)}) custom-call(f32[320,128]{1,0:T(8,128)S(1)} %bitcast.22, f32[320,128]{1,0:T(8,128)S(1)} %collective-permute-done.10.refs_1_, f32[320,128]{1,0:T(8,128)S(1)} %collective-permute-done.11.refs_2_, ...), custom_call_target="tpu_custom_call" | custom-call | flops 1048576 | bytes 1048576 | tf_op jit(solution)/shard_map/pallas_call | solution.py:344
  (1 shorter events, 0.0 us)
Async XLA Ops:
  7.1 4.5 %collective-permute-start.2 = (f32[64,128]{1,0:T(8,128)S(1)}, f32[64,128]{1,0:T(8,128)S(1)}, u32[]{:S(2)}, u32[]{:S(2)}) collective-permute-start(f32[64,128]{1,0:T(8,128)S(1)} %get-tuple-element.25.refs_0_.refs_4_), channel_id=1, source_target_pairs={{0,192},{64,0},{128,64},{192,128},{1,193},{65,1},{129,65},{193,129... | collective-permute-start | bytes 98312 | tf_op jit(solution)/shard_map/ppermute | solution.py:357
  10.0 5.4 %collective-permute-start.1 = (f32[64,128]{1,0:T(8,128)S(1)}, f32[64,128]{1,0:T(8,128)S(1)}, u32[]{:S(2)}, u32[]{:S(2)}) collective-permute-start(f32[64,128]{1,0:T(8,128)S(1)} %get-tuple-element.25.refs_0_.refs_4_), channel_id=1, source_target_pairs={{0,128},{64,192},{128,0},{192,64},{1,129},{65,193},{129,1},{193,65... | collective-permute-start | bytes 98312 | tf_op jit(solution)/shard_map/ppermute | solution.py:357
  10.8 5.1 %collective-permute-start = (f32[64,128]{1,0:T(8,128)S(1)}, f32[64,128]{1,0:T(8,128)S(1)}, u32[]{:S(2)}, u32[]{:S(2)}) collective-permute-start(f32[64,128]{1,0:T(8,128)S(1)} %get-tuple-element.25.refs_0_.refs_4_), channel_id=1, source_target_pairs={{0,64},{64,128},{128,192},{192,0},{1,65},{65,129},{129,193},{193,1... | collective-permute-start | bytes 98312 | tf_op jit(solution)/shard_map/ppermute | solution.py:357
  11.6 4.3 %collective-permute-start.3 = (f32[64,128]{1,0:T(8,128)S(1)}, f32[64,128]{1,0:T(8,128)S(1)}, u32[]{:S(2)}, u32[]{:S(2)}) collective-permute-start(f32[64,128]{1,0:T(8,128)S(1)} %get-tuple-element.25.refs_0_.refs_4_), channel_id=1, source_target_pairs={{0,32},{32,0},{1,33},{33,1},{2,34},{34,2},{3,35},{35,3},{4,36},{36... | collective-permute-start | bytes 98312 | tf_op jit(solution)/shard_map/ppermute | solution.py:357
  11.6 4.3 %collective-permute-start.6 = (f32[64,128]{1,0:T(8,128)S(1)}, f32[64,128]{1,0:T(8,128)S(1)}, u32[]{:S(2)}, u32[]{:S(2)}) collective-permute-start(f32[64,128]{1,0:T(8,128)S(1)} %collective-permute-done.2.refs_3_), channel_id=1, source_target_pairs={{0,32},{32,0},{1,33},{33,1},{2,34},{34,2},{3,35},{35,3},{4,36},{36... | collective-permute-start | bytes 98312 | tf_op jit(solution)/shard_map/ppermute | solution.py:357
  15.4 1.2 %collective-permute-start.5 = (f32[64,128]{1,0:T(8,128)S(1)}, f32[64,128]{1,0:T(8,128)S(1)}, u32[]{:S(2)}, u32[]{:S(2)}) collective-permute-start(f32[64,128]{1,0:T(8,128)S(1)} %collective-permute-done.1.refs_2_), channel_id=1, source_target_pairs={{0,32},{32,0},{1,33},{33,1},{2,34},{34,2},{3,35},{35,3},{4,36},{36... | collective-permute-start | bytes 98312 | tf_op jit(solution)/shard_map/ppermute | solution.py:357
  15.9 1.2 %collective-permute-start.4 = (f32[64,128]{1,0:T(8,128)S(1)}, f32[64,128]{1,0:T(8,128)S(1)}, u32[]{:S(2)}, u32[]{:S(2)}) collective-permute-start(f32[64,128]{1,0:T(8,128)S(1)} %collective-permute-done.refs_1_), channel_id=1, source_target_pairs={{0,32},{32,0},{1,33},{33,1},{2,34},{34,2},{3,35},{35,3},{4,36},{36... | collective-permute-start | bytes 98312 | tf_op jit(solution)/shard_map/ppermute | solution.py:357
  41.1 9.6 %collective-permute-start.7 = (f32[320,128]{1,0:T(8,128)S(1)}, f32[320,128]{1,0:T(8,128)S(1)}, u32[]{:S(2)}, u32[]{:S(2)}) collective-permute-start(f32[320,128]{1,0:T(8,128)S(1)} %get-tuple-element.38), channel_id=1, source_target_pairs={{0,8},{8,16},{16,24},{24,0},{1,9},{9,17},{17,25},{25,1},{2,10},{10... | collective-permute-start | bytes 491528 | tf_op jit(solution)/shard_map/ppermute | solution.py:357
  41.8 8.9 %collective-permute-start.8 = (f32[320,128]{1,0:T(8,128)S(1)}, f32[320,128]{1,0:T(8,128)S(1)}, u32[]{:S(2)}, u32[]{:S(2)}) collective-permute-start(f32[320,128]{1,0:T(8,128)S(1)} %get-tuple-element.39), channel_id=1, source_target_pairs={{0,16},{8,24},{16,0},{24,8},{1,17},{9,25},{17,1},{25,9},{2,18},{10... | collective-permute-start | bytes 491528 | tf_op jit(solution)/shard_map/ppermute | solution.py:357
  43.8 7.5 %collective-permute-start.9 = (f32[320,128]{1,0:T(8,128)S(1)}, f32[320,128]{1,0:T(8,128)S(1)}, u32[]{:S(2)}, u32[]{:S(2)}) collective-permute-start(f32[320,128]{1,0:T(8,128)S(1)} %get-tuple-element.40), channel_id=1, source_target_pairs={{0,24},{8,0},{16,8},{24,16},{1,25},{9,1},{17,9},{25,17},{2,26},{10... | collective-permute-start | bytes 491528 | tf_op jit(solution)/shard_map/ppermute | solution.py:357
  75.0 7.3 %collective-permute-start.12 = (f32[320,128]{1,0:T(8,128)S(1)}, f32[320,128]{1,0:T(8,128)S(1)}, u32[]{:S(2)}, u32[]{:S(2)}) collective-permute-start(f32[320,128]{1,0:T(8,128)S(1)} %bitcast.19), channel_id=1, source_target_pairs={{0,24},{8,0},{16,8},{24,16},{1,25},{9,1},{17,9},{25,17},{2,26},{10... | collective-permute-start | bytes 491528 | tf_op jit(solution)/shard_map/ppermute | solution.py:357
  77.7 6.9 %collective-permute-start.11 = (f32[320,128]{1,0:T(8,128)S(1)}, f32[320,128]{1,0:T(8,128)S(1)}, u32[]{:S(2)}, u32[]{:S(2)}) collective-permute-start(f32[320,128]{1,0:T(8,128)S(1)} %bitcast.20), channel_id=1, source_target_pairs={{0,16},{8,24},{16,0},{24,8},{1,17},{9,25},{17,1},{25,9},{2,18},{10... | collective-permute-start | bytes 491528 | tf_op jit(solution)/shard_map/ppermute | solution.py:357
  77.7 8.3 %collective-permute-start.10 = (f32[320,128]{1,0:T(8,128)S(1)}, f32[320,128]{1,0:T(8,128)S(1)}, u32[]{:S(2)}, u32[]{:S(2)}) collective-permute-start(f32[320,128]{1,0:T(8,128)S(1)} %bitcast.21), channel_id=1, source_target_pairs={{0,8},{8,16},{16,24},{24,0},{1,9},{9,17},{17,25},{25,1},{2,10},{10... | collective-permute-start | bytes 491528 | tf_op jit(solution)/shard_map/ppermute | solution.py:357

commit v6 on v5

--- a/solution.py
+++ b/solution.py
@@ -88,7 +88,7 @@
         turns[2, e], turns[3, e] = turn(2.0 * third)
         return carry
 
-    lax.fori_loop(0, electrons, phases, 0, unroll=5)
+    lax.fori_loop(0, electrons, phases, 0, unroll=10)
 
     def powers(e, rows, at, upto):
         one = (turns[at, e, rows], turns[at + 1, e, rows])
@@ -120,7 +120,7 @@
                 return tuple(t + p for t, p in zip(totals, parts, strict=True))
 
             number = 12 * len(firsts) + (12 if alone else 0)
-            totals = lax.fori_loop(0, electrons, add, (zero,) * number, unroll=6)
+            totals = lax.fori_loop(0, electrons, add, (zero,) * number, unroll=10)
             for i, m in enumerate(firsts):
                 for n in (1, 2, 3):
                     cc, ss, sc, cs = totals[12 * i + 4 * (n - 1) : 12 * i + 4 * n]
@@ -328,11 +328,10 @@
     note = summed[pl.ds(4 * (2 * COSINES + 1), 8), :]
     for half in range(slots // 8):
         energy[pl.ds(half * 8, 8), :] = note[:, half * slots : (half + 1) * slots]
+    value = jnp.concatenate([summed[pl.ds(at, BASIS, stride=4), :] for at in range(4)], axis=1)
+    rows = lax.dot_general(select[...], jnp.concatenate(three_parts(value), axis=0), NN, preferred_element_type=F32)
     for at in range(4):
-        value = summed[pl.ds(at, BASIS, stride=4), :]
-        parts = jnp.concatenate(three_parts(value), axis=0)
-        rows = lax.dot_general(select[...], parts, NN, preferred_element_type=F32)
-        grad_first[pl.ds(at, rows.shape[0], stride=4), :] = rows
+        grad_first[pl.ds(at, rows.shape[0], stride=4), :] = rows[:, at * 128 : (at + 1) * 128]
     grad_second[...] = summed[pl.ds(4 * BASIS, grad_second.shape[0]), :]
     grad_heads[...] = summed[pl.ds(4 * (2 * COSINES - 1), grad_heads.shape[0]), :]
 

time: 87.5 us -> 87.3 us (level)
  no operation moved by 1% of the time
where the time goes in v6:
time: 87.3 us; the launch traced here: 87.1 us
  blocking collectives  43.4 us (50%)
  waiting for transfers between devices  18.6 us (21%)
  starting transfers between devices  12.5 us (14%)
  Pallas kernels  11.9 us (14%)
    all_to_all x1, blocking collectives, shards(): messages = lax.all_to_all(message, ('y', 'z'), 0, 0, tiled=True)  19.8 us
    ppermute x13, waiting for transfers between devices, along(): lax.ppermute(array, axis, [(d, (d + shift) % size) for d in range(size)])  18.6 us
    ppermute x13, starting transfers between devices, along(): lax.ppermute(array, axis, [(d, (d + shift) % size) for d in range(size)])  12.5 us
    pallas_call x6, Pallas kernels, call(): pl.pallas_call(body, out_shape=[jax.ShapeDtypeStruct(s, t) for s, t in ou...  11.9 us
    all_to_all x1, blocking collectives, shards(): summed = lax.all_to_all(pieces, 'z', 0, 0, tiled=True).reshape(part, 128)  11.8 us
    all_to_all x1, blocking collectives, shards(): lines = lax.all_to_all(line.reshape(ZS, size, 128), 'z', 0, 0, tiled=True)  11.8 us
  transfers between devices with their start and end apart: 13, of which 9 were waited for; matrix products, arithmetic and copies ran while one was open for 0% of the time, Pallas kernels for 0%

profile of v6, /device:TPU:32, one launch (start us, length us, event | category | flops | bytes accessed | tf_op | source)
XLA Modules:
  0.0 87.1 jit_solution(2903362675246175891)
XLA Ops:
  0.6 6.4 %shard_map.102 = (f32[64,128]{1,0:T(8,128)S(1)}, f32[16,128]{1,0:T(8,128)S(1)}, bf16[64,2048]{1,0:T(8,128)(2,1)S(1)}, f32[2,256,2048]{2,1,0:T(8,128)S(1)}, f32[2...) custom-call(f32[2,30,16,128]{3,2,1,0:T(8,128)} %pos_in.1, ...), custom_call_target="tpu_custom_call" | custom-call | flops 1073741824 | bytes 1048576 | tf_op jit(solution)/shard_map/pallas_call | solution.py:343
  7.0 2.8 %collective-permute-start.2 = (f32[64,128]{1,0:T(8,128)S(1)}, f32[64,128]{1,0:T(8,128)S(1)}, u32[]{:S(2)}, u32[]{:S(2)}) collective-permute-start(f32[64,128]{1,0:T(8,128)S(1)} %get-tuple-element.25.refs_0_.refs_4_), channel_id=1, source_target_pairs={{0,192},{64,0},{128,64},{192,128},{1,193},{65,1},{129,65},{193,129... | collective-permute-start | bytes 98312 | tf_op jit(solution)/shard_map/ppermute | solution.py:356
  9.8 0.8 collective-permute-start.1
  10.6 0.9 %collective-permute-start = (f32[64,128]{1,0:T(8,128)S(1)}, f32[64,128]{1,0:T(8,128)S(1)}, u32[]{:S(2)}, u32[]{:S(2)}) collective-permute-start(f32[64,128]{1,0:T(8,128)S(1)} %get-tuple-element.25.refs_0_.refs_4_), channel_id=1, source_target_pairs={{0,64},{64,128},{128,192},{192,0},{1,65},{65,129},{129,193},{193,1... | collective-permute-start | bytes 98312 | tf_op jit(solution)/shard_map/ppermute | solution.py:356
  11.5 0.0 collective-permute-start.3
  11.5 0.0 collective-permute-done.2.refs_3_
  11.5 0.5 collective-permute-start.6
  12.0 3.2 %collective-permute-done.1.refs_2_ = f32[64,128]{1,0:T(8,128)S(1)} collective-permute-done((f32[64,128]{1,0:T(8,128)S(1)}, f32[64,128]{1,0:T(8,128)S(1)}, u32[]{:S(2)}, u32[]{:S(2)}) %collective-permute-start.1) | collective-permute-done | bytes 32800 | tf_op jit(solution)/shard_map/ppermute | solution.py:356
  15.3 0.0 collective-permute-start.5
  15.3 0.5 collective-permute-done.refs_1_
  15.8 0.0 collective-permute-start.4
  15.8 0.0 collective-permute-done.3.refs_4_
  15.8 0.0 collective-permute-done.6.refs_7_
  15.8 0.7 collective-permute-done.5.refs_6_
  16.5 0.5 collective-permute-done.4.refs_5_
  17.0 0.7 shard_map.103
  17.6 19.8 %all_to_all.15.refs_0_ = f32[32,1,128]{2,1,0:T(1,128)S(1)} all-to-all(f32[32,1,128]{2,1,0:T(1,128)S(1)} %get-tuple-element.28), channel_id=1, replica_groups=mesh['x'=4,'core'=2,'y'=4,'z'=8] {'y','z'}, dimensions={0} | all-to-all | bytes 32768 | tf_op jit(solution)/shard_map/all_to_all | solution.py:392
  37.4 3.6 %shard_map.104 = (f32[320,128]{1,0:T(8,128)S(1)}, f32[320,128]{1,0:T(8,128)S(1)}, f32[320,128]{1,0:T(8,128)S(1)}, f32[320,128]{1,0:T(8,128)S(1)}) custom-call(f32[32,1,128]{2,1,0:T(1,128)S(1)} %all_to_all.15.refs_0_, f32[2,16,128]{2,1,0:T(8,128)S(1)} %get-tuple-element.29.refs_1_, f32[2,16,128]{2,1,0:T(8,128)S(1)} %get-tuple-element.30.refs_2_, ...), custom_call_target="tpu_custom_call" | custom-call | flops 1610612736 | bytes 1048576 | tf_op jit(solution)/shard_map/pallas_call | solution.py:343
  41.0 0.7 collective-permute-start.7
  41.7 2.0 %collective-permute-start.8 = (f32[320,128]{1,0:T(8,128)S(1)}, f32[320,128]{1,0:T(8,128)S(1)}, u32[]{:S(2)}, u32[]{:S(2)}) collective-permute-start(f32[320,128]{1,0:T(8,128)S(1)} %get-tuple-element.39), channel_id=1, source_target_pairs={{0,16},{8,24},{16,0},{24,8},{1,17},{9,25},{17,1},{25,9},{2,18},{10... | collective-permute-start | bytes 491528 | tf_op jit(solution)/shard_map/ppermute | solution.py:356
  43.7 1.2 %collective-permute-start.9 = (f32[320,128]{1,0:T(8,128)S(1)}, f32[320,128]{1,0:T(8,128)S(1)}, u32[]{:S(2)}, u32[]{:S(2)}) collective-permute-start(f32[320,128]{1,0:T(8,128)S(1)} %get-tuple-element.40), channel_id=1, source_target_pairs={{0,24},{8,0},{16,8},{24,16},{1,25},{9,1},{17,9},{25,17},{2,26},{10... | collective-permute-start | bytes 491528 | tf_op jit(solution)/shard_map/ppermute | solution.py:356
  45.0 5.7 %collective-permute-done.7.refs_1_ = f32[320,128]{1,0:T(8,128)S(1)} collective-permute-done((f32[320,128]{1,0:T(8,128)S(1)}, f32[320,128]{1,0:T(8,128)S(1)}, u32[]{:S(2)}, u32[]{:S(2)}) %collective-permute-start.7) | collective-permute-done | bytes 163872 | tf_op jit(solution)/shard_map/ppermute | solution.py:356
  50.6 0.0 collective-permute-done.8.refs_2_
  50.6 0.6 collective-permute-done.9.refs_3_
  51.2 0.1 shard_map.105
  51.3 11.8 %all_to_all.16.parts = f32[8,40,128]{2,1,0:T(8,128)S(1)} all-to-all(f32[8,40,128]{2,1,0:T(8,128)S(1)} %bitcast.23), channel_id=1, replica_groups=mesh['x'=4,'core'=2,'y'=4,'z'=8] {'z'}, dimensions={0} | all-to-all | bytes 327680 | tf_op jit(solution)/shard_map/all_to_all | solution.py:403
  63.1 11.8 %all_to_all.17 = f32[8,40,128]{2,1,0:T(8,128)S(1)} all-to-all(f32[8,40,128]{2,1,0:T(8,128)S(1)} %shard_map.106), channel_id=1, replica_groups=mesh['x'=4,'core'=2,'y'=4,'z'=8] {'z'}, dimensions={0} | all-to-all | bytes 327680 | tf_op jit(solution)/shard_map/all_to_all | solution.py:405
  74.9 2.7 %collective-permute-start.12 = (f32[320,128]{1,0:T(8,128)S(1)}, f32[320,128]{1,0:T(8,128)S(1)}, u32[]{:S(2)}, u32[]{:S(2)}) collective-permute-start(f32[320,128]{1,0:T(8,128)S(1)} %bitcast.19), channel_id=1, source_target_pairs={{0,24},{8,0},{16,8},{24,16},{1,25},{9,1},{17,9},{25,17},{2,26},{10... | collective-permute-start | bytes 491528 | tf_op jit(solution)/shard_map/ppermute | solution.py:356
  77.5 0.0 collective-permute-start.11
  77.6 0.8 collective-permute-start.10
  78.4 3.8 %collective-permute-done.12.refs_3_ = f32[320,128]{1,0:T(8,128)S(1)} collective-permute-done((f32[320,128]{1,0:T(8,128)S(1)}, f32[320,128]{1,0:T(8,128)S(1)}, u32[]{:S(2)}, u32[]{:S(2)}) %collective-permute-start.12) | collective-permute-done | bytes 163872 | tf_op jit(solution)/shard_map/ppermute | solution.py:356
  82.2 2.3 %collective-permute-done.11.refs_2_ = f32[320,128]{1,0:T(8,128)S(1)} collective-permute-done((f32[320,128]{1,0:T(8,128)S(1)}, f32[320,128]{1,0:T(8,128)S(1)}, u32[]{:S(2)}, u32[]{:S(2)}) %collective-permute-start.11) | collective-permute-done | bytes 163872 | tf_op jit(solution)/shard_map/ppermute | solution.py:356
  84.5 1.4 %collective-permute-done.10.refs_1_ = f32[320,128]{1,0:T(8,128)S(1)} collective-permute-done((f32[320,128]{1,0:T(8,128)S(1)}, f32[320,128]{1,0:T(8,128)S(1)}, u32[]{:S(2)}, u32[]{:S(2)}) %collective-permute-start.10) | collective-permute-done | bytes 163872 | tf_op jit(solution)/shard_map/ppermute | solution.py:356
  85.9 1.3 %shard_map.107 = (f32[16,16]{1,0:T(8,128)}, f32[1024,128]{1,0:T(8,128)}, f32[1024,128]{1,0:T(8,128)}, f32[8,128]{1,0:T(8,128)}) custom-call(f32[320,128]{1,0:T(8,128)S(1)} %bitcast.22, f32[320,128]{1,0:T(8,128)S(1)} %collective-permute-done.10.refs_1_, f32[320,128]{1,0:T(8,128)S(1)} %collective-permute-done.11.refs_2_, ...), custom_call_target="tpu_custom_call" | custom-call | flops 1048576 | bytes 1048576 | tf_op jit(solution)/shard_map/pallas_call | solution.py:343
  (1 shorter events, 0.0 us)
Async XLA Ops:
  7.0 4.5 %collective-permute-start.2 = (f32[64,128]{1,0:T(8,128)S(1)}, f32[64,128]{1,0:T(8,128)S(1)}, u32[]{:S(2)}, u32[]{:S(2)}) collective-permute-start(f32[64,128]{1,0:T(8,128)S(1)} %get-tuple-element.25.refs_0_.refs_4_), channel_id=1, source_target_pairs={{0,192},{64,0},{128,64},{192,128},{1,193},{65,1},{129,65},{193,129... | collective-permute-start | bytes 98312 | tf_op jit(solution)/shard_map/ppermute | solution.py:356
  9.8 5.4 %collective-permute-start.1 = (f32[64,128]{1,0:T(8,128)S(1)}, f32[64,128]{1,0:T(8,128)S(1)}, u32[]{:S(2)}, u32[]{:S(2)}) collective-permute-start(f32[64,128]{1,0:T(8,128)S(1)} %get-tuple-element.25.refs_0_.refs_4_), channel_id=1, source_target_pairs={{0,128},{64,192},{128,0},{192,64},{1,129},{65,193},{129,1},{193,65... | collective-permute-start | bytes 98312 | tf_op jit(solution)/shard_map/ppermute | solution.py:356
  10.6 5.1 %collective-permute-start = (f32[64,128]{1,0:T(8,128)S(1)}, f32[64,128]{1,0:T(8,128)S(1)}, u32[]{:S(2)}, u32[]{:S(2)}) collective-permute-start(f32[64,128]{1,0:T(8,128)S(1)} %get-tuple-element.25.refs_0_.refs_4_), channel_id=1, source_target_pairs={{0,64},{64,128},{128,192},{192,0},{1,65},{65,129},{129,193},{193,1... | collective-permute-start | bytes 98312 | tf_op jit(solution)/shard_map/ppermute | solution.py:356
  11.5 4.3 %collective-permute-start.3 = (f32[64,128]{1,0:T(8,128)S(1)}, f32[64,128]{1,0:T(8,128)S(1)}, u32[]{:S(2)}, u32[]{:S(2)}) collective-permute-start(f32[64,128]{1,0:T(8,128)S(1)} %get-tuple-element.25.refs_0_.refs_4_), channel_id=1, source_target_pairs={{0,32},{32,0},{1,33},{33,1},{2,34},{34,2},{3,35},{35,3},{4,36},{36... | collective-permute-start | bytes 98312 | tf_op jit(solution)/shard_map/ppermute | solution.py:356
  11.5 4.3 %collective-permute-start.6 = (f32[64,128]{1,0:T(8,128)S(1)}, f32[64,128]{1,0:T(8,128)S(1)}, u32[]{:S(2)}, u32[]{:S(2)}) collective-permute-start(f32[64,128]{1,0:T(8,128)S(1)} %collective-permute-done.2.refs_3_), channel_id=1, source_target_pairs={{0,32},{32,0},{1,33},{33,1},{2,34},{34,2},{3,35},{35,3},{4,36},{36... | collective-permute-start | bytes 98312 | tf_op jit(solution)/shard_map/ppermute | solution.py:356
  15.3 1.2 %collective-permute-start.5 = (f32[64,128]{1,0:T(8,128)S(1)}, f32[64,128]{1,0:T(8,128)S(1)}, u32[]{:S(2)}, u32[]{:S(2)}) collective-permute-start(f32[64,128]{1,0:T(8,128)S(1)} %collective-permute-done.1.refs_2_), channel_id=1, source_target_pairs={{0,32},{32,0},{1,33},{33,1},{2,34},{34,2},{3,35},{35,3},{4,36},{36... | collective-permute-start | bytes 98312 | tf_op jit(solution)/shard_map/ppermute | solution.py:356
  15.8 1.2 %collective-permute-start.4 = (f32[64,128]{1,0:T(8,128)S(1)}, f32[64,128]{1,0:T(8,128)S(1)}, u32[]{:S(2)}, u32[]{:S(2)}) collective-permute-start(f32[64,128]{1,0:T(8,128)S(1)} %collective-permute-done.refs_1_), channel_id=1, source_target_pairs={{0,32},{32,0},{1,33},{33,1},{2,34},{34,2},{3,35},{35,3},{4,36},{36... | collective-permute-start | bytes 98312 | tf_op jit(solution)/shard_map/ppermute | solution.py:356
  41.0 9.6 %collective-permute-start.7 = (f32[320,128]{1,0:T(8,128)S(1)}, f32[320,128]{1,0:T(8,128)S(1)}, u32[]{:S(2)}, u32[]{:S(2)}) collective-permute-start(f32[320,128]{1,0:T(8,128)S(1)} %get-tuple-element.38), channel_id=1, source_target_pairs={{0,8},{8,16},{16,24},{24,0},{1,9},{9,17},{17,25},{25,1},{2,10},{10... | collective-permute-start | bytes 491528 | tf_op jit(solution)/shard_map/ppermute | solution.py:356
  41.7 8.9 %collective-permute-start.8 = (f32[320,128]{1,0:T(8,128)S(1)}, f32[320,128]{1,0:T(8,128)S(1)}, u32[]{:S(2)}, u32[]{:S(2)}) collective-permute-start(f32[320,128]{1,0:T(8,128)S(1)} %get-tuple-element.39), channel_id=1, source_target_pairs={{0,16},{8,24},{16,0},{24,8},{1,17},{9,25},{17,1},{25,9},{2,18},{10... | collective-permute-start | bytes 491528 | tf_op jit(solution)/shard_map/ppermute | solution.py:356
  43.7 7.5 %collective-permute-start.9 = (f32[320,128]{1,0:T(8,128)S(1)}, f32[320,128]{1,0:T(8,128)S(1)}, u32[]{:S(2)}, u32[]{:S(2)}) collective-permute-start(f32[320,128]{1,0:T(8,128)S(1)} %get-tuple-element.40), channel_id=1, source_target_pairs={{0,24},{8,0},{16,8},{24,16},{1,25},{9,1},{17,9},{25,17},{2,26},{10... | collective-permute-start | bytes 491528 | tf_op jit(solution)/shard_map/ppermute | solution.py:356
  74.9 7.3 %collective-permute-start.12 = (f32[320,128]{1,0:T(8,128)S(1)}, f32[320,128]{1,0:T(8,128)S(1)}, u32[]{:S(2)}, u32[]{:S(2)}) collective-permute-start(f32[320,128]{1,0:T(8,128)S(1)} %bitcast.19), channel_id=1, source_target_pairs={{0,24},{8,0},{16,8},{24,16},{1,25},{9,1},{17,9},{25,17},{2,26},{10... | collective-permute-start | bytes 491528 | tf_op jit(solution)/shard_map/ppermute | solution.py:356
  77.5 6.9 %collective-permute-start.11 = (f32[320,128]{1,0:T(8,128)S(1)}, f32[320,128]{1,0:T(8,128)S(1)}, u32[]{:S(2)}, u32[]{:S(2)}) collective-permute-start(f32[320,128]{1,0:T(8,128)S(1)} %bitcast.20), channel_id=1, source_target_pairs={{0,16},{8,24},{16,0},{24,8},{1,17},{9,25},{17,1},{25,9},{2,18},{10... | collective-permute-start | bytes 491528 | tf_op jit(solution)/shard_map/ppermute | solution.py:356
  77.6 8.3 %collective-permute-start.10 = (f32[320,128]{1,0:T(8,128)S(1)}, f32[320,128]{1,0:T(8,128)S(1)}, u32[]{:S(2)}, u32[]{:S(2)}) collective-permute-start(f32[320,128]{1,0:T(8,128)S(1)} %bitcast.21), channel_id=1, source_target_pairs={{0,8},{8,16},{16,24},{24,0},{1,9},{9,17},{17,25},{25,1},{2,10},{10... | collective-permute-start | bytes 491528 | tf_op jit(solution)/shard_map/ppermute | solution.py:356

commit v7 on v6

--- a/solution.py
+++ b/solution.py
@@ -254,7 +254,7 @@
 
 def backward_kernel(spread, *refs):
     (messages, d_amp, d_hps, sums, send, potential, basis, first, second, w_two, w_heads_t), outs, (
-        out, cot, first_bf, inner_one, inner_two) = refs[:11], refs[11 : 11 + YS], refs[11 + YS :]
+        out, cot) = refs[:11], refs[11 : 11 + YS], refs[11 + YS :]
     states, slots, walkers = d_amp.shape
     hidden = w_two.shape[1]
     total = jnp.sum(messages[...], axis=0)
@@ -283,18 +283,17 @@
         first_act = first[s]
         second_tanh = second[s]
         second_bf = (second_tanh + first_act).astype(BF16)
-        first_bf[s] = first_act.astype(BF16)
+        first_bf = first_act.astype(BF16)
         cot_bf = cot[s].astype(BF16)
         heads = lax.dot_general(cot_bf, second_bf, NT, preferred_element_type=F32)
         put(2 * COSINES - 1, s, heads[0:2])
         back_two = lax.dot_general(w_heads_t[s], cot_bf, NN, preferred_element_type=F32)
         inner = (back_two * (1.0 - second_tanh * second_tanh)).astype(BF16)
-        inner_two[s] = inner
         back_one = back_two + lax.dot_general(w_two[s], inner, NN, preferred_element_type=F32)
-        inner_one[s] = (back_one * (1.0 - first_act * first_act)).astype(BF16)
-        grad_one = lax.dot_general(basis[...], inner_one[s], NT, preferred_element_type=F32)
+        inner_one = (back_one * (1.0 - first_act * first_act)).astype(BF16)
+        grad_one = lax.dot_general(basis[...], inner_one, NT, preferred_element_type=F32)
         put(0, s, grad_one[0 : 2 * COSINES - 1])
-        put(BASIS, s, lax.dot_general(first_bf[s], inner_two[s], NT, preferred_element_type=F32))
+        put(BASIS, s, lax.dot_general(first_bf, inner, NT, preferred_element_type=F32))
     out[pl.ds(4 * (2 * COSINES + 1), 8), :] = sums[...] * share
     part = out.shape[0] // YS
     y = lax.axis_index("y")
@@ -395,8 +394,7 @@
     parts = call(
         backward_body,
         [((part, 128), F32)] * YS,
-        [((total, 128), F32), ((states, 16, rows), F32), ((states, hidden, rows), BF16),
-         ((states, hidden, rows), BF16), ((states, hidden, rows), BF16)],
+        [((total, 128), F32), ((states, 16, rows), F32)],
         20, (messages, d_amp, d_hps, sums, send, potential, basis, first, second, w_two, w_heads_t), 3 * work)
     parts = [parts[0]] + [along("y", parts[k], k) for k in range(1, YS)]
     line, = call(line_kernel, [((part, 128), F32)], [], 4, parts, 1 << 20)

time: 87.3 us -> 87.3 us (level)
  no operation moved by 1% of the time
where the time goes in v7:
time: 87.3 us; the launch traced here: 87.1 us
  blocking collectives  43.4 us (50%)
  waiting for transfers between devices  18.6 us (21%)
  starting transfers between devices  12.5 us (14%)
  Pallas kernels  11.9 us (14%)
    all_to_all x1, blocking collectives, shards(): messages = lax.all_to_all(message, ('y', 'z'), 0, 0, tiled=True)  19.8 us
    ppermute x13, waiting for transfers between devices, along(): lax.ppermute(array, axis, [(d, (d + shift) % size) for d in range(size)])  18.6 us
    ppermute x13, starting transfers between devices, along(): lax.ppermute(array, axis, [(d, (d + shift) % size) for d in range(size)])  12.5 us
    pallas_call x6, Pallas kernels, call(): pl.pallas_call(body, out_shape=[jax.ShapeDtypeStruct(s, t) for s, t in ou...  11.9 us
    all_to_all x1, blocking collectives, shards(): summed = lax.all_to_all(pieces, 'z', 0, 0, tiled=True).reshape(part, 128)  11.8 us
    all_to_all x1, blocking collectives, shards(): lines = lax.all_to_all(line.reshape(ZS, size, 128), 'z', 0, 0, tiled=True)  11.8 us
  transfers between devices with their start and end apart: 13, of which 9 were waited for; matrix products, arithmetic and copies ran while one was open for 0% of the time, Pallas kernels for 0%

profile of v7, /device:TPU:32, one launch (start us, length us, event | category | flops | bytes accessed | tf_op | source)
XLA Modules:
  0.0 87.1 jit_solution(4950352970862815462)
XLA Ops:
  0.6 6.4 %shard_map.102 = (f32[64,128]{1,0:T(8,128)S(1)}, f32[16,128]{1,0:T(8,128)S(1)}, bf16[64,2048]{1,0:T(8,128)(2,1)S(1)}, f32[2,256,2048]{2,1,0:T(8,128)S(1)}, f32[2...) custom-call(f32[2,30,16,128]{3,2,1,0:T(8,128)} %pos_in.1, ...), custom_call_target="tpu_custom_call" | custom-call | flops 1073741824 | bytes 1048576 | tf_op jit(solution)/shard_map/pallas_call | solution.py:342
  7.0 2.8 %collective-permute-start.2 = (f32[64,128]{1,0:T(8,128)S(1)}, f32[64,128]{1,0:T(8,128)S(1)}, u32[]{:S(2)}, u32[]{:S(2)}) collective-permute-start(f32[64,128]{1,0:T(8,128)S(1)} %get-tuple-element.25.refs_0_.refs_4_), channel_id=1, source_target_pairs={{0,192},{64,0},{128,64},{192,128},{1,193},{65,1},{129,65},{193,129... | collective-permute-start | bytes 98312 | tf_op jit(solution)/shard_map/ppermute | solution.py:355
  9.8 0.8 collective-permute-start.1
  10.6 0.9 %collective-permute-start = (f32[64,128]{1,0:T(8,128)S(1)}, f32[64,128]{1,0:T(8,128)S(1)}, u32[]{:S(2)}, u32[]{:S(2)}) collective-permute-start(f32[64,128]{1,0:T(8,128)S(1)} %get-tuple-element.25.refs_0_.refs_4_), channel_id=1, source_target_pairs={{0,64},{64,128},{128,192},{192,0},{1,65},{65,129},{129,193},{193,1... | collective-permute-start | bytes 98312 | tf_op jit(solution)/shard_map/ppermute | solution.py:355
  11.5 0.0 collective-permute-start.3
  11.5 0.0 collective-permute-done.2.refs_3_
  11.5 0.5 collective-permute-start.6
  12.0 3.2 %collective-permute-done.1.refs_2_ = f32[64,128]{1,0:T(8,128)S(1)} collective-permute-done((f32[64,128]{1,0:T(8,128)S(1)}, f32[64,128]{1,0:T(8,128)S(1)}, u32[]{:S(2)}, u32[]{:S(2)}) %collective-permute-start.1) | collective-permute-done | bytes 32800 | tf_op jit(solution)/shard_map/ppermute | solution.py:355
  15.3 0.0 collective-permute-start.5
  15.3 0.5 collective-permute-done.refs_1_
  15.8 0.0 collective-permute-start.4
  15.8 0.0 collective-permute-done.3.refs_4_
  15.8 0.0 collective-permute-done.6.refs_7_
  15.8 0.7 collective-permute-done.5.refs_6_
  16.5 0.5 collective-permute-done.4.refs_5_
  17.0 0.7 shard_map.103
  17.6 19.8 %all_to_all.15.refs_0_ = f32[32,1,128]{2,1,0:T(1,128)S(1)} all-to-all(f32[32,1,128]{2,1,0:T(1,128)S(1)} %get-tuple-element.28), channel_id=1, replica_groups=mesh['x'=4,'core'=2,'y'=4,'z'=8] {'y','z'}, dimensions={0} | all-to-all | bytes 32768 | tf_op jit(solution)/shard_map/all_to_all | solution.py:391
  37.4 3.6 %shard_map.104 = (f32[320,128]{1,0:T(8,128)S(1)}, f32[320,128]{1,0:T(8,128)S(1)}, f32[320,128]{1,0:T(8,128)S(1)}, f32[320,128]{1,0:T(8,128)S(1)}) custom-call(f32[32,1,128]{2,1,0:T(1,128)S(1)} %all_to_all.15.refs_0_, f32[2,16,128]{2,1,0:T(8,128)S(1)} %get-tuple-element.29.refs_1_, f32[2,16,128]{2,1,0:T(8,128)S(1)} %get-tuple-element.30.refs_2_, ...), custom_call_target="tpu_custom_call" | custom-call | flops 1610612736 | bytes 1048576 | tf_op jit(solution)/shard_map/pallas_call | solution.py:342
  41.0 0.7 collective-permute-start.7
  41.7 2.0 %collective-permute-start.8 = (f32[320,128]{1,0:T(8,128)S(1)}, f32[320,128]{1,0:T(8,128)S(1)}, u32[]{:S(2)}, u32[]{:S(2)}) collective-permute-start(f32[320,128]{1,0:T(8,128)S(1)} %get-tuple-element.39), channel_id=1, source_target_pairs={{0,16},{8,24},{16,0},{24,8},{1,17},{9,25},{17,1},{25,9},{2,18},{10... | collective-permute-start | bytes 491528 | tf_op jit(solution)/shard_map/ppermute | solution.py:355
  43.7 1.2 %collective-permute-start.9 = (f32[320,128]{1,0:T(8,128)S(1)}, f32[320,128]{1,0:T(8,128)S(1)}, u32[]{:S(2)}, u32[]{:S(2)}) collective-permute-start(f32[320,128]{1,0:T(8,128)S(1)} %get-tuple-element.40), channel_id=1, source_target_pairs={{0,24},{8,0},{16,8},{24,16},{1,25},{9,1},{17,9},{25,17},{2,26},{10... | collective-permute-start | bytes 491528 | tf_op jit(solution)/shard_map/ppermute | solution.py:355
  45.0 5.7 %collective-permute-done.7.refs_1_ = f32[320,128]{1,0:T(8,128)S(1)} collective-permute-done((f32[320,128]{1,0:T(8,128)S(1)}, f32[320,128]{1,0:T(8,128)S(1)}, u32[]{:S(2)}, u32[]{:S(2)}) %collective-permute-start.7) | collective-permute-done | bytes 163872 | tf_op jit(solution)/shard_map/ppermute | solution.py:355
  50.6 0.0 collective-permute-done.8.refs_2_
  50.6 0.6 collective-permute-done.9.refs_3_
  51.2 0.1 shard_map.105
  51.3 11.8 %all_to_all.16.parts = f32[8,40,128]{2,1,0:T(8,128)S(1)} all-to-all(f32[8,40,128]{2,1,0:T(8,128)S(1)} %bitcast.23), channel_id=1, replica_groups=mesh['x'=4,'core'=2,'y'=4,'z'=8] {'z'}, dimensions={0} | all-to-all | bytes 327680 | tf_op jit(solution)/shard_map/all_to_all | solution.py:401
  63.1 11.8 %all_to_all.17 = f32[8,40,128]{2,1,0:T(8,128)S(1)} all-to-all(f32[8,40,128]{2,1,0:T(8,128)S(1)} %shard_map.106), channel_id=1, replica_groups=mesh['x'=4,'core'=2,'y'=4,'z'=8] {'z'}, dimensions={0} | all-to-all | bytes 327680 | tf_op jit(solution)/shard_map/all_to_all | solution.py:403
  74.9 2.7 %collective-permute-start.12 = (f32[320,128]{1,0:T(8,128)S(1)}, f32[320,128]{1,0:T(8,128)S(1)}, u32[]{:S(2)}, u32[]{:S(2)}) collective-permute-start(f32[320,128]{1,0:T(8,128)S(1)} %bitcast.19), channel_id=1, source_target_pairs={{0,24},{8,0},{16,8},{24,16},{1,25},{9,1},{17,9},{25,17},{2,26},{10... | collective-permute-start | bytes 491528 | tf_op jit(solution)/shard_map/ppermute | solution.py:355
  77.5 0.0 collective-permute-start.11
  77.6 0.8 collective-permute-start.10
  78.4 3.8 %collective-permute-done.12.refs_3_ = f32[320,128]{1,0:T(8,128)S(1)} collective-permute-done((f32[320,128]{1,0:T(8,128)S(1)}, f32[320,128]{1,0:T(8,128)S(1)}, u32[]{:S(2)}, u32[]{:S(2)}) %collective-permute-start.12) | collective-permute-done | bytes 163872 | tf_op jit(solution)/shard_map/ppermute | solution.py:355
  82.2 2.3 %collective-permute-done.11.refs_2_ = f32[320,128]{1,0:T(8,128)S(1)} collective-permute-done((f32[320,128]{1,0:T(8,128)S(1)}, f32[320,128]{1,0:T(8,128)S(1)}, u32[]{:S(2)}, u32[]{:S(2)}) %collective-permute-start.11) | collective-permute-done | bytes 163872 | tf_op jit(solution)/shard_map/ppermute | solution.py:355
  84.5 1.4 %collective-permute-done.10.refs_1_ = f32[320,128]{1,0:T(8,128)S(1)} collective-permute-done((f32[320,128]{1,0:T(8,128)S(1)}, f32[320,128]{1,0:T(8,128)S(1)}, u32[]{:S(2)}, u32[]{:S(2)}) %collective-permute-start.10) | collective-permute-done | bytes 163872 | tf_op jit(solution)/shard_map/ppermute | solution.py:355
  85.9 1.3 %shard_map.107 = (f32[16,16]{1,0:T(8,128)}, f32[1024,128]{1,0:T(8,128)}, f32[1024,128]{1,0:T(8,128)}, f32[8,128]{1,0:T(8,128)}) custom-call(f32[320,128]{1,0:T(8,128)S(1)} %bitcast.22, f32[320,128]{1,0:T(8,128)S(1)} %collective-permute-done.10.refs_1_, f32[320,128]{1,0:T(8,128)S(1)} %collective-permute-done.11.refs_2_, ...), custom_call_target="tpu_custom_call" | custom-call | flops 1048576 | bytes 1048576 | tf_op jit(solution)/shard_map/pallas_call | solution.py:342
  (1 shorter events, 0.0 us)
Async XLA Ops:
  7.0 4.5 %collective-permute-start.2 = (f32[64,128]{1,0:T(8,128)S(1)}, f32[64,128]{1,0:T(8,128)S(1)}, u32[]{:S(2)}, u32[]{:S(2)}) collective-permute-start(f32[64,128]{1,0:T(8,128)S(1)} %get-tuple-element.25.refs_0_.refs_4_), channel_id=1, source_target_pairs={{0,192},{64,0},{128,64},{192,128},{1,193},{65,1},{129,65},{193,129... | collective-permute-start | bytes 98312 | tf_op jit(solution)/shard_map/ppermute | solution.py:355
  9.8 5.4 %collective-permute-start.1 = (f32[64,128]{1,0:T(8,128)S(1)}, f32[64,128]{1,0:T(8,128)S(1)}, u32[]{:S(2)}, u32[]{:S(2)}) collective-permute-start(f32[64,128]{1,0:T(8,128)S(1)} %get-tuple-element.25.refs_0_.refs_4_), channel_id=1, source_target_pairs={{0,128},{64,192},{128,0},{192,64},{1,129},{65,193},{129,1},{193,65... | collective-permute-start | bytes 98312 | tf_op jit(solution)/shard_map/ppermute | solution.py:355
  10.6 5.1 %collective-permute-start = (f32[64,128]{1,0:T(8,128)S(1)}, f32[64,128]{1,0:T(8,128)S(1)}, u32[]{:S(2)}, u32[]{:S(2)}) collective-permute-start(f32[64,128]{1,0:T(8,128)S(1)} %get-tuple-element.25.refs_0_.refs_4_), channel_id=1, source_target_pairs={{0,64},{64,128},{128,192},{192,0},{1,65},{65,129},{129,193},{193,1... | collective-permute-start | bytes 98312 | tf_op jit(solution)/shard_map/ppermute | solution.py:355
  11.5 4.3 %collective-permute-start.3 = (f32[64,128]{1,0:T(8,128)S(1)}, f32[64,128]{1,0:T(8,128)S(1)}, u32[]{:S(2)}, u32[]{:S(2)}) collective-permute-start(f32[64,128]{1,0:T(8,128)S(1)} %get-tuple-element.25.refs_0_.refs_4_), channel_id=1, source_target_pairs={{0,32},{32,0},{1,33},{33,1},{2,34},{34,2},{3,35},{35,3},{4,36},{36... | collective-permute-start | bytes 98312 | tf_op jit(solution)/shard_map/ppermute | solution.py:355
  11.5 4.3 %collective-permute-start.6 = (f32[64,128]{1,0:T(8,128)S(1)}, f32[64,128]{1,0:T(8,128)S(1)}, u32[]{:S(2)}, u32[]{:S(2)}) collective-permute-start(f32[64,128]{1,0:T(8,128)S(1)} %collective-permute-done.2.refs_3_), channel_id=1, source_target_pairs={{0,32},{32,0},{1,33},{33,1},{2,34},{34,2},{3,35},{35,3},{4,36},{36... | collective-permute-start | bytes 98312 | tf_op jit(solution)/shard_map/ppermute | solution.py:355
  15.3 1.2 %collective-permute-start.5 = (f32[64,128]{1,0:T(8,128)S(1)}, f32[64,128]{1,0:T(8,128)S(1)}, u32[]{:S(2)}, u32[]{:S(2)}) collective-permute-start(f32[64,128]{1,0:T(8,128)S(1)} %collective-permute-done.1.refs_2_), channel_id=1, source_target_pairs={{0,32},{32,0},{1,33},{33,1},{2,34},{34,2},{3,35},{35,3},{4,36},{36... | collective-permute-start | bytes 98312 | tf_op jit(solution)/shard_map/ppermute | solution.py:355
  15.8 1.2 %collective-permute-start.4 = (f32[64,128]{1,0:T(8,128)S(1)}, f32[64,128]{1,0:T(8,128)S(1)}, u32[]{:S(2)}, u32[]{:S(2)}) collective-permute-start(f32[64,128]{1,0:T(8,128)S(1)} %collective-permute-done.refs_1_), channel_id=1, source_target_pairs={{0,32},{32,0},{1,33},{33,1},{2,34},{34,2},{3,35},{35,3},{4,36},{36... | collective-permute-start | bytes 98312 | tf_op jit(solution)/shard_map/ppermute | solution.py:355
  41.0 9.6 %collective-permute-start.7 = (f32[320,128]{1,0:T(8,128)S(1)}, f32[320,128]{1,0:T(8,128)S(1)}, u32[]{:S(2)}, u32[]{:S(2)}) collective-permute-start(f32[320,128]{1,0:T(8,128)S(1)} %get-tuple-element.38), channel_id=1, source_target_pairs={{0,8},{8,16},{16,24},{24,0},{1,9},{9,17},{17,25},{25,1},{2,10},{10... | collective-permute-start | bytes 491528 | tf_op jit(solution)/shard_map/ppermute | solution.py:355
  41.7 8.9 %collective-permute-start.8 = (f32[320,128]{1,0:T(8,128)S(1)}, f32[320,128]{1,0:T(8,128)S(1)}, u32[]{:S(2)}, u32[]{:S(2)}) collective-permute-start(f32[320,128]{1,0:T(8,128)S(1)} %get-tuple-element.39), channel_id=1, source_target_pairs={{0,16},{8,24},{16,0},{24,8},{1,17},{9,25},{17,1},{25,9},{2,18},{10... | collective-permute-start | bytes 491528 | tf_op jit(solution)/shard_map/ppermute | solution.py:355
  43.7 7.5 %collective-permute-start.9 = (f32[320,128]{1,0:T(8,128)S(1)}, f32[320,128]{1,0:T(8,128)S(1)}, u32[]{:S(2)}, u32[]{:S(2)}) collective-permute-start(f32[320,128]{1,0:T(8,128)S(1)} %get-tuple-element.40), channel_id=1, source_target_pairs={{0,24},{8,0},{16,8},{24,16},{1,25},{9,1},{17,9},{25,17},{2,26},{10... | collective-permute-start | bytes 491528 | tf_op jit(solution)/shard_map/ppermute | solution.py:355
  74.9 7.3 %collective-permute-start.12 = (f32[320,128]{1,0:T(8,128)S(1)}, f32[320,128]{1,0:T(8,128)S(1)}, u32[]{:S(2)}, u32[]{:S(2)}) collective-permute-start(f32[320,128]{1,0:T(8,128)S(1)} %bitcast.19), channel_id=1, source_target_pairs={{0,24},{8,0},{16,8},{24,16},{1,25},{9,1},{17,9},{25,17},{2,26},{10... | collective-permute-start | bytes 491528 | tf_op jit(solution)/shard_map/ppermute | solution.py:355
  77.5 6.9 %collective-permute-start.11 = (f32[320,128]{1,0:T(8,128)S(1)}, f32[320,128]{1,0:T(8,128)S(1)}, u32[]{:S(2)}, u32[]{:S(2)}) collective-permute-start(f32[320,128]{1,0:T(8,128)S(1)} %bitcast.20), channel_id=1, source_target_pairs={{0,16},{8,24},{16,0},{24,8},{1,17},{9,25},{17,1},{25,9},{2,18},{10... | collective-permute-start | bytes 491528 | tf_op jit(solution)/shard_map/ppermute | solution.py:355
  77.6 8.3 %collective-permute-start.10 = (f32[320,128]{1,0:T(8,128)S(1)}, f32[320,128]{1,0:T(8,128)S(1)}, u32[]{:S(2)}, u32[]{:S(2)}) collective-permute-start(f32[320,128]{1,0:T(8,128)S(1)} %bitcast.21), channel_id=1, source_target_pairs={{0,8},{8,16},{16,24},{24,0},{1,9},{9,17},{17,25},{25,1},{2,10},{10... | collective-permute-start | bytes 491528 | tf_op jit(solution)/shard_map/ppermute | solution.py:355
